TPU v7x, 32 devices: a whole 2x2x4 slice. The times are simulated.
32 devices in a mesh: shard: 4 (over y, x), ctx: 4 (over z), tp: 2 (over core).
Axes of the slice: x: 2, y: 2, z: 4, core: 2. Of those that a mesh axis runs over, the one named last changes fastest.
Arguments:
- inputs: float32 [32, 512, 1024], P('shard', 'ctx'), may hold values from -6 to 6
- lengths: int32 [32], P('shard'), may hold values from 128 to 512, as said below
- query_weight: bfloat16 [1024, 1024], P('shard', 'tp'), may hold values from -0.1875 to 0.1875
- key_weight: bfloat16 [1024, 1024], P('shard', 'tp'), may hold values from -0.1875 to 0.1875
- value_weight: bfloat16 [1024, 1024], P('shard', 'tp'), may hold values from -0.1875 to 0.1875
- output_weight: bfloat16 [1024, 1024], P('tp', 'shard'), may hold values from -1.5 to 1.5
- expand_weight: bfloat16 [1024, 4096], P('shard', 'tp'), may hold values from -0.1875 to 0.1875
- reduce_weight: bfloat16 [4096, 1024], P('tp', 'shard'), may hold values from -0.09375 to 0.09375
- query_bias: bfloat16 [16, 64], P('tp', 'shard'), may hold values from -3 to 3
- value_bias: bfloat16 [16, 64], P('tp', 'shard'), may hold values from -0.59765625 to 0.59765625
- expand_bias: bfloat16 [64, 64], P('tp', 'shard'), may hold values from -3 to 3
- output_bias: bfloat16 [1024], P('shard'), may hold values from -3 to 3
- reduce_bias: bfloat16 [1024], P('shard'), may hold values from -3 to 3
- first_gain: bfloat16 [1024], P('shard'), may hold values from 0.25 to 1.75
- first_shift: bfloat16 [1024], P('shard'), may hold values from -3 to 3
- second_gain: bfloat16 [1024], P('shard'), may hold values from 0.25 to 1.75
- second_shift: bfloat16 [1024], P('shard'), may hold values from -3 to 3
- cotangent: float32 [32, 512, 1024], P('shard', 'ctx'), may hold values from -6 to 6
Outputs:
- layer_out: float32 [32, 512, 1024], P('shard', 'ctx')
- input_grad: float32 [32, 512, 1024], P('shard', 'ctx')
- query_weight_grad: float32 [1024, 1024], P('shard', 'tp')
- key_weight_grad: float32 [1024, 1024], P('shard', 'tp')
- value_weight_grad: float32 [1024, 1024], P('shard', 'tp')
- output_weight_grad: float32 [1024, 1024], P('tp', 'shard')
- expand_weight_grad: float32 [1024, 4096], P('shard', 'tp')
- reduce_weight_grad: float32 [4096, 1024], P('tp', 'shard')
- query_bias_grad: float32 [16, 64], P('tp', 'shard')
- value_bias_grad: float32 [16, 64], P('tp', 'shard')
- expand_bias_grad: float32 [64, 64], P('tp', 'shard')
- output_bias_grad: float32 [1024], P('shard')
- reduce_bias_grad: float32 [1024], P('shard')
- first_gain_grad: float32 [1024], P('shard')
- first_shift_grad: float32 [1024], P('shard')
- second_gain_grad: float32 [1024], P('shard')
- second_shift_grad: float32 [1024], P('shard')
Inputs may be any that keep to these rules, and one draw needn't show every extreme that they name: `lengths`: in each group of 8 sequences held by one index of shard, one sequence has all 512 slots valid.
All inputs are finite; a program needn't handle non-finite values.
Results may differ from a plain program's by a relative error of at most 0.019.
Values may be sent and summed in bfloat16 or wider, within the bound.
A program may use at most 192 MiB of HBM per device.

v0:
```python
import jax
import jax.numpy as jnp
from jax import lax
from jax.sharding import PartitionSpec as P

HD = 64


EPSILON = 1e-05
MASKED = -1e30


def layer_norm(hidden, gain, shift):
    row_mean = jnp.mean(hidden, -1, keepdims=True)
    centred = hidden - row_mean
    inv_std = lax.rsqrt(jnp.mean(centred * centred, -1, keepdims=True) + EPSILON)
    normed = centred * inv_std
    return (normed * gain + shift, normed, inv_std)


def norm_back(gradient, normed, inv_std, gain):
    gain_grad = jnp.sum(gradient * normed, 0)
    shift_grad = jnp.sum(gradient, 0)
    scaled = gradient * gain
    centred_grad = (
        scaled
        - jnp.mean(scaled, -1, keepdims=True)
        - normed * jnp.mean(scaled * normed, -1, keepdims=True)
    )
    return (centred_grad * inv_std, gain_grad, shift_grad)


def masked_scores(queries, key_block, length):
    score_scale = HD ** (-0.5)
    scores = (
        jnp.einsum("qhe,khe->hqk", queries, key_block, preferred_element_type=jnp.float32)
        * score_scale
    )
    live_keys = jnp.arange(key_block.shape[0]) < length
    return jnp.where(live_keys[None, None, :], scores, MASKED)


def attend(queries, key_block, values, length):
    block_rows = queries.shape[0]
    queries = queries.reshape(block_rows, -1, HD)
    key_block = key_block.reshape(key_block.shape[0], -1, HD)
    values = values.reshape(values.shape[0], -1, HD)
    scores = masked_scores(queries, key_block, length)
    row_peak = jnp.max(scores, -1, keepdims=True)
    exp_scores = jnp.exp(scores - row_peak)
    row_total = jnp.sum(exp_scores, -1, keepdims=True)
    weights_low = (exp_scores / row_total).astype(jnp.bfloat16)
    attended = jnp.einsum("hqk,khe->qhe", weights_low, values, preferred_element_type=jnp.float32)
    return (attended.reshape(block_rows, -1), (row_peak + jnp.log(row_total))[..., 0])


def attend_back(queries, key_block, values, out_grad, log_total, length):
    block_rows = queries.shape[0]
    key_count = key_block.shape[0]
    score_scale = HD ** (-0.5)
    queries = queries.reshape(block_rows, -1, HD)
    key_block = key_block.reshape(key_count, -1, HD)
    values = values.reshape(key_count, -1, HD)
    out_grad = out_grad.reshape(block_rows, -1, HD)
    scores = masked_scores(queries, key_block, length)
    probabilities = jnp.exp(scores - log_total[..., None])
    value_grad = jnp.einsum(
        "hqk,qhe->khe",
        probabilities.astype(jnp.bfloat16),
        out_grad,
        preferred_element_type=jnp.float32,
    )
    prob_grad = jnp.einsum("qhe,khe->hqk", out_grad, values, preferred_element_type=jnp.float32)
    score_grad = (
        probabilities * (prob_grad - jnp.sum(prob_grad * probabilities, -1, keepdims=True))
    ).astype(jnp.bfloat16)
    query_grad = (
        jnp.einsum("hqk,khe->qhe", score_grad, key_block, preferred_element_type=jnp.float32)
        * score_scale
    )
    key_grad = (
        jnp.einsum("hqk,qhe->khe", score_grad, queries, preferred_element_type=jnp.float32)
        * score_scale
    )
    return (
        query_grad.reshape(block_rows, -1),
        key_grad.reshape(key_count, -1),
        value_grad.reshape(key_count, -1),
    )


def exact_gelu(values):
    return jax.nn.gelu(values, approximate=False)


def body(
    inputs,
    lengths,
    query_weight,
    key_weight,
    value_weight,
    output_weight,
    expand_weight,
    reduce_weight,
    query_bias,
    value_bias,
    expand_bias,
    output_bias,
    reduce_bias,
    first_gain,
    first_shift,
    second_gain,
    second_shift,
    cotangent,
):
    positions = lax.axis_index("ctx") * inputs.shape[1] + jnp.arange(inputs.shape[1])
    seq_count, block_rows, model_width = inputs.shape
    tokens = seq_count * block_rows
    gathered = (
        lax.all_gather(query_weight, "shard", axis=0, tiled=True),
        lax.all_gather(key_weight, "shard", axis=0, tiled=True),
        lax.all_gather(value_weight, "shard", axis=0, tiled=True),
        lax.all_gather(output_weight, "shard", axis=1, tiled=True),
        lax.all_gather(expand_weight, "shard", axis=0, tiled=True),
        lax.all_gather(reduce_weight, "shard", axis=1, tiled=True),
        lax.all_gather(query_bias, "shard", axis=1, tiled=True),
        lax.all_gather(value_bias, "shard", axis=1, tiled=True),
        lax.all_gather(expand_bias, "shard", axis=1, tiled=True),
        lax.all_gather(output_bias, "shard", axis=0, tiled=True),
        lax.all_gather(reduce_bias, "shard", axis=0, tiled=True),
        lax.all_gather(first_gain, "shard", axis=0, tiled=True),
        lax.all_gather(first_shift, "shard", axis=0, tiled=True),
        lax.all_gather(second_gain, "shard", axis=0, tiled=True),
        lax.all_gather(second_shift, "shard", axis=0, tiled=True),
    )
    query_full, key_full, value_full, output_full, expand_full, reduce_full = gathered[:6]
    query_shift = gathered[6].reshape(-1).astype(jnp.float32)
    value_shift = gathered[7].reshape(-1).astype(jnp.float32)
    expand_shift = gathered[8].reshape(-1).astype(jnp.float32)
    output_shift = gathered[9].astype(jnp.float32)
    reduce_shift = gathered[10].astype(jnp.float32)
    gain_one = gathered[11].astype(jnp.float32)
    shift_one = gathered[12].astype(jnp.float32)
    gain_two = gathered[13].astype(jnp.float32)
    shift_two = gathered[14].astype(jnp.float32)
    local_width = query_full.shape[1]
    valid_rows = (positions[None, :] < lengths[:, None]).astype(jnp.float32)
    x_rows = inputs.reshape(tokens, model_width)
    inputs_low = x_rows.astype(jnp.bfloat16)
    queries = (
        jnp.dot(inputs_low, query_full, preferred_element_type=jnp.float32) + query_shift
    ).astype(jnp.bfloat16)
    key_local = jnp.dot(inputs_low, key_full, preferred_element_type=jnp.float32).astype(
        jnp.bfloat16
    )
    value_local = (
        jnp.dot(inputs_low, value_full, preferred_element_type=jnp.float32) + value_shift
    ).astype(jnp.bfloat16)
    query_seqs = queries.reshape(seq_count, block_rows, local_width)
    key_seqs = key_local.reshape(seq_count, block_rows, local_width)
    value_seqs = value_local.reshape(seq_count, block_rows, local_width)
    keys_all, values_all = (
        lax.all_gather(key_seqs, "ctx", axis=1, tiled=True),
        lax.all_gather(value_seqs, "ctx", axis=1, tiled=True),
    )
    attended, log_total = lax.map(
        lambda pieces: attend(pieces[0], pieces[1], pieces[2], pieces[3]),
        (query_seqs, keys_all, values_all, lengths),
    )
    attn_low = attended.reshape(tokens, local_width).astype(jnp.bfloat16)
    branch = (
        lax.psum(jnp.dot(attn_low, output_full, preferred_element_type=jnp.float32), "tp")
        + output_shift
    )
    first = x_rows + branch
    normed_one, norm_first, inv_first = layer_norm(first, gain_one, shift_one)
    normed_low = normed_one.astype(jnp.bfloat16)
    pre_act = jnp.dot(normed_low, expand_full, preferred_element_type=jnp.float32) + expand_shift
    hidden_low = exact_gelu(pre_act).astype(jnp.bfloat16)
    reduced = lax.psum(jnp.dot(hidden_low, reduce_full, preferred_element_type=jnp.float32), "tp")
    second = normed_one + (reduced + reduce_shift)
    output, norm_second, inv_second = layer_norm(second, gain_two, shift_two)
    query_full, key_full, value_full, output_full, expand_full, reduce_full = (
        lax.all_gather(query_weight, "shard", axis=0, tiled=True),
        lax.all_gather(key_weight, "shard", axis=0, tiled=True),
        lax.all_gather(value_weight, "shard", axis=0, tiled=True),
        lax.all_gather(output_weight, "shard", axis=1, tiled=True),
        lax.all_gather(expand_weight, "shard", axis=0, tiled=True),
        lax.all_gather(reduce_weight, "shard", axis=1, tiled=True),
    )
    keys_all, values_all = (
        lax.all_gather(key_seqs, "ctx", axis=1, tiled=True),
        lax.all_gather(value_seqs, "ctx", axis=1, tiled=True),
    )
    out_grad = cotangent.reshape(tokens, model_width) * valid_rows.reshape(tokens, 1)
    second_grad, gain_two_grad, shift_two_grad = norm_back(
        out_grad, norm_second, inv_second, gain_two
    )
    mlp_grad = second_grad.astype(jnp.bfloat16)
    reduce_bias_grad = jnp.sum(mlp_grad.astype(jnp.float32), 0)
    reduce_weight_grad = jnp.einsum(
        "tf,td->fd", hidden_low, mlp_grad, preferred_element_type=jnp.float32
    )
    hidden_grad = jnp.einsum("td,fd->tf", mlp_grad, reduce_full, preferred_element_type=jnp.float32)
    unused, gelu_back = jax.vjp(exact_gelu, pre_act)
    pre_grad = gelu_back(hidden_grad)[0].astype(jnp.bfloat16)
    expand_bias_grad = jnp.sum(pre_grad.astype(jnp.float32), 0)
    expand_weight_grad = jnp.einsum(
        "td,tf->df", normed_low, pre_grad, preferred_element_type=jnp.float32
    )
    normed_grad = second_grad + lax.psum(
        jnp.einsum("tf,df->td", pre_grad, expand_full, preferred_element_type=jnp.float32), "tp"
    )
    first_grad, gain_one_grad, shift_one_grad = norm_back(
        normed_grad, norm_first, inv_first, gain_one
    )
    branch_grad = first_grad.astype(jnp.bfloat16)
    output_bias_grad = jnp.sum(branch_grad.astype(jnp.float32), 0)
    output_weight_grad = jnp.einsum(
        "tc,td->cd", attn_low, branch_grad, preferred_element_type=jnp.float32
    )
    attn_grad = jnp.einsum(
        "td,cd->tc", branch_grad, output_full, preferred_element_type=jnp.float32
    ).astype(jnp.bfloat16)
    query_grad, key_grad_all, value_grad_all = lax.map(
        lambda pieces: attend_back(
            pieces[0], pieces[1], pieces[2], pieces[3], pieces[4], pieces[5]
        ),
        (
            query_seqs,
            keys_all,
            values_all,
            attn_grad.reshape(seq_count, block_rows, local_width),
            log_total,
            lengths,
        ),
    )
    key_grad, value_grad = (
        lax.psum_scatter(key_grad_all, "ctx", scatter_dimension=1, tiled=True),
        lax.psum_scatter(value_grad_all, "ctx", scatter_dimension=1, tiled=True),
    )
    query_low = query_grad.reshape(tokens, local_width).astype(jnp.bfloat16)
    key_low = key_grad.reshape(tokens, local_width).astype(jnp.bfloat16)
    value_low = value_grad.reshape(tokens, local_width).astype(jnp.bfloat16)
    query_bias_grad = jnp.sum(query_low.astype(jnp.float32), 0).reshape(-1, HD)
    value_bias_grad = jnp.sum(value_low.astype(jnp.float32), 0).reshape(-1, HD)
    expand_bias_grad = expand_bias_grad.reshape(-1, HD)
    query_weight_grad = jnp.einsum(
        "td,tc->dc", inputs_low, query_low, preferred_element_type=jnp.float32
    )
    key_weight_grad = jnp.einsum(
        "td,tc->dc", inputs_low, key_low, preferred_element_type=jnp.float32
    )
    value_weight_grad = jnp.einsum(
        "td,tc->dc", inputs_low, value_low, preferred_element_type=jnp.float32
    )
    x_part = jnp.einsum("tc,dc->td", query_low, query_full, preferred_element_type=jnp.float32)
    x_part = x_part + jnp.einsum("tc,dc->td", key_low, key_full, preferred_element_type=jnp.float32)
    x_part = x_part + jnp.einsum(
        "tc,dc->td", value_low, value_full, preferred_element_type=jnp.float32
    )
    input_grad = first_grad + lax.psum(x_part.astype(jnp.bfloat16), "tp").astype(jnp.float32)
    summed = (
        lax.psum_scatter(
            query_weight_grad.astype(jnp.bfloat16), "shard", scatter_dimension=0, tiled=True
        ).astype(jnp.float32),
        lax.psum_scatter(
            key_weight_grad.astype(jnp.bfloat16), "shard", scatter_dimension=0, tiled=True
        ).astype(jnp.float32),
        lax.psum_scatter(
            value_weight_grad.astype(jnp.bfloat16), "shard", scatter_dimension=0, tiled=True
        ).astype(jnp.float32),
        lax.psum_scatter(
            output_weight_grad.astype(jnp.bfloat16), "shard", scatter_dimension=1, tiled=True
        ).astype(jnp.float32),
        lax.psum_scatter(
            expand_weight_grad.astype(jnp.bfloat16), "shard", scatter_dimension=0, tiled=True
        ).astype(jnp.float32),
        lax.psum_scatter(
            reduce_weight_grad.astype(jnp.bfloat16), "shard", scatter_dimension=1, tiled=True
        ).astype(jnp.float32),
        lax.psum_scatter(
            query_bias_grad.astype(jnp.bfloat16), "shard", scatter_dimension=1, tiled=True
        ).astype(jnp.float32),
        lax.psum_scatter(
            value_bias_grad.astype(jnp.bfloat16), "shard", scatter_dimension=1, tiled=True
        ).astype(jnp.float32),
        lax.psum_scatter(
            expand_bias_grad.astype(jnp.bfloat16), "shard", scatter_dimension=1, tiled=True
        ).astype(jnp.float32),
        lax.psum_scatter(
            output_bias_grad.astype(jnp.bfloat16), "shard", scatter_dimension=0, tiled=True
        ).astype(jnp.float32),
        lax.psum_scatter(
            reduce_bias_grad.astype(jnp.bfloat16), "shard", scatter_dimension=0, tiled=True
        ).astype(jnp.float32),
        lax.psum_scatter(
            gain_one_grad.astype(jnp.bfloat16), "shard", scatter_dimension=0, tiled=True
        ).astype(jnp.float32),
        lax.psum_scatter(
            shift_one_grad.astype(jnp.bfloat16), "shard", scatter_dimension=0, tiled=True
        ).astype(jnp.float32),
        lax.psum_scatter(
            gain_two_grad.astype(jnp.bfloat16), "shard", scatter_dimension=0, tiled=True
        ).astype(jnp.float32),
        lax.psum_scatter(
            shift_two_grad.astype(jnp.bfloat16), "shard", scatter_dimension=0, tiled=True
        ).astype(jnp.float32),
    )
    results = (
        lax.psum(summed[0].astype(jnp.bfloat16), "ctx").astype(jnp.float32),
        lax.psum(summed[1].astype(jnp.bfloat16), "ctx").astype(jnp.float32),
        lax.psum(summed[2].astype(jnp.bfloat16), "ctx").astype(jnp.float32),
        lax.psum(summed[3].astype(jnp.bfloat16), "ctx").astype(jnp.float32),
        lax.psum(summed[4].astype(jnp.bfloat16), "ctx").astype(jnp.float32),
        lax.psum(summed[5].astype(jnp.bfloat16), "ctx").astype(jnp.float32),
        lax.psum(summed[6].astype(jnp.bfloat16), "ctx").astype(jnp.float32),
        lax.psum(summed[7].astype(jnp.bfloat16), "ctx").astype(jnp.float32),
        lax.psum(summed[8].astype(jnp.bfloat16), "ctx").astype(jnp.float32),
        lax.psum(summed[9].astype(jnp.bfloat16), "ctx").astype(jnp.float32),
        lax.psum(summed[10].astype(jnp.bfloat16), "ctx").astype(jnp.float32),
        lax.psum(summed[11].astype(jnp.bfloat16), "ctx").astype(jnp.float32),
        lax.psum(summed[12].astype(jnp.bfloat16), "ctx").astype(jnp.float32),
        lax.psum(summed[13].astype(jnp.bfloat16), "ctx").astype(jnp.float32),
        lax.psum(summed[14].astype(jnp.bfloat16), "ctx").astype(jnp.float32),
    )
    output_seqs = output.reshape(seq_count, block_rows, model_width)
    grad_seqs = input_grad.reshape(seq_count, block_rows, model_width)
    return (
        output_seqs,
        grad_seqs,
        results[0],
        results[1],
        results[2],
        results[3],
        results[4],
        results[5],
        results[6],
        results[7],
        results[8],
        results[9],
        results[10],
        results[11],
        results[12],
        results[13],
        results[14],
    )


def solution(mesh):
    return jax.shard_map(
        body,
        mesh=mesh,
        in_specs=(
            P("shard", "ctx", None),
            P("shard"),
            P("shard", "tp"),
            P("shard", "tp"),
            P("shard", "tp"),
            P("tp", "shard"),
            P("shard", "tp"),
            P("tp", "shard"),
            P("tp", "shard"),
            P("tp", "shard"),
            P("tp", "shard"),
            P("shard"),
            P("shard"),
            P("shard"),
            P("shard"),
            P("shard"),
            P("shard"),
            P("shard", "ctx", None),
        ),
        out_specs=(
            P("shard", "ctx", None),
            P("shard", "ctx", None),
            P("shard", "tp"),
            P("shard", "tp"),
            P("shard", "tp"),
            P("tp", "shard"),
            P("shard", "tp"),
            P("tp", "shard"),
            P("tp", "shard"),
            P("tp", "shard"),
            P("tp", "shard"),
            P("shard"),
            P("shard"),
            P("shard"),
            P("shard"),
            P("shard"),
            P("shard"),
        ),
        check_vma=False,
    )
```

profile of v0, /device:TPU:0, one launch (start us, length us, event | category | flops | bytes accessed | tf_op | source)
XLA Modules:
  0.0 1409.3 jit_solution(14524430317390675183)
XLA Ops:
  9.5 9.6 all-gather
  19.3 2.6 bitcast_convert_fusion
  21.9 17.3 %all-gather.17.cloned.1.call-done = bf16[1024,512]{1,0:T(8,128)(2,1)} async-done(((bf16[256,512]{1,0:T(8,128)(2,1)}), bf16[1024,512]{1,0:T(8,128)(2,1)}) %all-gather.17.cloned.1.call-update) | async-done | bytes 1048592 | tf_op jit(solution)/shard_map/all_gather | solution.py:122
  39.2 2.5 add_convert_fusion.3
  43.1 24.6 %all-gather.23.cloned.1.call-done = bf16[1024,512]{1,0:T(8,128)(2,1)} async-done(((bf16[256,512]{1,0:T(8,128)(2,1)}), bf16[1024,512]{1,0:T(8,128)(2,1)}) %all-gather.23.cloned.1.call-update) | async-done | bytes 1048592 | tf_op jit(solution)/shard_map/all_gather | solution.py:121
  67.7 2.5 convolution_convert_fusion.4
  72.2 8.0 all-gather.1
  80.4 15.9 %all-gather.21.cloned.1.call-done = bf16[1024,512]{1,0:T(8,128)(2,1)} async-done(((bf16[256,512]{1,0:T(8,128)(2,1)}), bf16[1024,512]{1,0:T(8,128)(2,1)}) %all-gather.21.cloned.1.call-update) | async-done | bytes 1048592 | tf_op jit(solution)/shard_map/all_gather | solution.py:120
  96.3 2.5 add_convert_fusion.2
  100.1 78.8 %all-gather.19.cloned.1.call-done = bf16[8,512,512]{1,2,0:T(8,128)(2,1)} async-done(((bf16[8,128,512]{1,2,0:T(8,128)(2,1)}), bf16[8,512,512]{1,2,0:T(8,128)(2,1)}) %all-gather.19.cloned.1.call-update) | async-done | bytes 4194320 | tf_op jit(solution)/shard_map/all_gather | solution.py:164
  178.8 80.8 %all-gather.25.cloned.1.call-done = bf16[8,512,512]{1,2,0:T(8,128)(2,1)} async-done(((bf16[8,128,512]{1,2,0:T(8,128)(2,1)}), bf16[8,512,512]{1,2,0:T(8,128)(2,1)}) %all-gather.25.cloned.1.call-update) | async-done | bytes 4194320 | tf_op jit(solution)/shard_map/all_gather | solution.py:163
  259.7 49.4 %while.26 = (s32[]{:T(128)}, bf16[8,128,512]{2,1,0:T(8,128)(2,1)S(1)}, f32[8,8,128]{2,1,0:T(8,128)}, bf16[8,512,512]{1,2,0:T(8,128)(2,1)}, s32[8]{0:T(128)S(1)},...) while((s32[]{:T(128)}, bf16[8,128,512]{2,1,0:T(8,128)(2,1)S(1)}, ...), condition=%wide.region_3.4_spmd, body=%wide.region_0.3_spmd.sunk | while | flops 140508672 | bytes 10520701 | solution.py:166
  309.1 4.9 fusion.37
  315.6 8.1 all_gather.71
  323.9 8.0 all-gather.2
  331.9 7.1 all-gather.4
  339.0 8.2 all-gather.3
  347.3 4.1 fusion.35
  351.5 2.0 copy-done
  354.0 42.6 %all-gather.29.cloned.1.call-done = bf16[1024,2048]{1,0:T(8,128)(2,1)} async-done(((bf16[256,2048]{1,0:T(8,128)(2,1)}), bf16[1024,2048]{1,0:T(8,128)(2,1)}) %all-gather.29.cloned.1.call-update) | async-done | bytes 4194320 | tf_op jit(solution)/shard_map/all_gather | solution.py:124
  396.7 28.0 %multiply_convert_fusion.1 = (bf16[1024,2048]{1,0:T(8,128)(2,1)}, f32[1024,2048]{1,0:T(8,128)}, f32[1024,2048]{1,0:T(8,128)}) fusion(f32[2048]{0:T(1024)S(1)} %reshape.271, bf16[1024,2048]{1,0:T(8,128)(2,1)} %all-gather.29.cloned.1.call-done, f32[1024,1024]{1,0:T(8,128)} %copy-done, f32[1024]{0:T(1024)S(1)} %bitcast.223, f32[1024]{0:T(1024)S(1)} %bitcast.215, ...), kind=kOutput, calls=%fused_computation.33 | convolution fusion | flops 4438622208 | bytes 29384704 | tf_op jit(solution)/shard_map/dot_general | solution.py:178
  424.7 26.6 %all-gather.31.cloned.1.call-done = bf16[2048,1024]{1,0:T(8,128)(2,1)} async-done(((bf16[2048,256]{1,0:T(8,128)(2,1)}), bf16[2048,1024]{1,0:T(8,128)(2,1)}) %all-gather.31.cloned.1.call-update) | async-done | bytes 4194320 | tf_op jit(solution)/shard_map/all_gather | solution.py:125
  451.2 10.0 fusion.38
  461.8 8.0 all-gather.5
  469.9 7.1 all-gather.6
  477.0 8.3 all-gather.7
  485.4 4.0 multiply_reduce_fusion.8
  489.8 4.3 fusion.33
  496.3 4.4 multiply_reduce_fusion.1
  500.8 2.2 convert_reduce_fusion.1
  503.0 14.4 %fusion.36 = (bf16[2048]{0:T(1024)(128)(2,1)}, bf16[1024,2048]{1,0:T(8,128)(2,1)}) fusion(f32[1024,2048]{1,0:T(8,128)} %get-tuple-element.360, bf16[2048,1024]{1,0:T(8,128)(2,1)S(1)} %copy-done.27, f32[1024,1024]{1,0:T(8,128)S(1)} %get-tuple-element.351, f32[1024,2048]{1,0:T(8,128)} %get-tuple-element.374, f32[2048]{0:T(1024)S(1)} %reshape.271), kind=kOutput, calls=%fused_computation.111 | convolution fusion | flops 4329568256 | bytes 29372416 | tf_op jit(solution)/shard_map/td,fd->tf/dot_general | solution.py:204
  517.4 8.3 fusion.39
  526.3 29.2 %all-reduce.22.cloned.1.call-done = f32[1024,1024]{1,0:T(8,128)} async-done(((f32[1024,1024]{1,0:T(8,128)}), f32[1024,1024]{1,0:T(8,128)}) %all-reduce.22.cloned.1.call-update) | async-done | bytes 4194320 | tf_op jit(solution)/shard_map/psum | solution.py:211
  555.5 6.7 multiply_reduce_fusion.2
  562.2 2.1 convert_reduce_fusion
  564.3 2.0 copy-done.5
  568.6 141.3 %while.27 = (s32[]{:T(128)}, bf16[8,128,512]{2,1,0:T(8,128)(2,1)}, f32[8,512,512]{2,1,0:T(8,128)}, f32[8,512,512]{2,1,0:T(8,128)}, bf16[8,512,512]{1,2,0:T(8,128...) while((s32[]{:T(128)}, bf16[8,128,512]{2,1,0:T(8,128)(2,1)}, ...), condition=%wide.region_17.18_spmd, body=%wide.region_15.17_spmd.sunk | while | flops 340655616 | bytes 44455496 | solution.py:225
  711.2 4.5 fusion.15
  715.8 5.2 convolution_convert_fusion.2
  721.3 10.3 convolution_convert_fusion.1
  731.7 10.1 convolution_convert_fusion
  741.8 113.9 %reduce-scatter.12.cloned.1.call-done = f32[8,128,512]{2,1,0:T(8,128)} async-done(((f32[8,512,512]{2,1,0:T(8,128)}), f32[8,128,512]{2,1,0:T(8,128)}) %reduce-scatter.12.cloned.1.call-update) | async-done | bytes 2097168 | tf_op jit(solution)/shard_map/reduce_scatter | solution.py:239
  855.8 1.7 convert_element_type.304
  857.5 4.4 fusion.16
  862.0 141.5 %reduce-scatter.14.cloned.1.call-done = f32[8,128,512]{2,1,0:T(8,128)} async-done(((f32[8,512,512]{2,1,0:T(8,128)}), f32[8,128,512]{2,1,0:T(8,128)}) %reduce-scatter.14.cloned.1.call-update) | async-done | bytes 2097168 | tf_op jit(solution)/shard_map/reduce_scatter | solution.py:240
  1003.5 1.9 fusion.32
  1005.3 4.5 fusion.17
  1010.1 2.6 fusion.40
  1014.0 2.7 add_convert_fusion.1
  1016.9 18.6 %reduce-scatter.16.cloned.1.call-done = bf16[256,512]{0,1:T(8,128)(2,1)} async-done(((bf16[1024,512]{0,1:T(8,128)(2,1)}), bf16[256,512]{0,1:T(8,128)(2,1)}) %reduce-scatter.16.cloned.1.call-update) | async-done | bytes 262160 | tf_op jit(solution)/shard_map/reduce_scatter | solution.py:264
  1035.5 30.5 %reduce-scatter.22.cloned.1.call-done = bf16[512,256]{1,0:T(8,128)(2,1)} async-done(((bf16[512,1024]{1,0:T(8,128)(2,1)}), bf16[512,256]{1,0:T(8,128)(2,1)}) %reduce-scatter.22.cloned.1.call-update) | async-done | bytes 262160 | tf_op jit(solution)/shard_map/reduce_scatter | solution.py:273
  1066.0 55.8 %reduce-scatter.24.cloned.1.call-done = bf16[256,2048]{1,0:T(8,128)(2,1)} async-done(((bf16[1024,2048]{1,0:T(8,128)(2,1)}), bf16[256,2048]{1,0:T(8,128)(2,1)}) %reduce-scatter.24.cloned.1.call-update) | async-done | bytes 1048592 | tf_op jit(solution)/shard_map/reduce_scatter | solution.py:276
  1121.8 56.1 %reduce-scatter.26.cloned.1.call-done = bf16[2048,256]{1,0:T(8,128)(2,1)} async-done(((bf16[2048,1024]{1,0:T(8,128)(2,1)}), bf16[2048,256]{1,0:T(8,128)(2,1)}) %reduce-scatter.26.cloned.1.call-update) | async-done | bytes 1048592 | tf_op jit(solution)/shard_map/reduce_scatter | solution.py:279
  1177.9 30.8 %reduce-scatter.18.cloned.1.call-done = bf16[256,512]{0,1:T(8,128)(2,1)} async-done(((bf16[1024,512]{0,1:T(8,128)(2,1)}), bf16[256,512]{0,1:T(8,128)(2,1)}) %reduce-scatter.18.cloned.1.call-update) | async-done | bytes 262160 | tf_op jit(solution)/shard_map/reduce_scatter | solution.py:267
  1208.7 30.6 %reduce-scatter.20.cloned.1.call-done = bf16[256,512]{0,1:T(8,128)(2,1)} async-done(((bf16[1024,512]{0,1:T(8,128)(2,1)}), bf16[256,512]{0,1:T(8,128)(2,1)}) %reduce-scatter.20.cloned.1.call-update) | async-done | bytes 262160 | tf_op jit(solution)/shard_map/reduce_scatter | solution.py:270
  1241.8 15.3 %all-reduce.11 = (bf16[32,64]{1,0:T(8,128)(2,1)S(1)}, bf16[8,64]{1,0:T(8,128)(2,1)S(1)}, bf16[8,64]{1,0:T(8,128)(2,1)S(1)}, bf16[1024]{0:T(1024)(128)(2,1)S(1)},...) all-reduce(bf16[32,64]{1,0:T(8,128)(2,1)S(1)} %convert_element_type, ...), channel_id=12, replica_groups=mesh['shard'=4,'ctx'=4,'tp'=2] {'shard'}, use_global_device_ids=true, to_apply=%region_40.41.clone | all-reduce | flops 9216 | bytes 36864
  1257.7 19.0 %all-reduce.9 = (bf16[32,16]{1,0:T(8,128)(2,1)S(1)}, bf16[8,16]{1,0:T(8,128)(2,1)S(1)}, bf16[8,16]{1,0:T(8,128)(2,1)S(1)}, bf16[256]{0:T(256)(128)(2,1)S(1)}, bf...) all-reduce(bf16[32,16]{1,0:T(8,128)(2,1)S(1)} %constant_dynamic-sli, ...), channel_id=1, replica_groups=mesh['shard'=4,'ctx'=4,'tp'=2] {'ctx'}, use_global_device_ids=true, to_apply=%region_41.42 | all-reduce | flops 2304 | bytes 9216 | tf_op jit(solution)/shard_map/psum | solution.py:319
  1282.0 5.9 convert_add_fusion
  1287.9 102.5 %all-reduce.26.cloned.1.call-done = (bf16[256,512]{0,1:T(8,128)(2,1)}, bf16[256,512]{0,1:T(8,128)(2,1)}, bf16[256,512]{0,1:T(8,128)(2,1)}, bf16[512,256]{1,0:T(8...) async-done(((bf16[256,512]{0,1:T(8,128)(2,1)}, bf16[256,512]{0,1:T(8,128)(2,1)}, bf16[256,512]{0,1:T(8,128)(2,1)}, bf16[512,256]{1,0:T(8,128)(2,1)}, ...) | async-done | bytes 3145744 | tf_op jit(solution)/shard_map/psum | solution.py:311
  1390.4 2.0 copy.115
  1392.4 1.9 copy.116
  1394.2 1.9 copy.117
  1396.1 1.8 convert_element_type.321
  1397.9 2.8 convert_element_type.323
  (499 shorter events, 217.1 us)
Async XLA Ops:
  7.2 32.0 %all-gather.17.cloned.1.call-start = ((), (), s32[]{:S(2)}) async-start(), calls=%async_computation.8 | async-start | bytes 1310720 | tf_op jit(solution)/shard_map/all_gather | solution.py:122
  7.9 59.8 %all-gather.23.cloned.1.call-start = ((), (), s32[]{:S(2)}) async-start(), calls=%async_computation.11 | async-start | bytes 1310720 | tf_op jit(solution)/shard_map/all_gather | solution.py:121
  8.7 87.6 %all-gather.21.cloned.1.call-start = ((), (), s32[]{:S(2)}) async-start(), calls=%async_computation.10 | async-start | bytes 1310720 | tf_op jit(solution)/shard_map/all_gather | solution.py:120
  9.4 169.4 %all-gather.19.cloned.1.call-start = ((), (), s32[]{:S(2)}) async-start(), calls=%async_computation.9 | async-start | bytes 5242880 | tf_op jit(solution)/shard_map/all_gather | solution.py:164
  43.0 29.1 %copy-start.22 = (bf16[8,16]{1,0:T(8,128)(2,1)S(1)}, bf16[8,16]{1,0:T(8,128)(2,1)}, u32[]{:S(2)}) copy-start(bf16[8,16]{1,0:T(8,128)(2,1)} %param.30) | copy-start | bytes 772
  43.0 216.6 %all-gather.25.cloned.1.call-start = ((), (), s32[]{:S(2)}) async-start(), calls=%async_computation.12 | async-start | bytes 5242880 | tf_op jit(solution)/shard_map/all_gather | solution.py:163
  71.5 237.6 %all-gather.27.cloned.1.call-start = ((), (), s32[]{:S(2)}) async-start(), calls=%async_computation.13 | async-start | bytes 1310720 | tf_op jit(solution)/shard_map/all_gather | solution.py:123
  72.1 275.2 %all-reduce.18.cloned.1.call-start = ((), (), s32[]{:S(2)}) async-start(), calls=%async_computation.14 | async-start | bytes 8388608 | tf_op jit(solution)/shard_map/psum | solution.py:172
  80.4 179.3 %copy-start.23 = (s32[8]{0:T(128)S(1)}, s32[8]{0:T(128)}, u32[]{:S(2)}) copy-start(s32[8]{0:T(128)} %param.23) | copy-start | bytes 100
  309.1 4.9 copy-start.10
  314.0 9.9 copy-start.30
  314.0 17.9 %copy-start.31 = (bf16[256]{0:T(256)(128)(2,1)S(1)}, bf16[256]{0:T(256)(128)(2,1)}, u32[]{:S(2)}) copy-start(bf16[256]{0:T(256)(128)(2,1)} %param.36) | copy-start | bytes 1540
  314.0 25.0 %copy-start.32 = (bf16[256]{0:T(256)(128)(2,1)S(1)}, bf16[256]{0:T(256)(128)(2,1)}, u32[]{:S(2)}) copy-start(bf16[256]{0:T(256)(128)(2,1)} %param.35) | copy-start | bytes 1540
  314.0 82.6 %all-gather.29.cloned.1.call-start = ((), (), s32[]{:S(2)}) async-start(), calls=%async_computation.15 | async-start | bytes 5242880 | tf_op jit(solution)/shard_map/all_gather | solution.py:124
  314.8 136.4 %all-gather.31.cloned.1.call-start = ((), (), s32[]{:S(2)}) async-start(), calls=%async_computation.16 | async-start | bytes 5242880 | tf_op jit(solution)/shard_map/all_gather | solution.py:125
  315.5 174.3 %all-reduce.20.cloned.1.call-start = ((), (), s32[]{:S(2)}) async-start(), calls=%async_computation.17 | async-start | bytes 8388608 | tf_op jit(solution)/shard_map/psum | solution.py:180
  461.2 8.7 copy-start.34
  461.2 15.8 %copy-start.35 = (bf16[256]{0:T(256)(128)(2,1)S(1)}, bf16[256]{0:T(256)(128)(2,1)}, u32[]{:S(2)}) copy-start(bf16[256]{0:T(256)(128)(2,1)} %param.38) | copy-start | bytes 1540
  461.2 94.3 %all-reduce.22.cloned.1.call-start = ((), (), s32[]{:S(2)}) async-start(), calls=%async_computation.18 | async-start | bytes 8388608 | tf_op jit(solution)/shard_map/psum | solution.py:211
  503.0 14.4 %copy-start.6 = (f32[1024,1024]{1,0:T(8,128)}, f32[1024,1024]{1,0:T(8,128)S(1)}, u32[]{:S(2)}) copy-start(f32[1024,1024]{1,0:T(8,128)S(1)} %get-tuple-element.351) | copy-start | bytes 12582916
  503.0 14.4 %copy-start.26 = (bf16[1024,2048]{1,0:T(8,128)(2,1)S(1)}, bf16[1024,2048]{1,0:T(8,128)(2,1)}, u32[]{:S(2)}) copy-start(bf16[1024,2048]{1,0:T(8,128)(2,1)} %all-gather.29.cloned.1.call-done) | copy-start | bytes 12582916
  525.7 330.0 %reduce-scatter.12.cloned.1.call-start = ((), (), s32[]{:S(2)}) async-start(), calls=%async_computation.19 | async-start | bytes 10485760 | tf_op jit(solution)/shard_map/reduce_scatter | solution.py:239
  555.5 6.7 copy-start.1
  568.6 5.1 copy-start.12
  568.6 6.9 copy-start.24
  586.2 5.1 copy-start.12
  586.2 6.9 copy-start.24
  599.4 4.5 copy-start.25
  603.9 5.1 copy-start.12
  603.9 6.9 copy-start.24
  621.6 5.1 copy-start.12
  621.6 6.9 copy-start.24
  634.7 4.5 copy-start.25
  639.2 5.1 copy-start.12
  639.2 6.9 copy-start.24
  652.4 4.5 copy-start.25
  656.9 5.1 copy-start.12
  656.9 6.9 copy-start.24
  670.0 4.5 copy-start.25
  674.6 5.1 copy-start.12
  674.6 6.9 copy-start.24
  687.7 4.5 copy-start.25
  692.2 5.1 copy-start.12
  692.2 6.9 copy-start.24
  705.4 4.5 copy-start.25
  710.0 293.5 %reduce-scatter.14.cloned.1.call-start = ((), (), s32[]{:S(2)}) async-start(), calls=%async_computation.20 | async-start | bytes 10485760 | tf_op jit(solution)/shard_map/reduce_scatter | solution.py:240
  710.7 324.8 %reduce-scatter.16.cloned.1.call-start = ((), (), s32[]{:S(2)}) async-start(), calls=%async_computation.22 | async-start | bytes 1310720 | tf_op jit(solution)/shard_map/reduce_scatter | solution.py:264
  711.2 4.6 copy-start.11
  715.8 350.2 %reduce-scatter.22.cloned.1.call-start = ((), (), s32[]{:S(2)}) async-start(), calls=%async_computation.25 | async-start | bytes 1310720 | tf_op jit(solution)/shard_map/reduce_scatter | solution.py:273
  721.0 400.8 %reduce-scatter.24.cloned.1.call-start = ((), (), s32[]{:S(2)}) async-start(), calls=%async_computation.26 | async-start | bytes 5242880 | tf_op jit(solution)/shard_map/reduce_scatter | solution.py:276
  731.6 446.3 %reduce-scatter.26.cloned.1.call-start = ((), (), s32[]{:S(2)}) async-start(), calls=%async_computation.27 | async-start | bytes 5242880 | tf_op jit(solution)/shard_map/reduce_scatter | solution.py:279
  741.8 466.9 %reduce-scatter.18.cloned.1.call-start = ((), (), s32[]{:S(2)}) async-start(), calls=%async_computation.23 | async-start | bytes 1310720 | tf_op jit(solution)/shard_map/reduce_scatter | solution.py:267
  861.9 377.4 %reduce-scatter.20.cloned.1.call-start = ((), (), s32[]{:S(2)}) async-start(), calls=%async_computation.24 | async-start | bytes 1310720 | tf_op jit(solution)/shard_map/reduce_scatter | solution.py:270
  1009.9 272.1 %all-reduce.24.cloned.1.call-start = ((), (), s32[]{:S(2)}) async-start(), calls=%async_computation.21 | async-start | bytes 4194304 | tf_op jit(solution)/shard_map/psum | solution.py:262
  1016.7 222.6 %copy-start.36 = (u32[32]{0:T(128)S(1)}, u32[32]{0:T(128)}, u32[]{:S(2)}) copy-start(u32[32]{0:T(128)} %constant.141) | copy-start | bytes 388
  1016.7 224.5 %copy-start.21 = (bf16[2048]{0:T(1024)(128)(2,1)S(1)}, bf16[2048]{0:T(1024)(128)(2,1)}, u32[]{:S(2)}) copy-start(bf16[2048]{0:T(1024)(128)(2,1)} %get-tuple-element.375) | copy-start | bytes 12292
  1016.8 225.0 %copy-start.14 = (bf16[1024]{0:T(1024)(128)(2,1)S(1)}, bf16[1024]{0:T(1024)(128)(2,1)}, u32[]{:S(2)}) copy-start(bf16[1024]{0:T(1024)(128)(2,1)} %get-tuple-element.289) | copy-start | bytes 6148
  1016.8 225.0 %copy-start.15 = (bf16[1024]{0:T(1024)(128)(2,1)S(1)}, bf16[1024]{0:T(1024)(128)(2,1)}, u32[]{:S(2)}) copy-start(bf16[1024]{0:T(1024)(128)(2,1)} %get-tuple-element.284) | copy-start | bytes 6148
  1016.8 225.0 %copy-start.16 = (bf16[1024]{0:T(1024)(128)(2,1)S(1)}, bf16[1024]{0:T(1024)(128)(2,1)}, u32[]{:S(2)}) copy-start(bf16[1024]{0:T(1024)(128)(2,1)} %get-tuple-element.350) | copy-start | bytes 6148
  1016.8 225.0 %copy-start.17 = (bf16[1024]{0:T(1024)(128)(2,1)S(1)}, bf16[1024]{0:T(1024)(128)(2,1)}, u32[]{:S(2)}) copy-start(bf16[1024]{0:T(1024)(128)(2,1)} %get-tuple-element.286) | copy-start | bytes 6148
  1016.8 225.0 %copy-start.18 = (bf16[1024]{0:T(1024)(128)(2,1)S(1)}, bf16[1024]{0:T(1024)(128)(2,1)}, u32[]{:S(2)}) copy-start(bf16[1024]{0:T(1024)(128)(2,1)} %get-tuple-element.291) | copy-start | bytes 6148
  1016.8 225.0 %copy-start.19 = (bf16[1024]{0:T(1024)(128)(2,1)S(1)}, bf16[1024]{0:T(1024)(128)(2,1)}, u32[]{:S(2)}) copy-start(bf16[1024]{0:T(1024)(128)(2,1)} %get-tuple-element.352) | copy-start | bytes 6148
  1016.8 373.6 %all-reduce.26.cloned.1.call-start = ((), (), s32[]{:S(2)}) async-start(), calls=%async_computation.28 | async-start | bytes 6291456 | tf_op jit(solution)/shard_map/psum | solution.py:311
  1390.4 10.3 copy-start.9
  (36 other events, 86.6 us)
Sparse Core Ops, SparseCore 0:
  9.9 29.3 all-gather.16
  41.1 26.6 all-gather.22
  69.6 26.6 all-gather.20
  98.2 80.5 all-gather.18
  180.8 78.7 all-gather.24
  261.3 24.6 all-gather.26
  314.2 26.5 all-reduce.17
  342.7 53.8 all-gather.28
  398.6 52.5 all-gather.30
  461.3 28.4 all-reduce.19
  525.9 29.5 all-reduce.21
  710.1 145.6 reduce-scatter.11
  858.2 145.1 reduce-scatter.13
  1007.0 28.4 reduce-scatter.15
  1038.3 27.7 reduce-scatter.21
  1069.1 52.6 reduce-scatter.23
  1125.2 52.6 reduce-scatter.25
  1180.9 27.7 reduce-scatter.17
  1211.6 27.7 reduce-scatter.19
  1242.2 21.1 all-reduce.23
  1266.3 124.0 all-reduce.25
where the time goes:
time: 1420 us; the launch traced here: 1410 us
  waiting for transfers between devices  901 us (63%)
  matrix products  171 us (12%)
  local copies, waits for them, and re-layouts  136 us (10%)
  blocking collectives  107 us (8%)
  other arithmetic  74.4 us (5%)
  between operations  16.3 us (1%)
    reduce_scatter x1, waiting for transfers between devices, body(): lax.psum_scatter(value_grad_all, 'ctx', scatter_dimension=1, tiled=True)  141 us
    reduce_scatter x1, waiting for transfers between devices, body(): lax.psum_scatter(key_grad_all, 'ctx', scatter_dimension=1, tiled=True)  114 us
    psum x1, waiting for transfers between devices, body(): lax.psum(summed[0].astype(jnp.bfloat16), 'ctx').astype(jnp.float32)  102 us
    all_gather x1, waiting for transfers between devices, body(): lax.all_gather(key_seqs, 'ctx', axis=1, tiled=True)  80.8 us
    all_gather x1, waiting for transfers between devices, body(): lax.all_gather(value_seqs, 'ctx', axis=1, tiled=True)  78.8 us
    dynamic_slice x72, local copies, waits for them, and re-layouts, body(): lax.map(lambda pieces: attend(pieces[0], pieces[1], pieces[2], pieces[3])...  56.8 us
    reduce_scatter x1, waiting for transfers between devices, body(): lax.psum_scatter(reduce_weight_grad.astype(jnp.bfloat16), 'shard', scatte...  56.1 us
    reduce_scatter x1, waiting for transfers between devices, body(): lax.psum_scatter(expand_weight_grad.astype(jnp.bfloat16), 'shard', scatte...  55.8 us
  transfers between devices with their start and end apart: 21, of which 18 were waited for; matrix products, arithmetic and copies ran while one was open for 12% of the time, Pallas kernels for 0%

commit v1 on v0

v1 whole, which is shorter than its diff:
```python
import functools

import jax
import jax.numpy as jnp
from jax import lax
from jax.experimental import pallas as pl
from jax.experimental.pallas import tpu as pltpu
from jax.sharding import PartitionSpec as P

HD = 64
UNIT = 512
EPSILON = 1e-05
MASKED = -1e30
MESH = pl.DeviceIdType.MESH
F32 = jnp.float32
BF16 = jnp.bfloat16


def place():
    return lax.axis_index("shard"), lax.axis_index("ctx"), lax.axis_index("tp")


def rcopy(src, dst, send, recv, dev):
    return pltpu.make_async_remote_copy(
        src_ref=src, dst_ref=dst, send_sem=send, recv_sem=recv, device_id=dev, device_id_type=MESH
    )


def greet(devices):
    barrier = pltpu.get_barrier_semaphore()
    for dev in devices:
        pl.semaphore_signal(barrier, inc=1, device_id=dev, device_id_type=MESH)
    pl.semaphore_wait(barrier, len(devices))


def partners(n, nz):
    s, z, c = place()
    return (
        [(s ^ k, z, c) for k in range(1, n)]
        + [(s, z, 1 - c)]
        + [(s, lax.rem(z + k, nz), c) for k in range(1, nz)]
    )


def gather_kernel(
    n, nz, own_ref, x_ref, g_ref, full_ref, xs_ref, gs_ref,
    own_send, own_recv, fwd_send, fwd_recv, core_send, core_recv, act_send, act_recv, local_sem,
):
    s, z, c = place()
    units, rows, width = own_ref.shape
    half = rows // 2
    greet(partners(n, nz))
    mine = pl.ds(pl.multiple_of(s * rows, rows), rows)
    block = x_ref.shape[1]
    zrows = pl.ds(pl.multiple_of(z * block, block), block)

    def block_at(k):
        return pl.ds(pl.multiple_of((s ^ k) * rows, rows), rows)

    def half_at(k, h):
        return pl.ds(pl.multiple_of((s ^ k) * rows + h * half, half), half)

    keep = pltpu.make_async_copy(own_ref, full_ref.at[c, :, mine, :], local_sem.at[0])
    keep.start()
    share = rcopy(
        own_ref, full_ref.at[c, :, mine, :], core_send.at[units, 0], core_recv.at[units, 0], (s, z, 1 - c)
    )
    share.start()

    def act(k, which):
        src, dst = ((x_ref, xs_ref), (g_ref, gs_ref))[which]
        to = lax.rem(z + k, nz)
        return rcopy(
            src.at[2 * to + c], dst.at[zrows, :], act_send.at[which, k], act_recv.at[which, k], (s, to, c)
        )

    def act_in(k, which):
        dst = (xs_ref, gs_ref)[which]
        src = lax.rem(z + nz - k, nz)
        at = dst.at[pl.ds(pl.multiple_of(src * block, block), block), :]
        return rcopy(at, at, act_send.at[which, k], act_recv.at[which, k], (s, src, c))

    for which in range(2):
        for k in range(1, nz):
            act(k, which).start()
    keep_x = pltpu.make_async_copy(x_ref.at[2 * z + c], xs_ref.at[zrows, :], local_sem.at[1])
    keep_g = pltpu.make_async_copy(g_ref.at[2 * z + c], gs_ref.at[zrows, :], local_sem.at[2])
    keep_x.start()
    keep_g.start()
    direct = [1, 2] if n == 4 else list(range(1, n))

    def own_copy(u, k):
        return rcopy(
            own_ref.at[u], full_ref.at[c, u, mine, :], own_send.at[u, k], own_recv.at[u, k], (s ^ k, z, c)
        )

    def own_in(u, k):
        at = full_ref.at[c, u, block_at(k), :]
        return rcopy(at, at, own_send.at[u, k], own_recv.at[u, k], (s ^ k, z, c))

    def fwd_copy(u, h):
        at = full_ref.at[c, u, half_at(2 - h, h), :]
        return rcopy(at, at, fwd_send.at[u, h], fwd_recv.at[u, h], (s ^ (1 + h), z, c))

    def fwd_in(u, h):
        at = full_ref.at[c, u, half_at(3, h), :]
        return rcopy(at, at, fwd_send.at[u, h], fwd_recv.at[u, h], (s ^ (1 + h), z, c))

    def core_copy(u, k):
        at = full_ref.at[c, u, block_at(k), :]
        return rcopy(at, at, core_send.at[u, k], core_recv.at[u, k], (s, z, 1 - c))

    def core_in(u, k):
        at = full_ref.at[1 - c, u, block_at(k), :]
        return rcopy(at, at, core_send.at[u, k], core_recv.at[u, k], (s, z, 1 - c))

    ahead = 2
    for u in range(ahead):
        for k in direct:
            own_copy(u, k).start()

    def step(u, carry):
        @pl.when(u + ahead < units)
        def _():
            for k in direct:
                own_copy(u + ahead, k).start()

        for k in direct:
            own_in(u, k).wait_recv()
            if n == 4:
                fwd_copy(u, 2 - k).start()
            core_copy(u, k).start()
        if n == 4:
            @pl.when(u > 0)
            def _():
                for h in range(2):
                    fwd_in(u - 1, h).wait_recv()
                core_copy(u - 1, 3).start()

        return carry

    lax.fori_loop(0, units, step, 0)
    if n == 4:
        for h in range(2):
            fwd_in(units - 1, h).wait_recv()
        core_copy(units - 1, 3).start()

    def finish(u, carry):
        for k in direct:
            own_copy(u, k).wait_send()
        if n == 4:
            for h in range(2):
                fwd_copy(u, h).wait_send()
        for k in range(1, n):
            core_copy(u, k).wait_send()
            core_in(u, k).wait_recv()
        return carry

    lax.fori_loop(0, units, finish, 0)
    share.wait_send()
    theirs = full_ref.at[1 - c, :, mine, :]
    rcopy(theirs, theirs, core_send.at[units, 0], core_recv.at[units, 0], (s, z, 1 - c)).wait_recv()
    for which in range(2):
        for k in range(1, nz):
            act(k, which).wait_send()
            act_in(k, which).wait_recv()
    keep.wait()
    keep_x.wait()
    keep_g.wait()


def gather(n, nz, own, x_low, g_low):
    units, rows, width = own.shape
    block, model = x_low.shape[1:]
    return pl.pallas_call(
        functools.partial(gather_kernel, n, nz),
        name="gather_weights",
        out_shape=(
            jax.ShapeDtypeStruct((2, units, rows * n, width), BF16),
            jax.ShapeDtypeStruct((nz * block, model), BF16),
            jax.ShapeDtypeStruct((nz * block, model), BF16),
        ),
        in_specs=[pl.BlockSpec(memory_space=pl.ANY)] * 3,
        out_specs=[pl.BlockSpec(memory_space=pl.ANY)] * 3,
        scratch_shapes=[
            pltpu.SemaphoreType.DMA((units, n)),
            pltpu.SemaphoreType.DMA((units, n)),
            pltpu.SemaphoreType.DMA((units, 2)),
            pltpu.SemaphoreType.DMA((units, 2)),
            pltpu.SemaphoreType.DMA((units + 1, n)),
            pltpu.SemaphoreType.DMA((units + 1, n)),
            pltpu.SemaphoreType.DMA((2, nz)),
            pltpu.SemaphoreType.DMA((2, nz)),
            pltpu.SemaphoreType.DMA((3,)),
        ],
        compiler_params=pltpu.CompilerParams(collective_id=0, has_side_effects=True),
    )(own, x_low, g_low)


def reduce_kernel(
    n, nz, part_ref, out_ref, in_ref, grad_ref, outs_ref, ins_ref,
    stage, got, total, near, far, pair_sum, up, across, down, block_out,
    core_send, core_recv, near_send, near_recv, far_send, far_recv, z_send, z_recv,
    act_send, act_recv, pass_send, pass_recv, load_sem, store_sem, keep_sem,
):
    s, z, c = place()
    units = part_ref.shape[1]
    rows = total.shape[1] // n
    half = rows // 2
    greet(partners(n, nz))
    block = outs_ref.shape[1]
    zrows = pl.ds(pl.multiple_of(z * block, block), block)

    def act(k, which):
        src, dst = ((out_ref, outs_ref), (in_ref, ins_ref))[which]
        to = lax.rem(z + k, nz)
        at = src.at[pl.ds(pl.multiple_of(to * block, block), block), :]
        return rcopy(at, dst.at[2 * z + c], act_send.at[which, k], act_recv.at[which, k], (s, to, c))

    def act_in(k, which):
        dst = (outs_ref, ins_ref)[which]
        src = lax.rem(z + nz - k, nz)
        at = dst.at[2 * src + c]
        return rcopy(at, at, act_send.at[which, k], act_recv.at[which, k], (s, src, c))

    def pass_copy(k, which):
        dst = (outs_ref, ins_ref)[which]
        src = lax.rem(z + nz - k, nz)
        at = dst.at[2 * src + c]
        return rcopy(at, at, pass_send.at[which, k], pass_recv.at[which, k], (s, z, 1 - c))

    def pass_in(k, which):
        dst = (outs_ref, ins_ref)[which]
        src = lax.rem(z + nz - k, nz)
        at = dst.at[2 * src + 1 - c]
        return rcopy(at, at, pass_send.at[which, k], pass_recv.at[which, k], (s, z, 1 - c))

    for which in range(2):
        src, dst = ((out_ref, outs_ref), (in_ref, ins_ref))[which]
        for k in range(1, nz):
            act(k, which).start()
        pltpu.make_async_copy(src.at[zrows, :], dst.at[2 * z + c], keep_sem.at[which]).start()

    def core_copy(u):
        return rcopy(
            part_ref.at[1 - c, u], got.at[u], core_send.at[u], core_recv.at[u], (s, z, 1 - c)
        )

    def load(u):
        return pltpu.make_async_copy(part_ref.at[c, u], stage.at[lax.rem(u, 2)], load_sem.at[lax.rem(u, 2)])

    def rows_of(k):
        return pl.ds(pl.multiple_of((s ^ k) * rows, rows), rows)

    def half_of(k, h):
        return pl.ds(pl.multiple_of((s ^ k) * rows + h * half, half), half)

    def near_copy(u, h, i):
        k = (1 + h, 3)[i]
        return rcopy(
            total.at[lax.rem(u, 2), half_of(k, h), :], near.at[u, h, i],
            near_send.at[u, h, i], near_recv.at[u, h, i], (s ^ (1 + h), z, c),
        )

    def far_copy(u, h):
        return rcopy(
            pair_sum.at[u, h], far.at[u, h], far_send.at[u, h], far_recv.at[u, h], (s ^ (2 - h), z, c)
        )

    def straight(u, k):
        return rcopy(
            total.at[lax.rem(u, 2), rows_of(k), :], near.at[u, k - 1],
            near_send.at[u, k - 1], near_recv.at[u, k - 1], (s ^ k, z, c),
        )

    def z_to(u, src, dst, i, to):
        return rcopy(src.at[u], dst.at[u], z_send.at[u, i], z_recv.at[u, i], (s, to, c))

    last = nz - 1
    edge = jnp.logical_or(z == 0, z == last)
    inner = jnp.where(z == 0, 1, nz - 2)
    outer = jnp.where(z == 1, 0, last)
    other = jnp.where(z == 1, 2, 1)

    def first(u):
        core_copy(u).start()
        load(u).start()

    def second(u):
        @pl.when(u >= 2)
        def _():
            if n == 4:
                for h in range(2):
                    for i in range(2):
                        near_copy(u - 2, h, i).wait_send()
            else:
                for k in range(1, n):
                    straight(u - 2, k).wait_send()
        load(u).wait()
        core_copy(u).wait_recv()
        slot = lax.rem(u, 2)

        def add(i, carry):
            at = pl.ds(pl.multiple_of(i * rows, rows), rows)
            total[slot, at, :] = (stage[slot, at, :].astype(F32) + got[u, at, :].astype(F32)).astype(BF16)
            return carry

        lax.fori_loop(0, n, add, 0)
        if n == 4:
            for h in range(2):
                for i in range(2):
                    near_copy(u, h, i).start()
        else:
            for k in range(1, n):
                straight(u, k).start()

    def third(u):
        slot = lax.rem(u, 2)
        if n == 4:
            for h in range(2):
                for i in range(2):
                    near_copy(u, h, i).wait_recv()
                pair_sum[u, h] = (
                    total[slot, half_of(2 - h, h), :].astype(F32) + near[u, h, 1].astype(F32)
                ).astype(BF16)
                far_copy(u, h).start()
        else:
            for k in range(1, n):
                straight(u, k).wait_recv()

    def fourth(u):
        slot = lax.rem(u, 2)
        if n == 4:
            for h in range(2):
                far_copy(u, h).wait_recv()
                block_out[u, h * half : (h + 1) * half] = (
                    total[slot, half_of(0, h), :].astype(F32)
                    + near[u, h, 0].astype(F32)
                    + far[u, h].astype(F32)
                ).astype(BF16)
        else:
            acc = total[slot, rows_of(0), :].astype(F32)
            for k in range(1, n):
                acc = acc + near[u, k - 1].astype(F32)
            block_out[u] = acc.astype(BF16)

        @pl.when(edge)
        def _():
            z_to(u, block_out, up, 0, inner).start()

    def fifth(u):
        @pl.when(jnp.logical_not(edge))
        def _():
            z_to(u, block_out, up, 0, outer).wait_recv()
            block_out[u] = (block_out[u].astype(F32) + up[u].astype(F32)).astype(BF16)
            z_to(u, block_out, across, 1, other).start()

    def sixth(u):
        @pl.when(jnp.logical_not(edge))
        def _():
            z_to(u, block_out, across, 1, other).wait_recv()
            down[u] = (block_out[u].astype(F32) + across[u].astype(F32)).astype(BF16)
            z_to(u, down, down, 2, outer).start()

    def seventh(u):
        @pl.when(edge)
        def _():
            z_to(u, down, down, 2, inner).wait_recv()

        pltpu.make_async_copy(down.at[u], grad_ref.at[u], store_sem.at[u]).start()

    stages = [first, second, third, fourth, fifth, sixth, seventh]

    def step(t, carry):
        for i, stage_of in reversed(list(enumerate(stages))):
            @pl.when(jnp.logical_and(t >= i, t - i < units))
            def _(stage_of=stage_of, i=i):
                stage_of(t - i)

        @pl.when(t == 3)
        def _():
            for which in range(2):
                for k in range(1, nz):
                    act_in(k, which).wait_recv()
                    pass_copy(k, which).start()
                src, dst = ((out_ref, outs_ref), (in_ref, ins_ref))[which]
                pltpu.make_async_copy(src.at[zrows, :], dst.at[2 * z + c], keep_sem.at[which]).wait()
                at = dst.at[2 * z + c]
                rcopy(at, at, pass_send.at[which, 0], pass_recv.at[which, 0], (s, z, 1 - c)).start()

        return carry

    lax.fori_loop(0, units + len(stages) - 1, step, 0)

    def finish(u, carry):
        core_copy(u).wait_send()
        if n == 4:
            for h in range(2):
                far_copy(u, h).wait_send()

        @pl.when(edge)
        def _():
            z_to(u, block_out, up, 0, inner).wait_send()

        @pl.when(jnp.logical_not(edge))
        def _():
            z_to(u, block_out, across, 1, other).wait_send()
            z_to(u, down, down, 2, outer).wait_send()

        pltpu.make_async_copy(down.at[u], grad_ref.at[u], store_sem.at[u]).wait()
        return carry

    lax.fori_loop(0, units, finish, 0)
    for u in (units - 2, units - 1):
        if n == 4:
            for h in range(2):
                for i in range(2):
                    near_copy(u, h, i).wait_send()
        else:
            for k in range(1, n):
                straight(u, k).wait_send()
    for which in range(2):
        for k in range(1, nz):
            act(k, which).wait_send()
        for k in range(nz):
            pass_copy(k, which).wait_send()
            pass_in(k, which).wait_recv()


def reduce(n, nz, parts, out_low, in_low):
    _, units, model, width = parts.shape
    rows = model // n
    half = rows // 2
    block = out_low.shape[0] // nz
    near_shape = (units, 2, 2, half, width) if n == 4 else (units, n - 1, rows, width)
    near_sems = (units, 2, 2) if n == 4 else (units, n - 1)
    dma = pltpu.SemaphoreType.DMA
    return pl.pallas_call(
        functools.partial(reduce_kernel, n, nz),
        name="reduce_grads",
        out_shape=(
            jax.ShapeDtypeStruct((units, rows, width), BF16),
            jax.ShapeDtypeStruct((2 * nz, block, model), BF16),
            jax.ShapeDtypeStruct((2 * nz, block, model), BF16),
        ),
        in_specs=[pl.BlockSpec(memory_space=pl.ANY)] * 3,
        out_specs=[pl.BlockSpec(memory_space=pl.ANY)] * 3,
        scratch_shapes=[
            pltpu.VMEM((2, model, width), BF16),
            pltpu.VMEM((units, model, width), BF16),
            pltpu.VMEM((2, model, width), BF16),
            pltpu.VMEM(near_shape, BF16),
            pltpu.VMEM((units, 2, half, width), BF16),
            pltpu.VMEM((units, 2, half, width), BF16),
            pltpu.VMEM((units, rows, width), BF16),
            pltpu.VMEM((units, rows, width), BF16),
            pltpu.VMEM((units, rows, width), BF16),
            pltpu.VMEM((units, rows, width), BF16),
            dma((units,)), dma((units,)),
            dma(near_sems), dma(near_sems),
            dma((units, 2)), dma((units, 2)),
            dma((units, 3)), dma((units, 3)),
            dma((2, nz)), dma((2, nz)),
            dma((2, nz)), dma((2, nz)),
            dma((2,)), dma((units,)), dma((2,)),
        ],
        compiler_params=pltpu.CompilerParams(
            collective_id=1, has_side_effects=True, vmem_limit_bytes=58 * 2**20
        ),
    )(parts, out_low, in_low)


def layer_norm(hidden):
    row_mean = jnp.mean(hidden, -1, keepdims=True)
    centred = hidden - row_mean
    inv_std = lax.rsqrt(jnp.mean(centred * centred, -1, keepdims=True) + EPSILON)
    return centred * inv_std, inv_std


def norm_back(gradient, normed, inv_std, gain):
    scaled = gradient * gain
    back = (
        scaled
        - jnp.mean(scaled, -1, keepdims=True)
        - normed * jnp.mean(scaled * normed, -1, keepdims=True)
    ) * inv_std
    return back, jnp.sum(gradient * normed, 0), jnp.sum(gradient, 0)


def mm(form, a, b):
    return jnp.einsum(form, a, b, preferred_element_type=F32)


def body(n, nz, inputs, lengths, wq, wk, wv, wo, we, wr, qb, vb, eb, ob, rb, g1, s1, g2, s2, cotangent):
    z, c = lax.axis_index("ctx"), lax.axis_index("tp")
    s = lax.axis_index("shard")
    seqs, block, model = inputs.shape
    rows = wq.shape[0]
    heads_half = qb.shape[0]
    heads = 2 * heads_half
    hidden_half = we.shape[1]

    def split(w):
        return w.reshape(rows, -1, UNIT).swapaxes(0, 1)

    own = jnp.concatenate([split(w) for w in (wq, wk, wv, wo.T, we, wr.T)], 0)
    units = own.shape[0]
    e_units = hidden_half // UNIT
    packed = jnp.concatenate([v.reshape(-1) for v in (qb, vb, eb, ob, rb, g1, s1, g2, s2)])
    packed = lax.all_gather(packed, ("shard", "tp"), axis=0).astype(F32).reshape(n, 2, -1)
    sizes = [v.size for v in (qb, vb, eb, ob, rb, g1, s1, g2, s2)]
    starts = [sum(sizes[:i]) for i in range(len(sizes))]

    def unpack(i, shape):
        piece = packed[:, :, starts[i] : starts[i] + sizes[i]]
        if shape is None:
            return piece[:, 0].reshape(-1)
        return piece.reshape(n, 2, shape[0], shape[1]).transpose(1, 2, 0, 3).reshape(-1)

    q_bias, v_bias, e_bias = unpack(0, qb.shape), unpack(1, vb.shape), unpack(2, eb.shape)
    o_bias, r_bias, gain1, shift1, gain2, shift2 = [unpack(i, None) for i in range(3, 9)]

    full, x_low, cot = gather(n, nz, own, inputs.astype(BF16), cotangent.astype(BF16))
    length = lengths[2 * z + c]
    slots = nz * block
    live = jnp.arange(slots) < length
    w_all = [full[:, i].transpose(1, 0, 2).reshape(model, -1) for i in range(4)]
    we_f = full[:, 4 : 4 + e_units].transpose(2, 0, 1, 3).reshape(model, -1)
    wr_f = full[:, 4 + e_units :].transpose(2, 0, 1, 3).reshape(model, -1)
    q = (mm("td,dc->tc", x_low, w_all[0]) + q_bias).astype(BF16)
    k = mm("td,dc->tc", x_low, w_all[1]).astype(BF16)
    v = (mm("td,dc->tc", x_low, w_all[2]) + v_bias).astype(BF16)
    qh, kh, vh = [a.reshape(slots, heads, HD) for a in (q, k, v)]
    scores = mm("qhe,khe->hqk", qh, kh) * HD**-0.5
    scores = jnp.where(live[None, None, :], scores, MASKED)
    probs = jax.nn.softmax(scores, -1)
    p_low = probs.astype(BF16)
    o = mm("hqk,khe->qhe", p_low, vh).reshape(slots, model).astype(BF16)
    first = x_low.astype(F32) + mm("tc,dc->td", o, w_all[3]) + o_bias
    n1, r1 = layer_norm(first)
    u = n1 * gain1 + shift1
    u_low = u.astype(BF16)
    pre = mm("td,df->tf", u_low, we_f) + e_bias
    gelu = lambda t: jax.nn.gelu(t, approximate=False)
    h = gelu(pre).astype(BF16)
    second = u + mm("tf,df->td", h, wr_f) + r_bias
    n2, r2 = layer_norm(second)
    out = n2 * gain2 + shift2

    grad = cot.astype(F32) * live[:, None].astype(F32)
    dsecond, dgain2, dshift2 = norm_back(grad, n2, r2, gain2)
    dz = dsecond.astype(BF16)
    drb = jnp.sum(dz.astype(F32), 0)
    dwr = mm("td,tf->df", dz, h)
    dh = mm("td,df->tf", dz, wr_f)
    dpre = jax.vjp(gelu, pre)[1](dh)[0].astype(BF16)
    deb = jnp.sum(dpre.astype(F32), 0)
    dwe = mm("td,tf->df", u_low, dpre)
    du = dsecond + mm("tf,df->td", dpre, we_f)
    dfirst, dgain1, dshift1 = norm_back(du, n1, r1, gain1)
    db = dfirst.astype(BF16)
    dob = jnp.sum(db.astype(F32), 0)
    dwo = mm("td,tc->dc", db, o)
    do = mm("td,dc->tc", db, w_all[3]).astype(BF16).reshape(slots, heads, HD)
    dv = mm("hqk,qhe->khe", p_low, do).reshape(slots, model).astype(BF16)
    dp = mm("qhe,khe->hqk", do, vh)
    ds = (probs * (dp - jnp.sum(dp * probs, -1, keepdims=True))).astype(BF16)
    dq = (mm("hqk,khe->qhe", ds, kh) * HD**-0.5).reshape(slots, model).astype(BF16)
    dk = (mm("hqk,qhe->khe", ds, qh) * HD**-0.5).reshape(slots, model).astype(BF16)
    dqb = jnp.sum(dq.astype(F32), 0)
    dvb = jnp.sum(dv.astype(F32), 0)
    dws = [mm("td,tc->dc", x_low, t) for t in (dq, dk, dv)]
    dx = dfirst + mm("tc,dc->td", dq, w_all[0]) + mm("tc,dc->td", dk, w_all[1]) + mm("tc,dc->td", dv, w_all[2])

    def unit_form(w):
        return w.astype(BF16).reshape(model, 2, -1, UNIT).transpose(1, 2, 0, 3)

    order = [unit_form(w) for w in (dwr, dwe, dwo, *dws)]
    parts = jnp.concatenate(order, 1)
    grads, outs, ins = reduce(n, nz, parts, out.astype(BF16), dx.astype(BF16))
    grads = grads.astype(F32)

    def joined(i, count):
        return grads[i : i + count].swapaxes(0, 1).reshape(rows, -1)

    dwr_s, dwe_s = joined(0, e_units), joined(e_units, e_units)
    dwo_s, dwq_s, dwk_s, dwv_s = [joined(2 * e_units + i, 1) for i in range(4)]
    small = jnp.concatenate([dqb, dvb, deb, dob, drb, dgain1, dshift1, dgain2, dshift2])
    small = lax.psum(small, ("shard", "ctx", "tp"))
    per = model // n
    he = HD // n
    vectors = []
    at = 0
    for size, heads_of in ((model, heads), (model, heads), (2 * hidden_half, eb.shape[0] * 2)):
        m = small[at : at + size].reshape(2, heads_of // 2, n, he)
        m = lax.dynamic_slice(m, (c, 0, s, 0), (1, heads_of // 2, 1, he))
        vectors.append(m.reshape(heads_of // 2, he))
        at += size
    for _ in range(6):
        vectors.append(lax.dynamic_slice(small, (at + s * per,), (per,)))
        at += model
    return (
        outs.astype(F32), ins.astype(F32),
        dwq_s, dwk_s, dwv_s, dwo_s.T, dwe_s, dwr_s.T, *vectors,
    )


def solution(mesh):
    w, wt, v = P("shard", "tp"), P("tp", "shard"), P("shard")
    rows = P("shard", "ctx", None)
    return jax.shard_map(
        functools.partial(body, mesh.shape["shard"], mesh.shape["ctx"]),
        mesh=mesh,
        in_specs=(rows, v, w, w, w, wt, w, wt, wt, wt, wt, v, v, v, v, v, v, rows),
        out_specs=(rows, rows, w, w, w, wt, w, wt, wt, wt, wt, v, v, v, v, v, v),
        check_vma=False,
    )
```

time: 1420 us -> 699 us (0.49)
  waiting for transfers between devices: 901 us -> 0 us
  Pallas kernels: 0 us -> 280 us
  blocking collectives: 107 us -> 49.6 us
  other arithmetic: 74.4 us -> 26.5 us
  local copies, waits for them, and re-layouts: 136 us -> 177 us
  matrix products: 171 us -> 153 us
  between operations: 16.3 us -> 1.53 us
    reduce_scatter x8 -> x0, waiting for transfers between devices: 478 us -> none  [the longest x1 141 us: body(): lax.psum_scatter(value_grad_all, 'ctx', scatter_dimension=1, tiled=True)]
    all_gather x8 -> x0, waiting for transfers between devices: 287 us -> none  [the longest x1 80.8 us: body(): lax.all_gather(key_seqs, 'ctx', axis=1, tiled=True)]
    pallas_call x0 -> x2, Pallas kernels: none -> 280 us  [the longest x1 161 us: reduce(): pl.pallas_call(functools.partial(reduce_kernel, n, nz), name='reduce_grad...]
    psum x5 -> x0, waiting for transfers between devices: 132 us -> none  [the longest x1 102 us: body(): lax.psum(summed[0].astype(jnp.bfloat16), 'ctx').astype(jnp.float32)]
    all_gather x9 -> x1, blocking collectives: 72.5 us -> 10.7 us  [body(): lax.all_gather(packed, ('shard', 'tp'), axis=0).astype(F32)]
    transpose x0 -> x13, local copies, waits for them, and re-layouts: none -> 58.8 us  [the longest x2 22.8 us: body(): wr_f = full[:, 4 + e_units:].transpose(2, 0, 1, 3).reshape(model, -1)]
    dynamic_slice x72 -> x6, local copies, waits for them, and re-layouts: 56.8 us -> 3.9 us  [the longest x4 1.9 us: body(): m = lax.dynamic_slice(m, (c, 0, s, 0), (1, heads_of // 2, 1, he))]
    dynamic_update_slice x56 -> x0, local copies, waits for them, and re-layouts: 52.1 us -> none  [the longest x24 37.6 us: body(): lax.map(lambda pieces: attend_back(pieces[0], pieces[1], pieces[2], piece...]
  transfers between devices with their start and end apart: 21 -> 0, of which waited for: 18 -> 0; matrix products, arithmetic and copies ran while one was open for 12% -> 0% of each run, Pallas kernels for 0% -> 0%
where the time goes in v1:
time: 699 us; the launch traced here: 687 us
  Pallas kernels  280 us (40%)
  local copies, waits for them, and re-layouts  177 us (25%)
  matrix products  153 us (22%)
  blocking collectives  49.6 us (7%)
  other arithmetic  26.5 us (4%)
    pallas_call x1, Pallas kernels, reduce(): pl.pallas_call(functools.partial(reduce_kernel, n, nz), name='reduce_grad...  161 us
    dot_general x23, matrix products, mm(): return jnp.einsum(form, a, b, preferred_element_type=F32)  143 us
    pallas_call x1, Pallas kernels, gather(): pl.pallas_call(functools.partial(gather_kernel, n, nz), name='gather_weig...  118 us
    psum x1, blocking collectives, body(): small = lax.psum(small, ('shard', 'ctx', 'tp'))  38.9 us
    reshape x6, local copies, waits for them, and re-layouts, unit_form(): return w.astype(BF16).reshape(model, 2, -1, UNIT).transpose(1, 2, 0, 3)  38.3 us
    unnamed x110, local copies, waits for them, and re-layouts  37.4 us
    convert_element_type x2, local copies, waits for them, and re-layouts, unit_form(): return w.astype(BF16).reshape(model, 2, -1, UNIT).transpose(1, 2, 0, 3)  23.9 us
    transpose x2, local copies, waits for them, and re-layouts, body(): wr_f = full[:, 4 + e_units:].transpose(2, 0, 1, 3).reshape(model, -1)  22.8 us

profile of v1, /device:TPU:0, one launch (start us, length us, event | category | flops | bytes accessed | tf_op | source)
XLA Modules:
  0.0 687.4 jit_solution(9774240820059675494)
XLA Ops:
  10.6 10.7 %all-gather.1 = bf16[8,1,2304]{2,1,0:T(2,128)(2,1)S(1)} all-gather(bf16[1,1,2304]{2,1,0:T(2,128)(2,1)S(1)} %reshape.276), channel_id=2, replica_groups=mesh['shard'=4,'ctx'=4,'tp'=2] {'shard','tp'}, dimensions={0}, use_global_device_ids=true | all-gather | bytes 41472 | tf_op jit(solution)/shard_map/all_gather | solution.py:510
  23.4 1.5 copy.119
  26.0 4.0 convert_element_type.150.x_ref
  30.0 1.6 convert_element_type.151.g_ref
  36.6 118.3 %gather_weights.1 = (bf16[2,12,1024,512]{3,2,1,0:T(8,128)(2,1)}, bf16[512,1024]{1,0:T(8,128)(2,1)}, bf16[512,1024]{1,0:T(8,128)(2,1)}) custom-call(bf16[12,256,512]{2,1,0:T(8,128)(2,1)} %bitcast_dynamic-update-slice_fusion.6.own_ref, bf16[8,128,1024]{2,1,0:T(8,128)(2,1)} %convert_element_type.150.x_ref, bf16[8,128,1024]{2,1,0:T(8,128)(2,1)} %convert_element_type.151.g_ref), custom_call_target="tpu_custom_call" | custom-call | tf_op jit(solution)/shard_map/gather_weights/pallas_call | solution.py:175
  154.9 5.7 slice_bitcast_fusion.4
  160.6 11.3 %slice_bitcast_fusion = (bf16[1024,2,4,512]{3,0,2,1:T(8,128)(2,1)}, bf16[1024,2,4,512]{3,0,2,1:T(8,128)(2,1)}) fusion(bf16[2,12,1024,512]{3,2,1,0:T(8,128)(2,1)} %get-tuple-element.25), kind=kLoop, calls=%fused_computation.12 | loop fusion | bytes 33554432 | tf_op jit(solution)/shard_map/transpose | solution.py:529
  171.9 11.5 %copy.135 = bf16[1024,2,4,512]{0,3,2,1:T(8,128)(2,1)} copy(bf16[1024,2,4,512]{3,0,2,1:T(8,128)(2,1)} %get-tuple-element.111) | data formatting | bytes 16777216 | tf_op jit(solution)/shard_map/transpose | solution.py:529
  183.4 2.4 copy.132
  185.8 3.0 copy.129
  188.8 2.3 convolution_convert_fusion.7
  191.1 1.5 copy.130
  192.6 3.4 copy.126
  196.0 4.2 add_convert_fusion.3
  200.2 2.3 copy.128
  202.5 3.0 copy.123
  205.5 4.2 add_convert_fusion.4
  209.8 2.3 copy.125
  212.0 11.6 %copy.133 = bf16[1024,2,4,512]{0,3,2,1:T(8,128)(2,1)} copy(bf16[1024,2,4,512]{3,0,2,1:T(8,128)(2,1)} %get-tuple-element.112) | data formatting | bytes 16777216 | tf_op jit(solution)/shard_map/transpose | solution.py:528
  223.6 10.3 %fusion.45 = (f32[16,512]{1,0:T(8,128)S(1)}, f32[16,512,512]{1,2,0:T(8,128)}) fusion(pred[512]{0:T(512)(128)(4,1)S(1)} %get-tuple-element.156, bf16[512,16,64]{0,2,1:T(8,128)(2,1)S(1)} %bitcast.181, bf16[512,16,64]{0,2,1:T(8,128)(2,1)S(1)} %bitcast.176), kind=kOutput, calls=%fused_computation.135 | convolution fusion | flops 553648640 | bytes 18907648 | tf_op jit(solution)/shard_map/sub | solution.py:536
  234.0 7.5 %fusion.21 = bf16[16,64,512]{2,1,0:T(8,128)(2,1)S(1)} fusion(bf16[512,16,64]{0,2,1:T(8,128)(2,1)S(1)} %bitcast.192, f32[16,512,512]{1,2,0:T(8,128)} %get-tuple-element.141, f32[16,512]{1,0:T(8,128)S(1)} %get-tuple-element.140), kind=kOutput, calls=%fused_computation.85 | convolution fusion | flops 545783808 | bytes 18907136 | tf_op jit(solution)/shard_map/hqk,khe->qhe/dot_general | solution.py:491
  241.5 1.4 fusion.46
  243.4 30.7 %multiply_convert_fusion.1 = (bf16[512,4096]{1,0:T(8,128)(2,1)S(1)}, f32[512,4096]{1,0:T(8,128)}, f32[512,4096]{1,0:T(8,128)}) fusion(f32[4096]{0:T(1024)S(1)} %add.168, bf16[1024,4096]{0,1:T(8,128)(2,1)S(1)} %bitcast.166, f32[512,1024]{1,0:T(8,128)S(1)} %get-tuple-element.143, f32[1024]{0:T(1024)S(1)} %bitcast.210, f32[1024]{0:T(1024)S(1)} %bitcast.203, ...), kind=kOutput, calls=%fused_computation.13 | convolution fusion | flops 4436000768 | bytes 31485952 | tf_op jit(solution)/shard_map/td,df->tf/dot_general | solution.py:491
  274.2 4.8 fusion.47
  279.3 2.2 multiply_reduce_fusion.1
  282.4 15.5 %convert_reduce_fusion = (f32[4096]{0:T(1024)S(1)}, bf16[512,4096]{1,0:T(8,128)(2,1)}) fusion(f32[512,4096]{1,0:T(8,128)} %get-tuple-element.110, bf16[1024,4096]{0,1:T(8,128)(2,1)} %bitcast.161, f32[512,1024]{1,0:T(8,128)S(1)} %get-tuple-element.106, f32[512,4096]{1,0:T(8,128)} %get-tuple-element.144, f32[4096]{0:T(1024)S(1)} %add.168), kind=kOutput, calls=%fused_computation.10 | convolution fusion | flops 4331139072 | bytes 31490048 | tf_op jit(solution)/shard_map/td,df->tf/dot_general | solution.py:491
  297.8 9.1 %multiply_reduce_fusion.2 = (f32[1024]{0:T(1024)S(1)}, f32[512]{0:T(512)S(1)}, f32[512]{0:T(512)S(1)}, f32[1024]{0:T(1024)S(1)}, f32[512,1024]{1,0:T(8,128)S(1)}) fusion(f32[512,1024]{1,0:T(8,128)S(1)} %get-tuple-element.143, f32[512]{0:T(512)S(1)} %add_rsqrt_fusion.1, f32[512]{0:T(512)S(1)} %broadcast_multiply_fusion.4, f32[1024]{0:T(1024)S(1)} %bitcast.205, ...), kind=kOutput, calls=%fused_computation.45 | convolution fusion | flops 4300207104 | bytes 18894848 | tf_op jit(solution)/shard_map/tf,df->td/dot_general | solution.py:491
  310.3 1.3 copy.141
  311.7 4.5 convolution_convert_fusion.5
  316.1 4.0 copy.140
  320.1 8.8 %convert_reduce_fusion.3 = (f32[16,64]{1,0:T(8,128)S(1)}, bf16[16,64,512]{2,1,0:T(8,128)(2,1)S(1)}) fusion(bf16[512,16,64]{0,2,1:T(8,128)(2,1)} %bitcast.193, f32[16,512,512]{1,2,0:T(8,128)} %get-tuple-element.141, f32[16,512]{1,0:T(8,128)S(1)} %get-tuple-element.140), kind=kOutput, calls=%fused_computation.48 | convolution fusion | flops 546831360 | bytes 18911232 | tf_op jit(solution)/shard_map/hqk,qhe->khe/dot_general | solution.py:491
  329.0 9.5 %convolution_convert_fusion = bf16[1024,4096]{1,0:T(8,128)(2,1)} fusion(bf16[512,4096]{1,0:T(8,128)(2,1)} %get-tuple-element.155, f32[512,1024]{1,0:T(8,128)S(1)} %get-tuple-element.143, f32[1024]{0:T(1024)S(1)} %bitcast.212, f32[1024]{0:T(1024)S(1)} %bitcast.207, f32[512]{0:T(512)S(1)} %add_rsqrt_fusion.1, f32[512]{0:T(512)S(1)} %broadcast_multiply_fusion.4), kind=kOutput, calls=%fused_computation.32 | convolution fusion | flops 4301783040 | bytes 14692352 | tf_op jit(solution)/shard_map/td,tf->df/dot_general | solution.py:491
  338.5 12.0 %copy.138 = bf16[1024,4096]{0,1:T(8,128)(2,1)} copy(bf16[1024,4096]{1,0:T(8,128)(2,1)} %convolution_convert_fusion) | data formatting | bytes 16777216 | tf_op jit(solution)/shard_map/convert_element_type | solution.py:576
  350.5 11.5 %copy.139 = bf16[1024,2,4,512]{3,0,2,1:T(8,128)(2,1)} copy(bf16[1024,2,4,512]{0,3,2,1:T(8,128)(2,1)} %bitcast.157) | data formatting | bytes 16777216 | tf_op jit(solution)/shard_map/reshape | solution.py:576
  362.0 2.6 convolution_convert_fusion.2
  364.5 4.1 copy.147
  368.6 8.9 %convolution_convert_fusion.1 = bf16[1024,4096]{1,0:T(8,128)(2,1)} fusion(bf16[512,4096]{1,0:T(8,128)(2,1)} %copy-done.36, f32[512,1024]{1,0:T(8,128)S(1)} %copy-done.22), kind=kOutput, calls=%fused_computation.33 | convolution fusion | flops 4299685888 | bytes 14680064 | tf_op jit(solution)/shard_map/td,tf->df/dot_general | solution.py:491
  377.5 12.0 %copy.136 = bf16[1024,4096]{0,1:T(8,128)(2,1)} copy(bf16[1024,4096]{1,0:T(8,128)(2,1)} %convolution_convert_fusion.1) | data formatting | bytes 16777216 | tf_op jit(solution)/shard_map/convert_element_type | solution.py:576
  389.5 11.9 %copy.137 = bf16[1024,2,4,512]{3,0,2,1:T(8,128)(2,1)} copy(bf16[1024,2,4,512]{0,3,2,1:T(8,128)(2,1)} %bitcast.158) | data formatting | bytes 16777216 | tf_op jit(solution)/shard_map/reshape | solution.py:576
  401.4 8.0 %multiply_reduce_fusion = (f32[16,512]{1,0:T(8,128)S(1)}, f32[16,512,512]{1,2,0:T(8,128)S(1)}) fusion(f32[16,512,512]{1,2,0:T(8,128)} %get-tuple-element.141, f32[16,512]{1,0:T(8,128)S(1)} %get-tuple-element.140, bf16[512,16,64]{0,2,1:T(8,128)(2,1)} %bitcast.194, bf16[512,16,64]{0,2,1:T(8,128)(2,1)} %bitcast.191), kind=kOutput, calls=%fused_computation.2 | convolution fusion | flops 549445632 | bytes 35717120 | tf_op jit(solution)/shard_map/qhe,khe->hqk/dot_general | solution.py:491
  409.4 8.1 %multiply_convert_fusion = bf16[16,512,512]{1,2,0:T(8,128)(2,1)S(1)} fusion(f32[16,512,512]{1,2,0:T(8,128)S(1)} %get-tuple-element.149, f32[16,512]{1,0:T(8,128)S(1)} %get-tuple-element.148, f32[16,512,512]{1,2,0:T(8,128)} %get-tuple-element.141, f32[16,512]{1,0:T(8,128)S(1)} %get-tuple-element.140), kind=kLoop, calls=%fused_computation.1 | loop fusion | flops 16777216 | bytes 42008576 | tf_op jit(solution)/shard_map/convert_element_type | solution.py:567
  417.4 3.9 multiply_convert_fusion.2
  421.4 1.5 convert_reduce_fusion.4
  423.4 2.6 fusion.49
  426.0 3.0 fusion.48
  429.1 2.4 add_convert_fusion.1.in_ref
  431.6 38.9 %psum.7 = f32[12288]{0:T(1024)S(1)} all-reduce(f32[12288]{0:T(1024)S(1)} %constant_dynamic-update-slice_fusion.3), channel_id=1, replica_groups=mesh['shard'=4,'ctx'=4,'tp'=2] {'shard','ctx','tp'}, use_global_device_ids=true, to_apply=%region_20.21 | all-reduce | flops 12288 | bytes 98304 | tf_op jit(solution)/shard_map/psum | solution.py:589
  473.4 3.9 convolution_convert_fusion.4
  477.3 2.6 convolution_convert_fusion.3
  479.9 2.9 copy.145
  482.8 3.9 copy.143
  486.7 7.1 %bitcast_dynamic-update-slice_fusion.1 = bf16[2,12,1024,512]{3,2,1,0:T(8,128)(2,1)} fusion(bf16[1024,2,4,512]{3,0,2,1:T(8,128)(2,1)} %copy.137), kind=kLoop, calls=%fused_computation.9 | loop fusion | bytes 16777216
  493.8 7.3 %bitcast_dynamic-update-slice_fusion = bf16[2,12,1024,512]{3,2,1,0:T(8,128)(2,1)} fusion(bf16[2,12,1024,512]{3,2,1,0:T(8,128)(2,1)} %bitcast_dynamic-update-slice_fusion.1, bf16[1024,2,4,512]{3,0,2,1:T(8,128)(2,1)} %copy.139), kind=kLoop, calls=%fused_computation.8 | loop fusion | bytes 16777216
  501.1 1.6 bitcast_dynamic-update-slice_fusion.5
  503.5 1.5 bitcast_dynamic-update-slice_fusion.4
  504.9 1.5 bitcast_dynamic-update-slice_fusion.3
  506.5 1.5 bitcast_dynamic-update-slice_fusion.2.part_ref
  508.0 161.5 %reduce_grads.1 = (bf16[12,256,512]{2,1,0:T(8,128)(2,1)}, bf16[8,128,1024]{2,1,0:T(8,128)(2,1)}, bf16[8,128,1024]{2,1,0:T(8,128)(2,1)}) custom-call(bf16[2,12,1024,512]{3,2,1,0:T(8,128)(2,1)} %bitcast_dynamic-update-slice_fusion.2.part_ref, bf16[512,1024]{1,0:T(8,128)(2,1)} %get-tuple-element.123.out_ref, bf16[512,1024]{1,0:T(8,128)(2,1)} %add_convert_fusion.1.in_ref), custom_call_target="tpu_custom_call" | custom-call | tf_op jit(solution)/shard_map/reduce_grads/pallas_call | solution.py:438
  669.5 4.2 convert_element_type.186
  673.7 2.5 convert_element_type.187
  678.7 2.0 slice_bitcast_fusion.2
  680.7 1.8 copy.149
  683.5 1.9 copy.148
  685.4 1.8 copy.152
  (156 shorter events, 31.0 us)
Async XLA Ops:
  0.7 24.8 %copy-start.26 = (bf16[2048,256]{1,0:T(8,128)(2,1)S(1)}, bf16[2048,256]{1,0:T(8,128)(2,1)}, u32[]{:S(2)}) copy-start(bf16[2048,256]{1,0:T(8,128)(2,1)} %param.25) | copy-start | bytes 3145732
  26.0 4.0 copy-start.18
  30.0 1.7 copy-start.33
  30.0 2.4 copy-start.34
  30.0 3.1 copy-start.35
  183.4 5.4 copy-start.28
  188.8 2.3 copy-start.6
  192.6 31.1 %copy-start.13 = (bf16[512,1024]{0,1:T(8,128)(2,1)}, bf16[512,1024]{0,1:T(8,128)(2,1)S(1)}, u32[]{:S(2)}) copy-start(bf16[512,1024]{0,1:T(8,128)(2,1)S(1)} %copy.130) | copy-start | bytes 3145732
  196.0 4.3 copy-start.8
  205.5 4.3 copy-start.2
  212.0 11.6 %copy-start.17 = (bf16[512,1024]{0,1:T(8,128)(2,1)S(1)}, bf16[512,1024]{0,1:T(8,128)(2,1)}, u32[]{:S(2)}) copy-start(bf16[512,1024]{0,1:T(8,128)(2,1)} %copy.128) | copy-start | bytes 3145732
  223.6 10.3 %copy-start.27 = (bf16[512,1024]{0,1:T(8,128)(2,1)S(1)}, bf16[512,1024]{0,1:T(8,128)(2,1)}, u32[]{:S(2)}) copy-start(bf16[512,1024]{0,1:T(8,128)(2,1)} %copy.125) | copy-start | bytes 3145732
  234.0 7.5 %copy-start.11 = (bf16[1024,2,512]{0,2,1:T(8,128)(2,1)S(1)}, bf16[1024,2,512]{0,2,1:T(8,128)(2,1)}, u32[]{:S(2)}) copy-start(bf16[1024,2,512]{0,2,1:T(8,128)(2,1)} %copy.132) | copy-start | bytes 6291460
  234.0 7.5 %copy-start.29 = (bf16[512,1024]{1,0:T(8,128)(2,1)S(1)}, bf16[512,1024]{1,0:T(8,128)(2,1)}, u32[]{:S(2)}) copy-start(bf16[512,1024]{1,0:T(8,128)(2,1)} %get-tuple-element.24) | copy-start | bytes 3145732
  234.0 9.5 %copy-start.5 = (bf16[1024,2,4,512]{0,3,2,1:T(8,128)(2,1)S(1)}, bf16[1024,2,4,512]{0,3,2,1:T(8,128)(2,1)}, u32[]{:S(2)}) copy-start(bf16[1024,2,4,512]{0,3,2,1:T(8,128)(2,1)} %copy.133) | copy-start | bytes 25165828
  241.5 1.8 copy-start.32
  241.5 32.7 %slice-start = ((s8[8388608]{0:T(1024)(128)(4,1)}), s8[4194304]{0:T(1024)(128)(4,1)S(1)}, s32[]{:S(2)}) async-start(s8[8388608]{0:T(1024)(128)(4,1)} %bitcast.162), calls=%async_computation | async-start | bytes 8388608
  243.4 30.7 %slice-start.1 = ((s8[8388608]{0:T(1024)(128)(4,1)}), s8[4194304]{0:T(1024)(128)(4,1)S(1)}, s32[]{:S(2)}) async-start(s8[8388608]{0:T(1024)(128)(4,1)} %bitcast.162), calls=%async_computation.1 | async-start | bytes 8388608
  274.1 4.8 copy-start.36
  274.2 5.1 copy-start.19
  282.4 15.5 %copy-start.21 = (f32[512,1024]{1,0:T(8,128)}, f32[512,1024]{1,0:T(8,128)S(1)}, u32[]{:S(2)}) copy-start(f32[512,1024]{1,0:T(8,128)S(1)} %get-tuple-element.106) | copy-start | bytes 6291460
  307.7 1.3 copy-start
  328.9 33.0 %copy-start.24 = (bf16[16,64,512]{2,1,0:T(8,128)(2,1)}, bf16[16,64,512]{2,1,0:T(8,128)(2,1)S(1)}, u32[]{:S(2)}) copy-start(bf16[16,64,512]{2,1,0:T(8,128)(2,1)S(1)} %get-tuple-element.153) | copy-start | bytes 3145732
  350.5 11.5 %copy-start.30 = (bf16[512,1024]{1,0:T(8,128)(2,1)S(1)}, bf16[512,1024]{1,0:T(8,128)(2,1)}, u32[]{:S(2)}) copy-start(bf16[512,1024]{1,0:T(8,128)(2,1)} %get-tuple-element.24) | copy-start | bytes 3145732
  364.5 4.1 copy-start.22
  417.4 4.0 copy-start.14
  421.4 1.5 copy-start.15
  421.4 2.0 copy-start.7
  423.4 5.7 copy-start.1
  426.0 3.0 copy-start.3
  426.0 3.0 copy-start.4
  426.0 3.1 copy-start.25
  473.4 4.0 copy-start.16
  473.4 4.0 copy-start.31
  493.8 7.3 %copy-start.9 = (bf16[1024,2,1,512]{3,0,2,1:T(8,128)(2,1)S(1)}, bf16[1024,2,1,512]{3,0,2,1:T(8,128)(2,1)}, u32[]{:S(2)}) copy-start(bf16[1024,2,1,512]{3,0,2,1:T(8,128)(2,1)} %copy.140) | copy-start | bytes 6291460
  501.1 2.3 copy-start.12
  503.4 3.1 copy-start.10
  669.4 4.2 copy-start.23
  673.7 3.0 copy-start.20

commit v2 on v1

v2 whole, which is shorter than its diff:
```python
import functools

import jax
import jax.numpy as jnp
from jax import lax
from jax.experimental import pallas as pl
from jax.experimental.pallas import tpu as pltpu
from jax.sharding import PartitionSpec as P

HD = 64
UNIT = 512
SUB = 256
EPSILON = 1e-05
MASKED = -1e30
MESH = pl.DeviceIdType.MESH
F32 = jnp.float32
BF16 = jnp.bfloat16
DMA = pltpu.SemaphoreType.DMA
ANY = pl.BlockSpec(memory_space=pl.ANY)
VMEM = pl.BlockSpec(memory_space=pltpu.VMEM)
SMEM = pl.BlockSpec(memory_space=pltpu.SMEM)


def place():
    return lax.axis_index("shard"), lax.axis_index("ctx"), lax.axis_index("tp")


def rcopy(src, dst, send, recv, dev):
    return pltpu.make_async_remote_copy(
        src_ref=src, dst_ref=dst, send_sem=send, recv_sem=recv, device_id=dev, device_id_type=MESH
    )


def lcopy(src, dst, sem):
    return pltpu.make_async_copy(src, dst, sem)


def greet(devices):
    barrier = pltpu.get_barrier_semaphore()
    for dev in devices:
        pl.semaphore_signal(barrier, inc=1, device_id=dev, device_id_type=MESH)
    pl.semaphore_wait(barrier, len(devices))


def rows_at(i, size):
    return pl.ds(pl.multiple_of(i * size, size), size)


def mm(a, b):
    return jnp.dot(a, b, preferred_element_type=F32)


def mm_nt(a, b):
    return lax.dot_general(a, b, (((1,), (1,)), ((), ())), preferred_element_type=F32)


def mm_tn(a, b):
    return lax.dot_general(a, b, (((0,), (0,)), ((), ())), preferred_element_type=F32)


def loop(count, fn):
    def step(i, carry):
        fn(i)
        return carry

    lax.fori_loop(0, count, step, 0)


def mean(v):
    return jnp.mean(v, -1, keepdims=True)


def forward_kernel(
    n, nz,
    len_ref, x_ref, g_ref, wq_ref, wk_ref, wv_ref, wo_ref, we_ref, wr_ref, pk_ref,
    full_ref, x_out, q_out, k_out, v_out, o_out, lse_out, n1_out, r1_out, u_out, h_out, gp_out,
    ds_out, dz_out, y_out, vec_out, small_out,
    own, wo_in, wr_in, xin, act_low, xv, cotv, qkv, o_v, lse_v, n1_v, r1_v, u_v, ulow_v, h_v, gp_v, acc,
    dz_v, y_v, wbuf, pkall, bias, vec, small,
    own_send, own_recv, fwd_send, fwd_recv, core_send, core_recv, act_send, act_recv,
    pk_send, pk_recv, in_sem, act_sem, fetch_sem, out_sem,
):
    s, z, c = place()
    units, rows, width = own.shape
    half = rows // 2
    model = rows * n
    slots = xv.shape[0]
    block = slots // nz
    e_units = we_ref.shape[1] // width
    group = [(s ^ k, z, c if j == 0 else 1 - c) for k in range(n) for j in range(2) if k + j > 0]
    greet(group + [(s, lax.rem(z + k, nz), c) for k in range(1, nz)])
    mine = rows_at(s, rows)
    zrows = rows_at(z, block)

    ins = [lcopy(r, own.at[i], in_sem.at[i]) for i, r in enumerate((wq_ref, wk_ref, wv_ref))]
    ins += [
        lcopy(we_ref.at[:, pl.ds(j * width, width)], own.at[4 + j], in_sem.at[3 + j]) for j in range(e_units)
    ]
    ins_o = lcopy(wo_ref, wo_in, in_sem.at[3 + e_units])
    ins_r = lcopy(wr_ref, wr_in, in_sem.at[4 + e_units])

    def to(k):
        return lax.rem(z + k, nz)

    def act_load(which, k):
        src = (x_ref, g_ref)[which]
        return lcopy(src.at[2 * to(k) + c], xin.at[k], act_sem.at[k])

    def act(which, k):
        dst = (xv, cotv)[which]
        return rcopy(
            act_low.at[which, k], dst.at[zrows, :], act_send.at[which, k], act_recv.at[which, k], (s, to(k), c)
        )

    def act_in(which, k):
        dst = (xv, cotv)[which]
        src = lax.rem(z + nz - k, nz)
        at = dst.at[rows_at(src, block), :]
        return rcopy(at, at, act_send.at[which, k], act_recv.at[which, k], (s, src, c))

    def act_share(which):
        for k in range(1, nz):
            act_load(which, k).wait()
            act_low[which, k] = xin[k].astype(BF16)
            act(which, k).start()
        act_load(which, 0).wait()
        (xv, cotv)[which][zrows, :] = xin[0].astype(BF16)

    for k in range(1, nz):
        act_load(0, k).start()
    for i in ins:
        i.start()
    act_load(0, 0).start()
    ins_o.start()
    ins_r.start()

    def pk_copy(k, j):
        return rcopy(
            pk_ref, pkall.at[s, c], pk_send.at[k, j], pk_recv.at[k, j], (s ^ k, z, c if j == 0 else 1 - c)
        )

    def pk_in(k, j):
        at = pkall.at[s ^ k, c if j == 0 else 1 - c]
        return rcopy(at, at, pk_send.at[k, j], pk_recv.at[k, j], (s ^ k, z, c if j == 0 else 1 - c))

    pk_pairs = [(k, j) for k in range(n) for j in range(2) if k + j > 0]
    for k, j in pk_pairs:
        pk_copy(k, j).start()
    pkall[s, c] = pk_ref[...]

    direct = [1, 2] if n == 4 else list(range(1, n))

    def own_copy(u, k):
        return rcopy(
            own.at[u], full_ref.at[c, u, mine, :], own_send.at[u, k], own_recv.at[u, k], (s ^ k, z, c)
        )

    def own_in(u, k):
        at = full_ref.at[c, u, rows_at(s ^ k, rows), :]
        return rcopy(at, at, own_send.at[u, k], own_recv.at[u, k], (s ^ k, z, c))

    def half_at(k, h):
        return pl.ds(pl.multiple_of((s ^ k) * rows + h * half, half), half)

    def fwd_copy(u, h):
        at = full_ref.at[c, u, half_at(2 - h, h), :]
        return rcopy(at, at, fwd_send.at[u, h], fwd_recv.at[u, h], (s ^ (1 + h), z, c))

    def fwd_in(u, h):
        at = full_ref.at[c, u, half_at(3, h), :]
        return rcopy(at, at, fwd_send.at[u, h], fwd_recv.at[u, h], (s ^ (1 + h), z, c))

    def core_copy(u, k):
        at = full_ref.at[c, u, rows_at(s ^ k, rows), :]
        return rcopy(at, at, core_send.at[u, k], core_recv.at[u, k], (s, z, 1 - c))

    def core_in(u, k):
        at = full_ref.at[1 - c, u, rows_at(s ^ k, rows), :]
        return rcopy(at, at, core_send.at[u, k], core_recv.at[u, k], (s, z, 1 - c))

    ahead = 2
    for i in ins[:ahead]:
        i.wait()
    for u in range(ahead):
        for k in direct:
            own_copy(u, k).start()
    act_share(0)
    for k in range(nz):
        act_load(1, k).start()
    for i in ins[ahead:]:
        i.wait()
    ins_o.wait()
    own[3] = wo_in[...].T
    ins_r.wait()

    def turn(j):
        own[4 + e_units + j] = wr_in[rows_at(j, width), :].T

    loop(e_units, turn)
    keep = lcopy(own, full_ref.at[c, :, mine, :], in_sem.at[5 + e_units])
    keep.start()
    share = rcopy(
        own, full_ref.at[c, :, mine, :], core_send.at[units, 0], core_recv.at[units, 0], (s, z, 1 - c)
    )
    share.start()
    theirs = full_ref.at[1 - c, :, mine, :]
    share_in = rcopy(theirs, theirs, core_send.at[units, 0], core_recv.at[units, 0], (s, z, 1 - c))
    act_share(1)

    for k, j in pk_pairs:
        pk_in(k, j).wait_recv()
    wide = pk_ref.shape[1]
    he = HD // n
    bias[...] = jnp.zeros_like(bias)
    vec[...] = jnp.zeros_like(vec)

    def place_one(sh):
        r = lax.broadcasted_iota(jnp.int32, (wide, width), 0)
        col = lax.broadcasted_iota(jnp.int32, (wide, width), 1)
        hit = jnp.logical_and(r < width // n, col == (r // he) * HD + sh * he + r % he)
        pick = jnp.where(hit, 1.0, 0.0).astype(BF16)
        for j in range(2):
            bias[j] += mm(pkall[sh, j], pick)
        r = lax.broadcasted_iota(jnp.int32, (wide, model), 0)
        col = lax.broadcasted_iota(jnp.int32, (wide, model), 1)
        hit = jnp.logical_and(r < rows, col == sh * rows + r)
        vec[...] += mm(pkall[sh, 0], jnp.where(hit, 1.0, 0.0).astype(BF16))

    loop(n, place_one)
    small[...] = jnp.zeros_like(small)
    vec_copy = lcopy(vec, vec_out, out_sem.at[0])
    vec_copy.start()
    length = len_ref[2 * z + c]
    live_keys = lax.broadcasted_iota(jnp.int32, (1, slots), 1) < length
    lane = lax.broadcasted_iota(jnp.int32, (slots, 128), 1)
    outs = []

    def fetch(u):
        return lcopy(full_ref.at[:, u], wbuf.at[lax.rem(u, 2)], fetch_sem.at[lax.rem(u, 2)])

    def ready(u):
        @pl.when(u == 0)
        def _():
            keep.wait()
            share_in.wait_recv()

        for k in range(1, n):
            core_in(u, k).wait_recv()

    def attention(p):
        hf, at = p // 4, rows_at(lax.rem(p, 4), 128)
        q, k, v = qkv[0, hf, :, at], qkv[1, hf, :, at], qkv[2, hf, :, at]
        out = None
        for h in range(2):
            part = lane < HD if h == 0 else lane >= HD
            scores = mm_nt(jnp.where(part, q, 0), k) * HD ** (-0.5)
            scores = jnp.where(live_keys, scores, MASKED)
            peak = jnp.max(scores, -1, keepdims=True)
            e = jnp.exp(scores - peak)
            total = jnp.sum(e, -1, keepdims=True)
            term = mm((e * (1.0 / total)).astype(BF16), jnp.where(part, v, 0))
            out = term if out is None else out + term
            lse_v[...] = jnp.where(lane == 2 * p + h, peak + jnp.log(total), lse_v[...])
        o_v[hf, :, at] = out.astype(BF16)

    lse_v[...] = jnp.zeros_like(lse_v)
    rb = 128

    def compute(u):
        w = wbuf.at[lax.rem(u, 2)]

        @pl.when(u == 0)
        def _():
            for k in range(1, nz):
                act_in(0, k).wait_recv()

        @pl.when(u < 3)
        def _():
            def one(hf):
                add = jnp.where(u == 0, bias[hf, 0:1, :], jnp.where(u == 2, bias[hf, 1:2, :], 0.0))
                qkv[u, hf] = (mm(xv[...], w[hf]) + add).astype(BF16)

            loop(2, one)

        @pl.when(u == 2)
        def _():
            loop(4, attention)

        @pl.when(u == 3)
        def _():
            loop(4, lambda p: attention(p + 4))
            acc[...] = mm_nt(o_v[0], w[0]) + xv[...].astype(F32)
            acc[...] += mm_nt(o_v[1], w[1])

            def norm(i):
                at = rows_at(i, rb)
                first = acc[at, :] + vec[8:9, :]
                centred = first - mean(first)
                inv = lax.rsqrt(mean(centred * centred) + EPSILON)
                n1 = centred * inv
                n1_v[at, :] = n1
                r1_v[at, :] = jnp.broadcast_to(inv, (rb, 128))
                up = n1 * vec[10:11, :] + vec[11:12, :]
                ulow_v[at, :] = up.astype(BF16)
                u_v[at, :] = up

            loop(slots // rb, norm)
            for i, (src, dst) in enumerate(
                ((qkv.at[0], q_out), (qkv.at[1], k_out), (qkv.at[2], v_out), (o_v, o_out), (lse_v, lse_out),
                 (n1_v, n1_out), (r1_v, r1_out), (ulow_v, u_out), (xv, x_out))
            ):
                lcopy(src, dst, out_sem.at[1 + i]).start()

        @pl.when(jnp.logical_and(u >= 4, u < 4 + e_units))
        def _():
            j = u - 4

            def one(hf):
                pre = mm(ulow_v[...], w[hf]) + bias[hf, pl.ds(2 + j, 1), :]
                phi = 0.5 * (1.0 + lax.erf(pre * 0.7071067811865476))
                h_v[j, hf] = (pre * phi).astype(BF16)
                gp_v[j, hf] = (phi + pre * jnp.exp(-0.5 * pre * pre) * 0.3989422804014327).astype(BF16)

            loop(2, one)
            lcopy(h_v.at[j], h_out.at[j], out_sem.at[10]).start()
            lcopy(gp_v.at[j], gp_out.at[j], out_sem.at[11]).start()
            lcopy(h_v.at[j], h_out.at[j], out_sem.at[10]).wait()
            lcopy(gp_v.at[j], gp_out.at[j], out_sem.at[11]).wait()

        @pl.when(u >= 4 + e_units)
        def _():
            j = u - 4 - e_units
            u_v[...] += mm_nt(h_v[j, 0], w[0])
            u_v[...] += mm_nt(h_v[j, 1], w[1])

    def step(u):
        @pl.when(u < units)
        def _():
            @pl.when(u + ahead < units)
            def _():
                for k in direct:
                    own_copy(u + ahead, k).start()

            for k in direct:
                own_in(u, k).wait_recv()
                if n == 4:
                    fwd_copy(u, 2 - k).start()
                core_copy(u, k).start()

        if n == 4:
            @pl.when(jnp.logical_and(u > 0, u <= units))
            def _():
                for h in range(2):
                    fwd_in(u - 1, h).wait_recv()
                core_copy(u - 1, 3).start()

        @pl.when(u >= 2)
        def _():
            fetch(u - 2).wait()
            compute(u - 2)

        @pl.when(jnp.logical_and(u > 0, u <= units))
        def _():
            ready(u - 1)
            fetch(u - 1).start()

    loop(units + 2, step)

    for k in range(1, nz):
        act_in(1, k).wait_recv()

    def norm2(i):
        at = rows_at(i, rb)
        second = u_v[at, :] + vec[9:10, :]
        centred = second - mean(second)
        inv = lax.rsqrt(mean(centred * centred) + EPSILON)
        n2 = centred * inv
        gain = vec[12:13, :]
        y_v[at, :] = (n2 * gain + vec[13:14, :]).astype(BF16)
        row = lax.broadcasted_iota(jnp.int32, (rb, 1), 0) + i * rb
        grad = jnp.where(row < length, cotv[at, :].astype(F32), 0.0)
        scaled = grad * gain
        back = inv * (scaled - mean(scaled) - n2 * mean(scaled * n2))
        acc[at, :] = back
        low = back.astype(BF16)
        dz_v[at, :] = low
        for r, v in ((14, low.astype(F32)), (20, grad * n2), (22, grad)):
            v = jnp.sum(v, 0, keepdims=True)
            small[r : r + 1, :] += v[:, :width]
            small[r + 1 : r + 2, :] += v[:, width:]

    loop(slots // rb, norm2)
    last = [
        lcopy(src, dst, out_sem.at[12 + i])
        for i, (src, dst) in enumerate(((acc, ds_out), (dz_v, dz_out), (y_v, y_out), (small, small_out)))
    ]
    for i in last:
        i.start()

    def finish(u):
        for k in direct:
            own_copy(u, k).wait_send()
        if n == 4:
            for h in range(2):
                fwd_copy(u, h).wait_send()
        for k in range(1, n):
            core_copy(u, k).wait_send()

    loop(units, finish)
    share.wait_send()
    for k, j in pk_pairs:
        pk_copy(k, j).wait_send()
    for which in range(2):
        for k in range(1, nz):
            act(which, k).wait_send()
    vec_copy.wait()
    for i, (src, dst) in enumerate(
        ((qkv.at[0], q_out), (qkv.at[1], k_out), (qkv.at[2], v_out), (o_v, o_out), (lse_v, lse_out),
         (n1_v, n1_out), (r1_v, r1_out), (ulow_v, u_out), (xv, x_out))
    ):
        lcopy(src, dst, out_sem.at[1 + i]).wait()
    for i in last:
        i.wait()


def forward(n, nz, lengths, inputs, cotangent, wq, wk, wv, wo, we, wr, pk):
    seqs, block, model = inputs.shape
    rows = wq.shape[0]
    e_units = we.shape[1] // UNIT
    units = 4 + 2 * e_units
    slots = nz * block
    by_half = (2, slots, UNIT)
    outs = [
        ((2, units, model, UNIT), BF16), ((slots, model), BF16),
        (by_half, BF16), (by_half, BF16), (by_half, BF16), (by_half, BF16), ((slots, 128), F32),
        ((slots, model), F32), ((slots, 128), F32), ((slots, model), BF16),
        ((e_units, *by_half), BF16), ((e_units, *by_half), BF16),
        ((slots, model), F32), ((slots, model), BF16), ((slots, model), BF16), ((16, model), F32),
        ((24, UNIT), F32),
    ]
    scratch = [
        ((units, rows, UNIT), BF16), (wo.shape, BF16), (wr.shape, BF16), ((nz, block, model), F32),
        ((2, nz, block, model), BF16), ((slots, model), BF16), ((slots, model), BF16), ((3, *by_half), BF16),
        (by_half, BF16), ((slots, 128), F32), ((slots, model), F32), ((slots, 128), F32), ((slots, model), F32),
        ((slots, model), BF16), ((e_units, *by_half), BF16), ((e_units, *by_half), BF16), ((slots, model), F32),
        ((slots, model), BF16), ((slots, model), BF16), ((2, 2, model, UNIT), BF16), ((n, 2, *pk.shape), BF16),
        ((2, 16, UNIT), F32), ((16, model), F32), ((24, UNIT), F32),
    ]
    return pl.pallas_call(
        functools.partial(forward_kernel, n, nz),
        name="gather_and_forward",
        out_shape=[jax.ShapeDtypeStruct(a, b) for a, b in outs],
        in_specs=[SMEM] + [ANY] * 8 + [VMEM],
        out_specs=[ANY] * len(outs),
        scratch_shapes=[pltpu.VMEM(a, b) for a, b in scratch]
        + [
            DMA((units, n)), DMA((units, n)), DMA((units, 2)), DMA((units, 2)),
            DMA((units + 1, n)), DMA((units + 1, n)), DMA((2, nz)), DMA((2, nz)),
            DMA((n, 2)), DMA((n, 2)), DMA((6 + e_units,)), DMA((nz,)), DMA((2,)), DMA((16,)),
        ],
        compiler_params=pltpu.CompilerParams(
            collective_id=0, has_side_effects=True, vmem_limit_bytes=60 * 2**20
        ),
    )(lengths, inputs, cotangent, wq, wk, wv, wo, we, wr, pk)


def backward_kernel(
    n, nz,
    len_ref, full_ref, x_ref, q_ref, k_ref, v_ref, o_ref, lse_ref, n1_ref, r1_ref, u_ref, h_ref, gp_ref,
    ds_ref, dz_ref, y_ref, vec_ref, small_ref,
    grad_ref, ys_ref, dx_ref, small_out, part_ref, got_ref,
    x_v, qkv, o_v, lse_v, n1_v, r1_v, u_v, dz_v, du, do_v, dqkv, wr_v, we_v, h_v, gp_v, dpre, pbuf, small, round_in,
    stage, gstage, total, near, pair_sum, far, up, across, down, block_out, dx_low,
    load_sem, w_sem, part_sem, core_send, core_recv, stage_sem, near_send, near_recv, far_send, far_recv,
    z_send, z_recv, store_sem, act_send, act_recv, pass_send, pass_recv, keep_sem, small_send, small_recv,
):
    s, z, c = place()
    units = part_ref.shape[0]
    subs = 2 * units
    e_units = h_ref.shape[0]
    model = total.shape[1]
    rows = model // n
    half = rows // 2
    slots = x_v.shape[0]
    block = slots // nz
    greet(
        [(s ^ k, z, c) for k in range(1, n)]
        + [(s, z, 1 - c)]
        + [(s, lax.rem(z + k, nz), c) for k in range(1, nz)]
    )
    zrows = rows_at(z, block)
    mates = [(dz_ref, dz_v), (ds_ref, du), (small_ref, small), (u_ref, u_v), (r1_ref, r1_v), (n1_ref, n1_v),
             (o_ref, o_v), (lse_ref, lse_v), (q_ref, qkv.at[0]), (k_ref, qkv.at[1]), (v_ref, qkv.at[2]), (x_ref, x_v)]
    loads = [lcopy(a, b, load_sem.at[i]) for i, (a, b) in enumerate(mates)]

    def load_r(j):
        return [
            lcopy(full_ref.at[:, 4 + e_units + j], wr_v, w_sem.at[0]),
            lcopy(h_ref.at[j], h_v, w_sem.at[1]),
            lcopy(gp_ref.at[j], gp_v, w_sem.at[2]),
        ]

    def load_e(j):
        return lcopy(full_ref.at[:, 4 + j], we_v, w_sem.at[3])

    def load_into(u, buf, i):
        return lcopy(full_ref.at[:, u], buf, w_sem.at[i])

    for i in load_r(0):
        i.start()
    for i in loads:
        i.start()

    def act(which, k):
        src, dst = ((y_ref, ys_ref), (dx_low, dx_ref))[which]
        to = lax.rem(z + k, nz)
        return rcopy(
            src.at[rows_at(to, block), :], dst.at[2 * z + c], act_send.at[which, k], act_recv.at[which, k], (s, to, c)
        )

    def act_in(which, k):
        src = lax.rem(z + nz - k, nz)
        at = (ys_ref, dx_ref)[which].at[2 * src + c]
        return rcopy(at, at, act_send.at[which, k], act_recv.at[which, k], (s, src, c))

    def act_keep(which):
        src, dst = ((y_ref, ys_ref), (dx_low, dx_ref))[which]
        return lcopy(src.at[zrows, :], dst.at[2 * z + c], keep_sem.at[which])

    def pass_copy(which, k):
        at = (ys_ref, dx_ref)[which].at[2 * lax.rem(z + nz - k, nz) + c]
        return rcopy(at, at, pass_send.at[which, k], pass_recv.at[which, k], (s, z, 1 - c))

    def pass_in(which, k):
        at = (ys_ref, dx_ref)[which].at[2 * lax.rem(z + nz - k, nz) + 1 - c]
        return rcopy(at, at, pass_send.at[which, k], pass_recv.at[which, k], (s, z, 1 - c))

    def act_start(which):
        for k in range(1, nz):
            act(which, k).start()
        act_keep(which).start()

    def act_pass(which):
        for k in range(1, nz):
            act_in(which, k).wait_recv()
            pass_copy(which, k).start()
        act_keep(which).wait()
        pass_copy(which, 0).start()

    act_start(0)

    def core_copy(u):
        return rcopy(pbuf.at[0], got_ref.at[u], core_send.at[u], core_recv.at[u], (s, z, 1 - c))

    def core_in(u):
        return rcopy(got_ref.at[u], got_ref.at[u], core_send.at[u], core_recv.at[u], (s, z, 1 - c))

    def part_copy(u):
        return lcopy(pbuf.at[1], part_ref.at[u], part_sem.at[0])

    def free_part(u):
        @pl.when(u > 0)
        def _():
            core_copy(u - 1).wait_send()

    def emit(u, i, value):
        low = value.astype(BF16)
        for b in range(2):
            pbuf[i, b] = low[:, b * SUB : (b + 1) * SUB]

    def produce(u, make):
        free_part(u)

        def one(i):
            emit(u, i, make(lax.rem(1 - c + i, 2)))

            @pl.when(i == 0)
            def _():
                core_copy(u).start()

        loop(2, one)
        part_copy(u).start()
        part_copy(u).wait()

    length = len_ref[2 * z + c]
    live_keys = lax.broadcasted_iota(jnp.int32, (1, slots), 1) < length
    lane = lax.broadcasted_iota(jnp.int32, (slots, 128), 1)
    rb = 128

    def add_small(r, v):
        small[pl.ds(r, 1), :] += v

    def tick_r(j):
        load_e(j).start()
        for i in load_r(j):
            i.wait()

        def one(hf):
            low = (mm(dz_v[...], wr_v[hf]) * gp_v[hf].astype(F32)).astype(BF16)
            dpre[hf] = low
            add_small(4 + hf * e_units + j, jnp.sum(low.astype(F32), 0, keepdims=True))

        loop(2, one)
        produce(2 * j, lambda hf: mm_tn(dz_v[...], h_v[hf]))

    def tick_e(j):
        load_e(j).wait()

        @pl.when(j + 1 < e_units)
        def _():
            for i in load_r(j + 1):
                i.start()

        @pl.when(j + 1 == e_units)
        def _():
            load_into(3, wr_v, 0).start()

        produce(2 * j + 1, lambda hf: mm_tn(u_v[...], dpre[hf]))

        def one(hf):
            du[...] += mm_nt(dpre[hf], we_v[hf])

        loop(2, one)

    def tick_o():
        load_into(1, we_v, 3).start()

        def norm(i):
            at = rows_at(i, rb)
            grad = du[at, :]
            n1 = n1_v[at, :]
            scaled = grad * vec_ref[10:11, :]
            back = r1_v[at, 0:1] * (scaled - mean(scaled) - n1 * mean(scaled * n1))
            du[at, :] = back
            low = back.astype(BF16)
            dz_v[at, :] = low
            for r, v in ((12, low.astype(F32)), (16, grad * n1), (18, grad)):
                v = jnp.sum(v, 0, keepdims=True)
                small[r : r + 1, :] += v[:, :UNIT]
                small[r + 1 : r + 2, :] += v[:, UNIT:]

        loop(slots // rb, norm)
        load_into(3, wr_v, 0).wait()
        produce(2 * e_units, lambda hf: mm_tn(dz_v[...], o_v[hf]))

        def one(hf):
            do_v[hf] = mm(dz_v[...], wr_v[hf]).astype(BF16)

        loop(2, one)
        load_into(0, wr_v, 0).start()

    def attention(p):
        hf, at = p // 4, rows_at(lax.rem(p, 4), 128)
        q, k, v = qkv[0, hf, :, at], qkv[1, hf, :, at], qkv[2, hf, :, at]
        do = do_v[hf, :, at]
        dq = dk = dv = None
        for h in range(2):
            part = lane < HD if h == 0 else lane >= HD
            qh, kh, doh = jnp.where(part, q, 0), jnp.where(part, k, 0), jnp.where(part, do, 0)
            scores = mm_nt(qh, k) * HD ** (-0.5)
            scores = jnp.where(live_keys, scores, MASKED)
            lse = jnp.sum(jnp.where(lane == 2 * p + h, lse_v[...], 0.0), -1, keepdims=True)
            probs = jnp.exp(scores - lse)
            dp = mm_nt(doh, v)
            low = (probs * (dp - jnp.sum(dp * probs, -1, keepdims=True))).astype(BF16)
            tv, tk, tq = mm_tn(probs.astype(BF16), doh), mm_tn(low, qh), mm(low, kh)
            dv, dk, dq = (tv, tk, tq) if h == 0 else (dv + tv, dk + tk, dq + tq)
        dqkv[0, hf, :, at] = (dq * HD ** (-0.5)).astype(BF16)
        dqkv[1, hf, :, at] = (dk * HD ** (-0.5)).astype(BF16)
        dqkv[2, hf, :, at] = dv.astype(BF16)

    def tick_qkv(i, buf, sem, u):
        load_into(u, buf, sem).wait()
        produce(2 * e_units + 1 + u, lambda hf: mm_tn(x_v[...], dqkv[u, hf]))

        def one(hf):
            du[...] += mm_nt(dqkv[u, hf], buf[hf])
            if u != 1:
                add_small(u + hf, jnp.sum(dqkv[u, hf].astype(F32), 0, keepdims=True))

        loop(2, one)

    def compute(t):
        ffn = 2 * e_units

        @pl.when(jnp.logical_and(t < ffn, lax.rem(t, 2) == 0))
        def _():
            tick_r(t // 2)

        @pl.when(jnp.logical_and(t < ffn, lax.rem(t, 2) == 1))
        def _():
            tick_e(t // 2)

        pl.when(t == ffn)(tick_o)

        @pl.when(jnp.logical_and(t > ffn, t <= ffn + 4))
        def _():
            loop(2, lambda i: attention(2 * (t - ffn - 1) + i))

        @pl.when(t == ffn + 5)
        def _():
            tick_qkv(0, wr_v, 0, 0)
            load_into(2, wr_v, 0).start()

        @pl.when(t == ffn + 6)
        def _():
            tick_qkv(1, we_v, 3, 1)

        @pl.when(t == ffn + 7)
        def _():
            tick_qkv(2, wr_v, 0, 2)
            dx_low[...] = du[...].astype(BF16)
            act_start(1)

    def loads_of(w):
        slot = lax.rem(w, 2)
        u, b = w // 2, lax.rem(w, 2)
        return [
            lcopy(part_ref.at[u, b], stage.at[slot], stage_sem.at[slot, 0]),
            lcopy(got_ref.at[u, b], gstage.at[slot], stage_sem.at[slot, 1]),
        ]

    def blk(k):
        return rows_at(s ^ k, rows)

    def blk_half(k, h):
        return pl.ds(pl.multiple_of((s ^ k) * rows + h * half, half), half)

    def near_copy(w, h, i):
        k = (1 + h, 3)[i]
        return rcopy(
            total.at[lax.rem(w, 2), blk_half(k, h), :], near.at[w, h, i],
            near_send.at[w, h, i], near_recv.at[w, h, i], (s ^ (1 + h), z, c),
        )

    def far_copy(w, h):
        return rcopy(
            pair_sum.at[w, h], far.at[w, h], far_send.at[w, h], far_recv.at[w, h], (s ^ (2 - h), z, c)
        )

    def straight(w, k):
        return rcopy(
            total.at[lax.rem(w, 2), blk(k), :], near.at[w, k - 1],
            near_send.at[w, k - 1], near_recv.at[w, k - 1], (s ^ k, z, c),
        )

    def sends_of(w):
        if n == 4:
            return [near_copy(w, h, i) for h in range(2) for i in range(2)]
        return [straight(w, k) for k in range(1, n)]

    def z_to(w, src, dst, i, to):
        return rcopy(src.at[w], dst.at[w], z_send.at[w, i], z_recv.at[w, i], (s, to, c))

    last = nz - 1
    edge = jnp.logical_or(z == 0, z == last)
    inner = jnp.where(z == 0, 1, nz - 2)
    outer = jnp.where(z == 1, 0, last)
    other = jnp.where(z == 1, 2, 1)

    def s0(w):
        @pl.when(lax.rem(w, 2) == 0)
        def _():
            core_in(w // 2).wait_recv()

        for i in loads_of(w):
            i.start()

    def s1(w):
        @pl.when(w >= 2)
        def _():
            for i in sends_of(w - 2):
                i.wait_send()

        for i in loads_of(w):
            i.wait()
        slot = lax.rem(w, 2)

        def add(i):
            at = rows_at(i, 256)
            total[slot, at, :] = (stage[slot, at, :].astype(F32) + gstage[slot, at, :].astype(F32)).astype(BF16)

        loop(model // 256, add)
        for i in sends_of(w):
            i.start()

    def s2(w):
        slot = lax.rem(w, 2)
        for i in sends_of(w):
            i.wait_recv()
        if n == 4:
            for h in range(2):
                pair_sum[w, h] = (
                    total[slot, blk_half(2 - h, h), :].astype(F32) + near[w, h, 1].astype(F32)
                ).astype(BF16)
                far_copy(w, h).start()

    def s3(w):
        slot = lax.rem(w, 2)
        if n == 4:
            for h in range(2):
                far_copy(w, h).wait_recv()
                block_out[w, h * half : (h + 1) * half] = (
                    total[slot, blk_half(0, h), :].astype(F32) + near[w, h, 0].astype(F32) + far[w, h].astype(F32)
                ).astype(BF16)
        else:
            acc = total[slot, blk(0), :].astype(F32)
            for k in range(1, n):
                acc = acc + near[w, k - 1].astype(F32)
            block_out[w] = acc.astype(BF16)

        @pl.when(edge)
        def _():
            z_to(w, block_out, up, 0, inner).start()

    def s4(w):
        @pl.when(jnp.logical_not(edge))
        def _():
            z_to(w, block_out, up, 0, outer).wait_recv()
            block_out[w] = (block_out[w].astype(F32) + up[w].astype(F32)).astype(BF16)
            z_to(w, block_out, across, 1, other).start()

    def s5(w):
        @pl.when(jnp.logical_not(edge))
        def _():
            z_to(w, block_out, across, 1, other).wait_recv()
            down[w] = (block_out[w].astype(F32) + across[w].astype(F32)).astype(BF16)
            z_to(w, down, down, 2, outer).start()

    def s6(w):
        @pl.when(edge)
        def _():
            z_to(w, down, down, 2, inner).wait_recv()

        lcopy(down.at[w], grad_ref.at[w], store_sem.at[w]).start()

    stages = [s0, s1, s2, s3, s4, s5, s6]

    hops = [(s, z, 1 - c)]
    hops += [(s ^ (1 << b), z, c) for b in range(n.bit_length() - 1)]
    hops += [(s, z ^ (1 << b), c) for b in range(nz.bit_length() - 1)]

    def small_copy(i):
        return rcopy(small, round_in.at[i], small_send.at[i], small_recv.at[i], hops[i])

    for i in loads:
        i.wait()
    done = 2 * e_units + 8

    def step(t):
        @pl.when(t < done)
        def _():
            compute(t)

        for i, stage_of in reversed(list(enumerate(stages))):
            @pl.when(jnp.logical_and(t >= i, t - i < subs))
            def _(stage_of=stage_of, i=i):
                stage_of(t - i)

        @pl.when(t == 4)
        def _():
            act_pass(0)

        @pl.when(t == done + 5)
        def _():
            act_pass(1)

        for i in range(len(hops) + 1):
            @pl.when(t == done + i)
            def _(i=i):
                if i > 0:
                    small_copy(i - 1).wait_send()
                    small_copy(i - 1).wait_recv()
                    small[...] += round_in[i - 1]
                if i < len(hops):
                    small_copy(i).start()
                else:
                    lcopy(small, small_out, keep_sem.at[2]).start()

    loop(subs + len(stages) - 1, step)

    def finish(w):
        if n == 4:
            for h in range(2):
                far_copy(w, h).wait_send()

        @pl.when(edge)
        def _():
            z_to(w, block_out, up, 0, inner).wait_send()

        @pl.when(jnp.logical_not(edge))
        def _():
            z_to(w, block_out, across, 1, other).wait_send()
            z_to(w, down, down, 2, outer).wait_send()

        lcopy(down.at[w], grad_ref.at[w], store_sem.at[w]).wait()

    loop(subs, finish)
    core_copy(units - 1).wait_send()
    for w in (subs - 2, subs - 1):
        for i in sends_of(w):
            i.wait_send()
    for which in range(2):
        for k in range(1, nz):
            act(which, k).wait_send()
        for k in range(nz):
            pass_copy(which, k).wait_send()
            pass_in(which, k).wait_recv()
    lcopy(small, small_out, keep_sem.at[2]).wait()


def backward(n, nz, lengths, full, x, q, k, v, o, lse, n1, r1, u, h, gp, ds, dz, y, vec, small):
    _, units, model, width = full.shape
    e_units = h.shape[0]
    rows = model // n
    half = rows // 2
    slots = x.shape[0]
    block = slots // nz
    subs = 2 * units
    by_half = (2, slots, UNIT)
    near = (subs, 2, 2, half, SUB) if n == 4 else (subs, n - 1, rows, SUB)
    near_sems = near[:3] if n == 4 else near[:2]
    far = (subs, 2, half, SUB) if n == 4 else (1, 2, 16, SUB)
    blocks = (subs, rows, SUB)
    hops = 1 + (n.bit_length() - 1) + (nz.bit_length() - 1)
    outs = [
        (blocks, BF16), ((2 * nz, block, model), BF16), ((2 * nz, block, model), BF16), ((24, UNIT), F32),
        ((units, 2, model, SUB), BF16), ((units, 2, model, SUB), BF16),
    ]
    scratch = [
        ((slots, model), BF16), ((3, *by_half), BF16), (by_half, BF16), ((slots, 128), F32), ((slots, model), F32),
        ((slots, 128), F32), ((slots, model), BF16), ((slots, model), BF16), ((slots, model), F32), (by_half, BF16),
        ((3, *by_half), BF16), ((2, model, UNIT), BF16), ((2, model, UNIT), BF16), (by_half, BF16), (by_half, BF16),
        (by_half, BF16), ((2, 2, model, SUB), BF16), ((24, UNIT), F32), ((hops, 24, UNIT), F32),
        ((2, model, SUB), BF16), ((2, model, SUB), BF16), ((2, model, SUB), BF16),
        (near, BF16), (far, BF16), (far, BF16), (blocks, BF16), (blocks, BF16), (blocks, BF16), (blocks, BF16),
        ((slots, model), BF16),
    ]
    return pl.pallas_call(
        functools.partial(backward_kernel, n, nz),
        name="backward_and_reduce",
        out_shape=[jax.ShapeDtypeStruct(a, b) for a, b in outs],
        in_specs=[SMEM] + [ANY] * 15 + [VMEM, ANY],
        out_specs=[ANY] * len(outs),
        scratch_shapes=[pltpu.VMEM(a, b) for a, b in scratch]
        + [
            DMA((12,)), DMA((4,)), DMA((1,)), DMA((units,)), DMA((units,)), DMA((2, 2)),
            DMA(near_sems), DMA(near_sems), DMA((subs, 2)), DMA((subs, 2)),
            DMA((subs, 3)), DMA((subs, 3)), DMA((subs,)),
            DMA((2, nz)), DMA((2, nz)), DMA((2, nz)), DMA((2, nz)), DMA((3,)), DMA((hops,)), DMA((hops,)),
        ],
        compiler_params=pltpu.CompilerParams(
            collective_id=1, has_side_effects=True, vmem_limit_bytes=61 * 2**20
        ),
    )(lengths, full, x, q, k, v, o, lse, n1, r1, u, h, gp, ds, dz, y, vec, small)


def body(n, nz, inputs, lengths, wq, wk, wv, wo, we, wr, qb, vb, eb, ob, rb, g1, s1, g2, s2, cotangent):
    s, c = lax.axis_index("shard"), lax.axis_index("tp")
    rows = wq.shape[0]
    model = rows * n
    e_units = we.shape[1] // UNIT
    wide = max(rows, 128)

    def lines(v, count):
        v = v.reshape(count, -1)
        return jnp.pad(v, ((0, 0), (0, wide - v.shape[1])))

    blank = jnp.zeros((2, wide), BF16)
    pk = jnp.concatenate(
        [lines(qb, 1), lines(vb, 1), lines(eb, e_units), blank]
        + [lines(v, 1) for v in (ob, rb, g1, s1, g2, s2)]
        + [blank]
    )
    (full, x, q, k, v, o, lse, n1, r1, u, h, gp, ds, dz, y, vec, small) = forward(
        n, nz, lengths, inputs, cotangent, wq, wk, wv, wo, we, wr, pk
    )
    grads, ys, dx, small, _, _ = backward(
        n, nz, lengths, full, x, q, k, v, o, lse, n1, r1, u, h, gp, ds, dz, y, vec, small
    )

    def joined(picks):
        return jnp.concatenate([grads[i] for i in picks], 1).astype(F32)

    dwr = joined([4 * j + b for j in range(e_units) for b in range(2)])
    dwe = joined([4 * j + 2 + b for j in range(e_units) for b in range(2)])
    at = 4 * e_units
    dwo, dwq, dwk, dwv = [joined([at + 2 * i, at + 2 * i + 1]) for i in range(4)]
    he = HD // n
    small = small.reshape(-1)
    vectors = []
    at = 0
    for v in (qb, vb, eb):
        m = small[at : at + 2 * v.shape[0] * HD].reshape(2, v.shape[0], n, he)
        m = lax.dynamic_slice(m, (c, 0, s, 0), (1, v.shape[0], 1, he))
        vectors.append(m.reshape(v.shape))
        at += 2 * v.shape[0] * HD
    for _ in range(6):
        vectors.append(lax.dynamic_slice(small, (at + s * rows,), (rows,)))
        at += model
    return (ys.astype(F32), dx.astype(F32), dwq, dwk, dwv, dwo.T, dwe, dwr.T, *vectors)


def solution(mesh):
    w, wt, v = P("shard", "tp"), P("tp", "shard"), P("shard")
    rows = P("shard", "ctx", None)
    return jax.shard_map(
        functools.partial(body, mesh.shape["shard"], mesh.shape["ctx"]),
        mesh=mesh,
        in_specs=(rows, v, w, w, w, wt, w, wt, wt, wt, wt, v, v, v, v, v, v, rows),
        out_specs=(rows, rows, w, w, w, wt, w, wt, wt, wt, wt, v, v, v, v, v, v),
        check_vma=False,
    )
```

time: 699 us -> 344 us (0.49); the launches traced: 687 us -> 343 us
  local copies, waits for them, and re-layouts: 177 us -> 23 us
  matrix products: 153 us -> 0 us
  blocking collectives: 49.6 us -> 0 us
  Pallas kernels: 280 us -> 311 us
  other arithmetic: 26.5 us -> 8.78 us
    dot_general x23 -> x0, matrix products: 143 us -> none  [mm(): return jnp.einsum(form, a, b, preferred_element_type=F32)]
    transpose x13 -> x0, local copies, waits for them, and re-layouts: 58.8 us -> none  [the longest x2 22.8 us: body(): wr_f = full[:, 4 + e_units:].transpose(2, 0, 1, 3).reshape(model, -1)]
    psum x1 -> x0, blocking collectives: 38.9 us -> none  [body(): small = lax.psum(small, ('shard', 'ctx', 'tp'))]
    reshape x20 -> x12, local copies, waits for them, and re-layouts: 41.6 us -> 5.9 us  [the longest x9 5.58 us: lines(): v = v.reshape(count, -1)]
    convert_element_type x6 -> x0, local copies, waits for them, and re-layouts: 31.3 us -> none  [the longest x2 23.9 us: unit_form(): return w.astype(BF16).reshape(model, 2, -1, UNIT).transpose(1, 2, 0, 3)]
    pallas_call x2, Pallas kernels: 280 us -> 311 us  [the longest x1 184 us: backward(): pl.pallas_call(functools.partial(backward_kernel, n, nz), name='backward_...]
    unnamed x110 -> x17, local copies, waits for them, and re-layouts: 37.4 us -> 10.6 us
    convert_element_type x6 -> x4, other arithmetic: 21.3 us -> 7.62 us  [the longest x2 2.66 us: joined(): return jnp.concatenate([grads[i] for i in picks], 1).astype(F32)]
where the time goes in v2:
time: 344 us; the launch traced here: 343 us
  Pallas kernels  311 us (90%)
  local copies, waits for them, and re-layouts  23 us (7%)
  other arithmetic  8.78 us (3%)
    pallas_call x1, Pallas kernels, backward(): pl.pallas_call(functools.partial(backward_kernel, n, nz), name='backward_...  184 us
    pallas_call x1, Pallas kernels, forward(): pl.pallas_call(functools.partial(forward_kernel, n, nz), name='gather_and...  127 us
    unnamed x17, local copies, waits for them, and re-layouts  10.6 us

profile of v2, /device:TPU:0, one launch (start us, length us, event | category | flops | bytes accessed | tf_op | source)
XLA Modules:
  0.0 343.4 jit_solution(7563048379688360842)
XLA Ops:
  0.7 0.8 copy.46
  1.4 0.1 reshape.90
  1.5 0.8 reshape.88
  2.3 0.8 reshape.89
  3.1 0.7 reshape.91
  3.7 0.7 reshape.92
  4.4 0.7 reshape.93
  5.1 0.7 reshape.94
  5.7 0.7 reshape.95
  6.4 0.7 reshape.96
  7.0 1.2 concatenate.21.pk_ref
  8.3 127.3 %gather_and_forward.1 = (bf16[2,12,1024,512]{3,2,1,0:T(8,128)(2,1)}, bf16[512,1024]{1,0:T(8,128)(2,1)}, bf16[2,512,512]{2,1,0:T(8,128)(2,1)}, bf16[2,512,512]{2,...) custom-call(s32[8]{0:T(128)} %len_ref.3, ...), custom_call_target="tpu_custom_call" | custom-call | tf_op jit(solution)/shard_map/gather_and_forward/pallas_call | solution.py:449
  135.6 183.5 %backward_and_reduce.1 = (bf16[24,256,256]{2,1,0:T(8,128)(2,1)}, bf16[8,128,1024]{2,1,0:T(8,128)(2,1)}, bf16[8,128,1024]{2,1,0:T(8,128)(2,1)}, f32[24,512]{1,0:T...) custom-call(s32[8]{0:T(128)} %len_ref.3, ...), custom_call_target="tpu_custom_call" | custom-call | tf_op jit(solution)/shard_map/backward_and_reduce/pallas_call | solution.py:939
  319.1 0.8 fusion.1
  319.9 0.1 reshape.97
  320.0 0.1 reshape.99
  320.1 0.6 constant_dynamic-slice_fusion.1
  320.7 1.0 bitcast_dynamic-update-slice_fusion.7
  321.7 1.0 bitcast_dynamic-update-slice_fusion.6
  322.7 1.0 bitcast_dynamic-update-slice_fusion.5
  323.7 1.0 bitcast_dynamic-update-slice_fusion.4
  324.7 1.0 bitcast_dynamic-update-slice_fusion.3
  325.7 1.0 bitcast_dynamic-update-slice_fusion.2
  326.7 1.0 bitcast_dynamic-update-slice_fusion.1
  327.7 1.0 bitcast_dynamic-update-slice_fusion
  328.7 0.2 convert_bitcast_fusion
  329.0 1.8 copy.51
  330.8 1.6 convert_element_type.30
  332.4 0.0 copy-start.1
  332.4 1.5 slice_bitcast_fusion.1
  333.9 1.1 maximum_convert_fusion.1
  335.0 0.9 convert_bitcast_fusion.1
  335.9 1.0 copy.50
  336.9 0.0 copy-done.1
  336.9 0.0 copy-start
  336.9 2.5 convert_element_type.25
  339.4 0.0 copy-done
  339.4 0.0 copy-start.2
  339.4 2.5 convert_element_type.26
  341.9 0.0 copy-done.2
  341.9 0.1 reshape.101
  342.0 0.7 copy.49
  342.7 0.7 fusion
  (7 shorter events, 0.1 us)
Async XLA Ops:
  332.4 4.5 %copy-start.1 = (bf16[8,128,1024]{2,1,0:T(8,128)(2,1)S(1)}, bf16[8,128,1024]{2,1,0:T(8,128)(2,1)}, u32[]{:S(2)}) copy-start(bf16[8,128,1024]{2,1,0:T(8,128)(2,1)} %get-tuple-element.55) | copy-start | bytes 6291460
  336.9 2.5 copy-start
  339.4 2.5 copy-start.2

commit v3 on v2

v3 whole, which is shorter than its diff:
```python
import functools

import jax
import jax.numpy as jnp
from jax import lax
from jax.experimental import pallas as pl
from jax.experimental.pallas import tpu as pltpu
from jax.sharding import PartitionSpec as P

HD = 64
UNIT = 512
SUB = 256
SLOTS = 4
LAGS = (0, 5, 3, 1, 11, 9, 7)
PACE = 5
PASS = 24
PIECES = 8
ACTS = (0, 10)
EPSILON = 1e-05
MASKED = -1e30
MESH = pl.DeviceIdType.MESH
F32 = jnp.float32
BF16 = jnp.bfloat16
DMA = pltpu.SemaphoreType.DMA
ANY = pl.BlockSpec(memory_space=pl.ANY)
VMEM = pl.BlockSpec(memory_space=pltpu.VMEM)
SMEM = pl.BlockSpec(memory_space=pltpu.SMEM)


def place():
    return lax.axis_index("shard"), lax.axis_index("ctx"), lax.axis_index("tp")


def rcopy(src, dst, send, recv, dev):
    return pltpu.make_async_remote_copy(
        src_ref=src, dst_ref=dst, send_sem=send, recv_sem=recv, device_id=dev, device_id_type=MESH
    )


def lcopy(src, dst, sem):
    return pltpu.make_async_copy(src, dst, sem)


def greet(devices):
    barrier = pltpu.get_barrier_semaphore()
    for dev in devices:
        pl.semaphore_signal(barrier, inc=1, device_id=dev, device_id_type=MESH)
    pl.semaphore_wait(barrier, len(devices))


def rows_at(i, size):
    return pl.ds(pl.multiple_of(i * size, size), size)


def mm(a, b):
    return jnp.dot(a, b, preferred_element_type=F32)


def mm_nt(a, b):
    return lax.dot_general(a, b, (((1,), (1,)), ((), ())), preferred_element_type=F32)


def mm_tn(a, b):
    return lax.dot_general(a, b, (((0,), (0,)), ((), ())), preferred_element_type=F32)


def loop(count, fn):
    def step(i, carry):
        fn(i)
        return carry

    lax.fori_loop(0, count, step, 0)


def mean(v):
    return jnp.mean(v, -1, keepdims=True)


def forward_kernel(
    n, nz,
    len_ref, x_ref, g_ref, wq_ref, wk_ref, wv_ref, wo_ref, we_ref, wr_ref,
    qb_ref, vb_ref, eb_ref, ob_ref, rb_ref, g1_ref, s1_ref, g2_ref, s2_ref,
    full_ref, x_out, q_out, k_out, v_out, o_out, p_out, n1_out, r1_out, u_out, h_out, gp_out,
    ds_out, dz_out, y_out, vec_out, small_out,
    own, wo_in, wr_in, xin, act_low, xv, cotv, qkv, o_v, p_v, n1_v, r1_v, u_v, ulow_v, h_v, gp_v, acc,
    dz_v, y_v, wbuf, pk_ref, pk_wide, pkall, head_bias, bias, vec, small,
    own_send, own_recv, fwd_send, fwd_recv, core_send, core_recv, act_send, act_recv,
    pk_send, pk_recv, in_sem, act_sem, fetch_sem, out_sem, p_sem,
):
    s, z, c = place()
    units, rows, width = own.shape
    half = rows // 2
    model = rows * n
    slots = xv.shape[0]
    block = slots // nz
    e_units = we_ref.shape[1] // width
    group = [(s ^ k, z, c if j == 0 else 1 - c) for k in range(n) for j in range(2) if k + j > 0]
    mine = rows_at(s, rows)
    zrows = rows_at(z, block)

    ins = [lcopy(r, own.at[i], in_sem.at[i]) for i, r in enumerate((wq_ref, wk_ref, wv_ref))]
    ins += [
        lcopy(we_ref.at[:, pl.ds(j * width, width)], own.at[4 + j], in_sem.at[3 + j]) for j in range(e_units)
    ]
    ins_o = lcopy(wo_ref, wo_in, in_sem.at[3 + e_units])
    ins_r = lcopy(wr_ref, wr_in, in_sem.at[4 + e_units])

    def to(k):
        return lax.rem(z + k, nz)

    def act_load(which, k):
        src = (x_ref, g_ref)[which]
        return lcopy(src.at[2 * to(k) + c], xin.at[k], act_sem.at[k])

    def act(which, k):
        dst = (xv, cotv)[which]
        return rcopy(
            act_low.at[which, k], dst.at[zrows, :], act_send.at[which, k], act_recv.at[which, k], (s, to(k), c)
        )

    def act_in(which, k):
        dst = (xv, cotv)[which]
        src = lax.rem(z + nz - k, nz)
        at = dst.at[rows_at(src, block), :]
        return rcopy(at, at, act_send.at[which, k], act_recv.at[which, k], (s, src, c))

    def act_share(which):
        for k in range(1, nz):
            act_load(which, k).wait()
            act_low[which, k] = xin[k].astype(BF16)
            act(which, k).start()
        act_load(which, 0).wait()
        (xv, cotv)[which][zrows, :] = xin[0].astype(BF16)

    for k in range(1, nz):
        act_load(0, k).start()
    for i in ins:
        i.start()
    act_load(0, 0).start()
    ins_o.start()
    ins_r.start()

    he = HD // n
    heads = [qb_ref, vb_ref, eb_ref]
    head_rows = sum(r.shape[0] for r in heads)
    pk_wide[...] = jnp.zeros_like(pk_wide)
    at = 0
    for r in heads:
        pk_wide[at : at + r.shape[0], :he] = r[...].astype(F32)
        at += r.shape[0]
    for i, r in enumerate((ob_ref, rb_ref, g1_ref, s1_ref, g2_ref, s2_ref)):
        pk_wide[at + 8 + i : at + 9 + i, :rows] = r[...].reshape(1, rows).astype(F32)
    pk_ref[...] = pk_wide[...].astype(BF16)
    greet(group + [(s, lax.rem(z + k, nz), c) for k in range(1, nz)])

    def pk_copy(k, j):
        return rcopy(
            pk_ref, pkall.at[s, c], pk_send.at[k, j], pk_recv.at[k, j], (s ^ k, z, c if j == 0 else 1 - c)
        )

    def pk_in(k, j):
        at = pkall.at[s ^ k, c if j == 0 else 1 - c]
        return rcopy(at, at, pk_send.at[k, j], pk_recv.at[k, j], (s ^ k, z, c if j == 0 else 1 - c))

    pk_pairs = [(k, j) for k in range(n) for j in range(2) if k + j > 0]
    for k, j in pk_pairs:
        pk_copy(k, j).start()
    pkall[s, c] = pk_ref[...]

    direct = [1, 2] if n == 4 else list(range(1, n))

    def own_copy(u, k):
        return rcopy(
            own.at[u], full_ref.at[c, u, mine, :], own_send.at[u, k], own_recv.at[u, k], (s ^ k, z, c)
        )

    def own_in(u, k):
        at = full_ref.at[c, u, rows_at(s ^ k, rows), :]
        return rcopy(at, at, own_send.at[u, k], own_recv.at[u, k], (s ^ k, z, c))

    def half_at(k, h):
        return pl.ds(pl.multiple_of((s ^ k) * rows + h * half, half), half)

    def fwd_copy(u, h):
        at = full_ref.at[c, u, half_at(2 - h, h), :]
        return rcopy(at, at, fwd_send.at[u, h], fwd_recv.at[u, h], (s ^ (1 + h), z, c))

    def fwd_in(u, h):
        at = full_ref.at[c, u, half_at(3, h), :]
        return rcopy(at, at, fwd_send.at[u, h], fwd_recv.at[u, h], (s ^ (1 + h), z, c))

    def core_copy(u, k):
        at = full_ref.at[c, u, rows_at(s ^ k, rows), :]
        return rcopy(at, at, core_send.at[u, k], core_recv.at[u, k], (s, z, 1 - c))

    def core_in(u, k):
        at = full_ref.at[1 - c, u, rows_at(s ^ k, rows), :]
        return rcopy(at, at, core_send.at[u, k], core_recv.at[u, k], (s, z, 1 - c))

    ahead = 2
    for i in ins[:ahead]:
        i.wait()
    for u in range(ahead):
        for k in direct:
            own_copy(u, k).start()
    act_share(0)
    for k in range(nz):
        act_load(1, k).start()
    for i in ins[ahead:]:
        i.wait()
    ins_o.wait()
    own[3] = wo_in[...].T
    ins_r.wait()

    def turn(j):
        own[4 + e_units + j] = wr_in[rows_at(j, width), :].T

    loop(e_units, turn)
    keep = lcopy(own, full_ref.at[c, :, mine, :], in_sem.at[5 + e_units])
    keep.start()
    share = rcopy(
        own, full_ref.at[c, :, mine, :], core_send.at[units, 0], core_recv.at[units, 0], (s, z, 1 - c)
    )
    share.start()
    theirs = full_ref.at[1 - c, :, mine, :]
    share_in = rcopy(theirs, theirs, core_send.at[units, 0], core_recv.at[units, 0], (s, z, 1 - c))
    act_share(1)

    for k, j in pk_pairs:
        pk_in(k, j).wait_recv()
    wide = pk_ref.shape[1]
    head_bias[...] = jnp.zeros_like(head_bias)
    vec[...] = jnp.zeros_like(vec)

    def place_one(sh):
        r = lax.broadcasted_iota(jnp.int32, (wide, width), 0)
        col = lax.broadcasted_iota(jnp.int32, (wide, width), 1)
        pick = jnp.where(jnp.logical_and(r < he, col % HD == sh * he + r), 1.0, 0.0).astype(BF16)
        row = lax.broadcasted_iota(jnp.int32, (head_rows, width), 0)
        col = lax.broadcasted_iota(jnp.int32, (head_rows, width), 1)
        own_head = col // HD == row % 8
        for j in range(2):
            head_bias[j] += jnp.where(own_head, mm(pkall[sh, j, :head_rows, :], pick), 0.0)
        r = lax.broadcasted_iota(jnp.int32, (wide, model), 0)
        col = lax.broadcasted_iota(jnp.int32, (wide, model), 1)
        hit = jnp.logical_and(r < rows, col == sh * rows + r)
        vec[...] += mm(pkall[sh, 0, head_rows:, :], jnp.where(hit, 1.0, 0.0).astype(BF16))

    loop(n, place_one)
    for j in range(2):
        for i in range(head_rows // 8):
            bias[i : i + 1, j * width : (j + 1) * width] = jnp.sum(
                head_bias[j, 8 * i : 8 * i + 8, :], 0, keepdims=True
            )
    small[...] = jnp.zeros_like(small)
    vec_copy = lcopy(vec, vec_out, out_sem.at[0])
    vec_copy.start()
    length = len_ref[2 * z + c]
    live_keys = lax.broadcasted_iota(jnp.int32, (1, slots), 1) < length
    lane = lax.broadcasted_iota(jnp.int32, (slots, 128), 1)
    outs = []

    def fetch(u):
        slot = lax.rem(u, 2)
        return [
            lcopy(full_ref.at[hf, u], wbuf.at[slot, :, hf * width : (hf + 1) * width], fetch_sem.at[slot, hf])
            for hf in range(2)
        ]

    def ready(u):
        @pl.when(u == 0)
        def _():
            keep.wait()
            share_in.wait_recv()

        for k in range(1, n):
            core_in(u, k).wait_recv()

    def p_copy(p):
        return lcopy(p_v.at[lax.rem(p, 2)], p_out.at[p], p_sem.at[lax.rem(p, 2)])

    def attention(p):
        at = rows_at(p, 128)
        q, k, v = qkv[0, :, at], qkv[1, :, at], qkv[2, :, at]

        @pl.when(p >= 2)
        def _():
            p_copy(p - 2).wait()

        out = None
        for h in range(2):
            part = lane < HD if h == 0 else lane >= HD
            scores = mm_nt(jnp.where(part, q, 0), k) * HD ** (-0.5)
            scores = jnp.where(live_keys, scores, MASKED)
            e = jnp.exp(scores - jnp.max(scores, -1, keepdims=True))
            low = (e * (1.0 / jnp.sum(e, -1, keepdims=True))).astype(BF16)
            p_v[lax.rem(p, 2), h] = low
            term = mm(low, jnp.where(part, v, 0))
            out = term if out is None else out + term
        o_v[:, at] = out.astype(BF16)
        p_copy(p).start()

    pairs = model // 128
    rb = 128

    def compute(u):
        w = wbuf.at[lax.rem(u, 2)]

        @pl.when(u == 0)
        def _():
            for k in range(1, nz):
                act_in(0, k).wait_recv()

        @pl.when(u < 3)
        def _():
            add = jnp.where(u == 0, bias[0:1, :], jnp.where(u == 2, bias[1:2, :], 0.0))
            qkv[u] = (mm(xv[...], w[...]) + add).astype(BF16)

        @pl.when(u == 2)
        def _():
            loop(pairs // 2, attention)

        @pl.when(u == 3)
        def _():
            loop(pairs // 2, lambda p: attention(p + pairs // 2))
            acc[...] = mm_nt(o_v[...], w[...]) + xv[...].astype(F32)

            def norm(i):
                at = rows_at(i, rb)
                first = acc[at, :] + vec[8:9, :]
                centred = first - mean(first)
                inv = lax.rsqrt(mean(centred * centred) + EPSILON)
                n1 = centred * inv
                n1_v[at, :] = n1
                r1_v[at, :] = jnp.broadcast_to(inv, (rb, 128))
                up = n1 * vec[10:11, :] + vec[11:12, :]
                ulow_v[at, :] = up.astype(BF16)
                u_v[at, :] = up

            loop(slots // rb, norm)
            for i, (src, dst) in enumerate(
                ((qkv.at[0], q_out), (qkv.at[1], k_out), (qkv.at[2], v_out), (o_v, o_out),
                 (n1_v, n1_out), (r1_v, r1_out), (ulow_v, u_out), (xv, x_out))
            ):
                lcopy(src, dst, out_sem.at[1 + i]).start()

        @pl.when(jnp.logical_and(u >= 4, u < 4 + e_units))
        def _():
            j = u - 4
            pre = mm(ulow_v[...], w[...]) + bias[pl.ds(2 + j, 1), :]
            phi = 0.5 * (1.0 + lax.erf(pre * 0.7071067811865476))
            h_v[j] = (pre * phi).astype(BF16)
            gp_v[j] = (phi + pre * jnp.exp(-0.5 * pre * pre) * 0.3989422804014327).astype(BF16)
            lcopy(h_v.at[j], h_out.at[j], out_sem.at[10]).start()
            lcopy(gp_v.at[j], gp_out.at[j], out_sem.at[11]).start()
            lcopy(h_v.at[j], h_out.at[j], out_sem.at[10]).wait()
            lcopy(gp_v.at[j], gp_out.at[j], out_sem.at[11]).wait()

        @pl.when(u >= 4 + e_units)
        def _():
            u_v[...] += mm_nt(h_v[u - 4 - e_units], w[...])

    def step(u):
        @pl.when(u < units)
        def _():
            @pl.when(u + ahead < units)
            def _():
                for k in direct:
                    own_copy(u + ahead, k).start()

            for k in direct:
                own_in(u, k).wait_recv()
                if n == 4:
                    fwd_copy(u, 2 - k).start()
                core_copy(u, k).start()

        if n == 4:
            @pl.when(jnp.logical_and(u > 0, u <= units))
            def _():
                for h in range(2):
                    fwd_in(u - 1, h).wait_recv()
                core_copy(u - 1, 3).start()

        @pl.when(u >= 2)
        def _():
            for i in fetch(u - 2):
                i.wait()
            compute(u - 2)

        @pl.when(jnp.logical_and(u > 0, u <= units))
        def _():
            ready(u - 1)
            for i in fetch(u - 1):
                i.start()

    loop(units + 2, step)

    for k in range(1, nz):
        act_in(1, k).wait_recv()

    def norm2(i):
        at = rows_at(i, rb)
        second = u_v[at, :] + vec[9:10, :]
        centred = second - mean(second)
        inv = lax.rsqrt(mean(centred * centred) + EPSILON)
        n2 = centred * inv
        gain = vec[12:13, :]
        y_v[at, :] = (n2 * gain + vec[13:14, :]).astype(BF16)
        row = lax.broadcasted_iota(jnp.int32, (rb, 1), 0) + i * rb
        grad = jnp.where(row < length, cotv[at, :].astype(F32), 0.0)
        scaled = grad * gain
        back = inv * (scaled - mean(scaled) - n2 * mean(scaled * n2))
        acc[at, :] = back
        low = back.astype(BF16)
        dz_v[at, :] = low
        for r, v in ((14, low.astype(F32)), (20, grad * n2), (22, grad)):
            v = jnp.sum(v, 0, keepdims=True)
            small[r : r + 1, :] += v[:, :width]
            small[r + 1 : r + 2, :] += v[:, width:]

    loop(slots // rb, norm2)
    last = [
        lcopy(src, dst, out_sem.at[12 + i])
        for i, (src, dst) in enumerate(((acc, ds_out), (dz_v, dz_out), (y_v, y_out), (small, small_out)))
    ]
    for i in last:
        i.start()

    def finish(u):
        for k in direct:
            own_copy(u, k).wait_send()
        if n == 4:
            for h in range(2):
                fwd_copy(u, h).wait_send()
        for k in range(1, n):
            core_copy(u, k).wait_send()

    loop(units, finish)
    share.wait_send()
    for k, j in pk_pairs:
        pk_copy(k, j).wait_send()
    for which in range(2):
        for k in range(1, nz):
            act(which, k).wait_send()
    vec_copy.wait()
    for p in (pairs - 2, pairs - 1):
        p_copy(p).wait()
    for i, (src, dst) in enumerate(
        ((qkv.at[0], q_out), (qkv.at[1], k_out), (qkv.at[2], v_out), (o_v, o_out),
         (n1_v, n1_out), (r1_v, r1_out), (ulow_v, u_out), (xv, x_out))
    ):
        lcopy(src, dst, out_sem.at[1 + i]).wait()
    for i in last:
        i.wait()


def forward(n, nz, lengths, inputs, cotangent, wq, wk, wv, wo, we, wr, heads, vectors):
    seqs, block, model = inputs.shape
    rows = wq.shape[0]
    e_units = we.shape[1] // UNIT
    units = 4 + 2 * e_units
    slots = nz * block
    head_rows = sum(v.shape[0] for v in heads)
    pk = (head_rows + 16, max(rows, 128))
    outs = [
        ((2, units, model, UNIT), BF16), ((slots, model), BF16),
        ((slots, model), BF16), ((slots, model), BF16), ((slots, model), BF16), ((slots, model), BF16),
        ((model // 128, 2, slots, slots), BF16), ((slots, model), F32), ((slots, 128), F32), ((slots, model), BF16),
        ((e_units, slots, model), BF16), ((e_units, slots, model), BF16),
        ((slots, model), F32), ((slots, model), BF16), ((slots, model), BF16), ((16, model), F32),
        ((24, UNIT), F32),
    ]
    scratch = [
        ((units, rows, UNIT), BF16), (wo.shape, BF16), (wr.shape, BF16), ((nz, block, model), F32),
        ((2, nz, block, model), BF16), ((slots, model), BF16), ((slots, model), BF16), ((3, slots, model), BF16),
        ((slots, model), BF16), ((2, 2, slots, slots), BF16), ((slots, model), F32), ((slots, 128), F32),
        ((slots, model), F32), ((slots, model), BF16), ((e_units, slots, model), BF16),
        ((e_units, slots, model), BF16), ((slots, model), F32),
        ((slots, model), BF16), ((slots, model), BF16), ((2, model, 2 * UNIT), BF16),
        (pk, BF16), (pk, F32), ((n, 2, *pk), BF16), ((2, head_rows, UNIT), F32), ((16, 2 * UNIT), F32), ((16, model), F32), ((24, UNIT), F32),
    ]
    return pl.pallas_call(
        functools.partial(forward_kernel, n, nz),
        name="gather_and_forward",
        out_shape=[jax.ShapeDtypeStruct(a, b) for a, b in outs],
        in_specs=[SMEM] + [ANY] * 8 + [VMEM] * 9,
        out_specs=[ANY] * len(outs),
        scratch_shapes=[pltpu.VMEM(a, b) for a, b in scratch]
        + [
            DMA((units, n)), DMA((units, n)), DMA((units, 2)), DMA((units, 2)),
            DMA((units + 1, n)), DMA((units + 1, n)), DMA((2, nz)), DMA((2, nz)),
            DMA((n, 2)), DMA((n, 2)), DMA((6 + e_units,)), DMA((nz,)), DMA((2, 2)), DMA((16,)), DMA((2,)),
        ],
        compiler_params=pltpu.CompilerParams(
            collective_id=0, has_side_effects=True, vmem_limit_bytes=60 * 2**20
        ),
    )(lengths, inputs, cotangent, wq, wk, wv, wo, we, wr, *heads, *vectors)


def backward_kernel(
    n, nz,
    full_ref, x_ref, q_ref, k_ref, v_ref, o_ref, p_ref, n1_ref, r1_ref, u_ref, h_ref, gp_ref,
    ds_ref, dz_ref, y_ref, vec_ref, small_ref,
    grad_ref, ys_ref, dx_ref, small_out, part_ref, got_ref,
    x_v, qkv, o_v, p_v, n1_v, r1_v, u_v, dz_v, du, wr_v, we_v, h_v, gp_v, dpre, pbuf, small, round_in,
    stage, gstage, total, near, pair_sum, far, up, across, down, block_out,
    load_sem, w_sem, p_sem, part_sem, core_send, core_recv, stage_sem, near_send, near_recv, far_send, far_recv,
    z_send, z_recv, store_sem, act_send, act_recv, pass_send, pass_recv, keep_sem, small_send, small_recv,
):
    s, z, c = place()
    units = part_ref.shape[0]
    subs = 2 * units
    e_units = h_ref.shape[0]
    model = total.shape[1]
    width = UNIT
    rows = model // n
    half = rows // 2
    slots = x_v.shape[0]
    block = slots // nz
    zrows = rows_at(z, block)
    mates = [(dz_ref, dz_v), (small_ref, small), (ds_ref, du), (n1_ref, n1_v), (r1_ref, r1_v), (o_ref, o_v),
             (u_ref, u_v), (q_ref, qkv.at[0]), (k_ref, qkv.at[1]), (v_ref, qkv.at[2]), (x_ref, x_v)]
    loads = [lcopy(a, b, load_sem.at[i]) for i, (a, b) in enumerate(mates)]

    class Weights:
        def __init__(self, buf, i):
            self.buf, self.i = buf, i

        def copies(self, u):
            return [
                lcopy(full_ref.at[hf, u], self.buf.at[:, hf * width : (hf + 1) * width], w_sem.at[self.i, hf])
                for hf in range(2)
            ]

        def start(self, u):
            for i in self.copies(u):
                i.start()

        def wait(self, u):
            for i in self.copies(u):
                i.wait()

    wr, we = Weights(wr_v, 0), Weights(we_v, 1)

    def load_h(j):
        return lcopy(h_ref.at[j], h_v, w_sem.at[2, 0])

    def load_gp(j):
        return lcopy(gp_ref.at[j], gp_v, w_sem.at[2, 1])

    def load_p(p):
        return lcopy(p_ref.at[p], p_v.at[lax.rem(p, 2)], p_sem.at[lax.rem(p, 2)])

    loads[0].start()
    load_h(0).start()
    loads[1].start()
    load_gp(0).start()
    wr.start(4 + e_units)
    we.start(4)
    for i in loads[2:]:
        i.start()
    for p in range(2):
        load_p(p).start()
    greet(
        [(s ^ k, z, c) for k in range(1, n)]
        + [(s, z, 1 - c)]
        + [(s, lax.rem(z + k, nz), c) for k in range(1, nz)]
    )

    def act(which, k, i):
        src, dst = ((y_ref, ys_ref), (dz_v, dx_ref))[which]
        to = lax.rem(z + k, nz)
        some = block // PIECES
        return rcopy(
            src.at[pl.ds(pl.multiple_of(to * block + i * some, some), some), :],
            dst.at[2 * z + c, rows_at(i, some), :],
            act_send.at[which, k, i], act_recv.at[which, k, i], (s, to, c),
        )

    def act_in(which, k, i):
        src = lax.rem(z + nz - k, nz)
        at = (ys_ref, dx_ref)[which].at[2 * src + c, rows_at(i, block // PIECES), :]
        return rcopy(at, at, act_send.at[which, k, i], act_recv.at[which, k, i], (s, src, c))

    def act_keep(which):
        src, dst = ((y_ref, ys_ref), (dz_v, dx_ref))[which]
        return lcopy(src.at[zrows, :], dst.at[2 * z + c], keep_sem.at[which])

    def pass_copy(which, k):
        at = (ys_ref, dx_ref)[which].at[2 * lax.rem(z + nz - k, nz) + c]
        return rcopy(at, at, pass_send.at[which, k], pass_recv.at[which, k], (s, z, 1 - c))

    def pass_in(which, k):
        at = (ys_ref, dx_ref)[which].at[2 * lax.rem(z + nz - k, nz) + 1 - c]
        return rcopy(at, at, pass_send.at[which, k], pass_recv.at[which, k], (s, z, 1 - c))

    def act_some(which, i):
        for k in range(1, nz):
            act(which, k, i).start()

    def act_pass(which):
        for k in range(1, nz):
            loop(PIECES, lambda i: act_in(which, k, i).wait_recv())
            pass_copy(which, k).start()
        act_keep(which).wait()
        pass_copy(which, 0).start()

    act_keep(0).start()

    def core_copy(u):
        return rcopy(pbuf.at[0], got_ref.at[u], core_send.at[u], core_recv.at[u], (s, z, 1 - c))

    def core_in(u):
        return rcopy(got_ref.at[u], got_ref.at[u], core_send.at[u], core_recv.at[u], (s, z, 1 - c))

    def part_copy(u):
        return lcopy(pbuf.at[1], part_ref.at[u], part_sem.at[0])

    def settle(u):
        core_copy(u).wait_send()
        part_copy(u).wait()

    def emit(u, i, value):
        low = value.astype(BF16)
        for b in range(2):
            pbuf[i, b] = low[:, b * SUB : (b + 1) * SUB]

    def produce(u, make):
        def one(i):
            emit(u, i, make(lax.rem(1 - c + i, 2)))

            @pl.when(i == 0)
            def _():
                core_copy(u).start()

        loop(2, one)
        part_copy(u).start()

    lane = lax.broadcasted_iota(jnp.int32, (slots, 128), 1)
    rb = 128
    last_e = e_units - 1

    def cols(hf):
        return rows_at(hf, width)

    def add_small(r, v):
        v = jnp.sum(v, 0, keepdims=True)
        for hf in range(2):
            small[pl.ds(r[hf], 1), :] += v[:, hf * width : (hf + 1) * width]

    def make_r(j):
        load_h(j).wait()
        produce(j, lambda hf: mm_tn(dz_v[...], h_v[:, cols(hf)]))

        @pl.when(j < last_e)
        def _():
            load_h(j + 1).start()

    def make_dpre(j):
        wr.wait(4 + e_units + j)
        load_gp(j).wait()
        low = (mm(dz_v[...], wr_v[...]) * gp_v[...].astype(F32)).astype(BF16)
        dpre[j] = low
        add_small((4 + j, 4 + e_units + j), low.astype(F32))

        @pl.when(j < last_e)
        def _():
            wr.start(5 + e_units + j)
            load_gp(j + 1).start()

        @pl.when(j == last_e)
        def _():
            wr.start(3)

    def make_du(j):
        we.wait(4 + j)
        du[...] += mm_nt(dpre[j], we_v[...])

        @pl.when(j < last_e)
        def _():
            we.start(5 + j)

        @pl.when(j == last_e)
        def _():
            we.start(1)

    def make_e(u, j):
        produce(u, lambda hf: mm_tn(u_v[...], dpre[j, :, cols(hf)]))

    def norm(i):
        at = rows_at(i, rb)
        grad = du[at, :]
        n1 = n1_v[at, :]
        scaled = grad * vec_ref[10:11, :]
        back = r1_v[at, 0:1] * (scaled - mean(scaled) - n1 * mean(scaled * n1))
        du[at, :] = back
        low = back.astype(BF16)
        dz_v[at, :] = low
        for r, v in ((12, low.astype(F32)), (16, grad * n1), (18, grad)):
            add_small((r, r + 1), v)

    def make_o():
        for i in loads[3:6]:
            i.wait()
        loop(slots // rb, norm)
        produce(e_units, lambda hf: mm_tn(dz_v[...], o_v[:, cols(hf)]))

    def make_do():
        wr.wait(3)
        o_v[...] = mm(dz_v[...], wr_v[...]).astype(BF16)
        wr.start(0)

    def attention(p):
        at = rows_at(p, 128)
        q, k, v, do = qkv[0, :, at], qkv[1, :, at], qkv[2, :, at], o_v[:, at]
        load_p(p).wait()
        dq = dk = dv = None
        for h in range(2):
            part = lane < HD if h == 0 else lane >= HD
            qh, kh, doh = jnp.where(part, q, 0), jnp.where(part, k, 0), jnp.where(part, do, 0)
            low = p_v[lax.rem(p, 2), h]
            probs = low.astype(F32)
            dp = mm_nt(doh, v)
            ds = (probs * (dp - jnp.sum(dp * probs, -1, keepdims=True))).astype(BF16)
            tv, tk, tq = mm_tn(low, doh), mm_tn(ds, qh), mm(ds, kh)
            dv, dk, dq = (tv, tk, tq) if h == 0 else (dv + tv, dk + tk, dq + tq)
        qkv[0, :, at] = (dq * HD ** (-0.5)).astype(BF16)
        qkv[1, :, at] = (dk * HD ** (-0.5)).astype(BF16)
        qkv[2, :, at] = dv.astype(BF16)

        @pl.when(p + 2 < pairs)
        def _():
            load_p(p + 2).start()

    pairs = model // 128

    def make_w(u, i):
        produce(u, lambda hf: mm_tn(x_v[...], qkv[i, :, cols(hf)]))

    def make_dx(i, weights):
        weights.wait(i)
        du[...] += mm_nt(qkv[i], weights.buf[...])
        if i != 1:
            add_small((i, i + 1), qkv[i].astype(F32))

    def one_of(t, ticks):
        hit = t == ticks[0]
        for i in ticks[1:]:
            hit = jnp.logical_or(hit, t == i)
        return hit

    makes = {0: 0, 1: 1, 2: 2, 3: 3, 4: 4, 6: 5, 7: 6, 8: 7, 10: 8, 11: 9, 12: 10, 13: 11}

    def unit_of(t):
        return t - jnp.where(t > 4, 1, 0) - jnp.where(t > 9, 1, 0)

    def compute(t):
        @pl.when(t == 0)
        def _():
            loads[0].wait()
            loads[1].wait()

        pl.when(t < 4)(lambda: make_r(t))
        pl.when(t == 1)(lambda: loads[2].wait())
        pl.when(jnp.logical_and(t > 0, t < 5))(lambda: make_du(t - 1))
        pl.when(t < 4)(lambda: make_dpre(t))
        pl.when(t == 4)(make_o)

        @pl.when(t == 5)
        def _():
            make_do()
            for i in loads[6:]:
                i.wait()

        pl.when(jnp.logical_and(t > 4, t < 9))(lambda: loop(2, lambda i: attention(2 * (t - 5) + i)))

        @pl.when(one_of(t, (6, 7, 12, 13)))
        def _():
            make_e(unit_of(t), t - jnp.where(t > 7, 10, 6))

        @pl.when(one_of(t, (8, 10, 11)))
        def _():
            make_w(unit_of(t), t - jnp.where(t > 8, 9, 8))

        @pl.when(t == 9)
        def _():
            make_dx(0, wr)
            wr.start(2)
            make_dx(1, we)
            make_dx(2, wr)
            dz_v[...] = du[...].astype(BF16)
            act_keep(1).start()

    def loads_of(w):
        slot = lax.rem(w, 2)
        u, b = w // 2, lax.rem(w, 2)
        return [
            lcopy(part_ref.at[u, b], stage.at[slot], stage_sem.at[slot, 0]),
            lcopy(got_ref.at[u, b], gstage.at[slot], stage_sem.at[slot, 1]),
        ]

    def blk(k):
        return rows_at(s ^ k, rows)

    def blk_half(k, h):
        return pl.ds(pl.multiple_of((s ^ k) * rows + h * half, half), half)

    def near_copy(w, h, i):
        k = (1 + h, 3)[i]
        return rcopy(
            total.at[lax.rem(w, SLOTS), blk_half(k, h), :], near.at[w, h, i],
            near_send.at[w, h, i], near_recv.at[w, h, i], (s ^ (1 + h), z, c),
        )

    def far_copy(w, h):
        return rcopy(
            pair_sum.at[w, h], far.at[w, h], far_send.at[w, h], far_recv.at[w, h], (s ^ (2 - h), z, c)
        )

    def straight(w, k):
        return rcopy(
            total.at[lax.rem(w, SLOTS), blk(k), :], near.at[w, k - 1],
            near_send.at[w, k - 1], near_recv.at[w, k - 1], (s ^ k, z, c),
        )

    def sends_of(w):
        if n == 4:
            return [near_copy(w, h, i) for h in range(2) for i in range(2)]
        return [straight(w, k) for k in range(1, n)]

    def z_to(w, src, dst, i, to):
        return rcopy(src.at[w], dst.at[w], z_send.at[w, i], z_recv.at[w, i], (s, to, c))

    last = nz - 1
    edge = jnp.logical_or(z == 0, z == last)
    inner = jnp.where(z == 0, 1, nz - 2)
    outer = jnp.where(z == 1, 0, last)
    other = jnp.where(z == 1, 2, 1)

    def s0(w):
        @pl.when(lax.rem(w, 2) == 0)
        def _():
            core_in(w // 2).wait_recv()

        for i in loads_of(w):
            i.start()

    def s1(w):
        @pl.when(w >= SLOTS)
        def _():
            for i in sends_of(w - SLOTS):
                i.wait_send()

        for i in loads_of(w):
            i.wait()
        slot, to = lax.rem(w, 2), lax.rem(w, SLOTS)

        def add(i):
            at = rows_at(i, 256)
            total[to, at, :] = (stage[slot, at, :].astype(F32) + gstage[slot, at, :].astype(F32)).astype(BF16)

        loop(model // 256, add)
        for i in sends_of(w):
            i.start()

    def s2(w):
        slot = lax.rem(w, SLOTS)
        for i in sends_of(w):
            i.wait_recv()
        if n == 4:
            for h in range(2):
                pair_sum[w, h] = (
                    total[slot, blk_half(2 - h, h), :].astype(F32) + near[w, h, 1].astype(F32)
                ).astype(BF16)
                far_copy(w, h).start()

    def s3(w):
        slot = lax.rem(w, SLOTS)
        if n == 4:
            for h in range(2):
                far_copy(w, h).wait_recv()
                block_out[w, h * half : (h + 1) * half] = (
                    total[slot, blk_half(0, h), :].astype(F32) + near[w, h, 0].astype(F32) + far[w, h].astype(F32)
                ).astype(BF16)
        else:
            acc = total[slot, blk(0), :].astype(F32)
            for k in range(1, n):
                acc = acc + near[w, k - 1].astype(F32)
            block_out[w] = acc.astype(BF16)

        @pl.when(edge)
        def _():
            z_to(w, block_out, up, 0, inner).start()

    def s4(w):
        @pl.when(jnp.logical_not(edge))
        def _():
            z_to(w, block_out, up, 0, outer).wait_recv()
            block_out[w] = (block_out[w].astype(F32) + up[w].astype(F32)).astype(BF16)
            z_to(w, block_out, across, 1, other).start()

    def s5(w):
        @pl.when(jnp.logical_not(edge))
        def _():
            z_to(w, block_out, across, 1, other).wait_recv()
            down[w] = (block_out[w].astype(F32) + across[w].astype(F32)).astype(BF16)
            z_to(w, down, down, 2, outer).start()

    def s6(w):
        @pl.when(edge)
        def _():
            z_to(w, down, down, 2, inner).wait_recv()

        lcopy(down.at[w], grad_ref.at[w], store_sem.at[w]).start()

    stages = list(zip(LAGS, (s0, s3, s2, s1, s6, s5, s4)))

    def serve(w):
        for lag, stage_of in stages:
            @pl.when(jnp.logical_and(w >= lag, w - lag < subs))
            def _(stage_of=stage_of, lag=lag):
                stage_of(w - lag)

    hops = [(s, z, 1 - c)]
    hops += [(s ^ (1 << b), z, c) for b in range(n.bit_length() - 1)]
    hops += [(s, z ^ (1 << b), c) for b in range(nz.bit_length() - 1)]

    def small_copy(i):
        return rcopy(small, round_in.at[i], small_send.at[i], small_recv.at[i], hops[i])

    done = max(makes) + 2

    def served(t):
        return jnp.clip(2 * (t - 1), 0, 4) + jnp.maximum(PACE * (t - 3) // 4, 0)

    def step(t):
        pl.when(one_of(t, [i + 1 for i in makes]))(lambda: settle(unit_of(t - 1)))

        lax.fori_loop(served(t), served(t + 1), lambda w, carry: (serve(w), carry)[1], 0)
        pl.when(t <= max(makes))(lambda: compute(t))

        for which, first in enumerate(ACTS):
            pl.when(jnp.logical_and(t >= first, t < first + PIECES))(lambda: act_some(which, t - first))

        @pl.when(t == PIECES)
        def _():
            act_pass(0)

        @pl.when(t == PASS)
        def _():
            act_pass(1)

        for i in range(len(hops) + 1):
            @pl.when(t == done + i)
            def _(i=i):
                if i > 0:
                    small_copy(i - 1).wait_send()
                    small_copy(i - 1).wait_recv()
                    small[...] += round_in[i - 1]
                if i < len(hops):
                    small_copy(i).start()
                else:
                    lcopy(small, small_out, keep_sem.at[2]).start()

    ticks = (4 * (subs + max(LAGS) - 4) + PACE - 1) // PACE + 3
    loop(ticks, step)

    def finish(w):
        if n == 4:
            for h in range(2):
                far_copy(w, h).wait_send()

        @pl.when(edge)
        def _():
            z_to(w, block_out, up, 0, inner).wait_send()

        @pl.when(jnp.logical_not(edge))
        def _():
            z_to(w, block_out, across, 1, other).wait_send()
            z_to(w, down, down, 2, outer).wait_send()

        lcopy(down.at[w], grad_ref.at[w], store_sem.at[w]).wait()

    loop(subs, finish)
    for w in range(subs - SLOTS, subs):
        for i in sends_of(w):
            i.wait_send()
    for which in range(2):
        for k in range(1, nz):
            loop(PIECES, lambda i: act(which, k, i).wait_send())
        for k in range(nz):
            pass_copy(which, k).wait_send()
            pass_in(which, k).wait_recv()
    lcopy(small, small_out, keep_sem.at[2]).wait()


def backward(n, nz, full, x, q, k, v, o, p, n1, r1, u, h, gp, ds, dz, y, vec, small):
    _, units, model, width = full.shape
    e_units = h.shape[0]
    rows = model // n
    half = rows // 2
    slots = x.shape[0]
    block = slots // nz
    subs = 2 * units
    near = (subs, 2, 2, half, SUB) if n == 4 else (subs, n - 1, rows, SUB)
    near_sems = near[:3] if n == 4 else near[:2]
    far = (subs, 2, half, SUB) if n == 4 else (1, 2, 16, SUB)
    blocks = (subs, rows, SUB)
    hops = 1 + (n.bit_length() - 1) + (nz.bit_length() - 1)
    outs = [
        (blocks, BF16), ((2 * nz, block, model), BF16), ((2 * nz, block, model), BF16), ((24, UNIT), F32),
        ((units, 2, model, SUB), BF16), ((units, 2, model, SUB), BF16),
    ]
    scratch = [
        ((slots, model), BF16), ((3, slots, model), BF16), ((slots, model), BF16), ((2, 2, slots, slots), BF16),
        ((slots, model), F32), ((slots, 128), F32), ((slots, model), BF16), ((slots, model), BF16),
        ((slots, model), F32), ((model, 2 * UNIT), BF16), ((model, 2 * UNIT), BF16), ((slots, model), BF16),
        ((slots, model), BF16), ((e_units, slots, model), BF16), ((2, 2, model, SUB), BF16), ((24, UNIT), F32),
        ((hops, 24, UNIT), F32),
        ((2, model, SUB), BF16), ((2, model, SUB), BF16), ((SLOTS, model, SUB), BF16),
        (near, BF16), (far, BF16), (far, BF16), (blocks, BF16), (blocks, BF16), (blocks, BF16), (blocks, BF16),
    ]
    return pl.pallas_call(
        functools.partial(backward_kernel, n, nz),
        name="backward_and_reduce",
        out_shape=[jax.ShapeDtypeStruct(a, b) for a, b in outs],
        in_specs=[ANY] * 15 + [VMEM, ANY],
        out_specs=[ANY] * len(outs),
        scratch_shapes=[pltpu.VMEM(a, b) for a, b in scratch]
        + [
            DMA((12,)), DMA((3, 2)), DMA((2,)), DMA((1,)), DMA((units,)), DMA((units,)), DMA((2, 2)),
            DMA(near_sems), DMA(near_sems), DMA((subs, 2)), DMA((subs, 2)),
            DMA((subs, 3)), DMA((subs, 3)), DMA((subs,)),
            DMA((2, nz, PIECES)), DMA((2, nz, PIECES)), DMA((2, nz)), DMA((2, nz)), DMA((3,)), DMA((hops,)), DMA((hops,)),
        ],
        compiler_params=pltpu.CompilerParams(
            collective_id=1, has_side_effects=True, vmem_limit_bytes=61 * 2**20
        ),
    )(full, x, q, k, v, o, p, n1, r1, u, h, gp, ds, dz, y, vec, small)


def finish_kernel(
    n, grad_ref, ys_ref, dx_ref, small_ref,
    y_out, dx_out, dq_out, dk_out, dv_out, do_out, de_out, dr_out,
    qb_out, vb_out, eb_out, ob_out, rb_out, g1_out, s1_out, g2_out, s2_out,
    grads, act, act_wide, dq, dk, dv, do, de, dr, in_sem, out_sem, act_in, act_out,
):
    s, _, c = place()
    rows = dq.shape[0]
    seqs = act.shape[1]
    e_units = de.shape[1] // UNIT
    he = HD // n
    load = lcopy(grad_ref, grads, in_sem)
    load.start()

    def act_load(i, which):
        return lcopy((ys_ref, dx_ref)[which].at[i], act.at[which, i], act_in.at[which, i])

    def act_store(i, which):
        return lcopy(act_wide.at[which, i], (y_out, dx_out)[which].at[i], act_out.at[which, i])

    for which in range(2):
        loop(seqs, lambda i: act_load(i, which).start())
    load.wait()
    stores = []

    def store(src, dst):
        stores.append(lcopy(src, dst, out_sem.at[len(stores)]))
        stores[-1].start()

    def part(u, b):
        return grads[2 * u + b].astype(F32)

    spots = [e_units + 1, e_units + 2, e_units + 6, e_units + 7]
    for j in range(e_units):
        for b in range(2):
            at = j * UNIT + b * SUB
            dr[at : at + SUB, :] = part(j, b).T
            de[:, at : at + SUB] = part(spots[j], b)
    store(dr, dr_out)
    store(de, de_out)
    for i, (v, out) in enumerate(((dq, dq_out), (dk, dk_out), (dv, dv_out))):
        for b in range(2):
            v[:, b * SUB : (b + 1) * SUB] = part(e_units + 3 + i, b)
        store(v, out)
    for b in range(2):
        do[b * SUB : (b + 1) * SUB, :] = part(e_units, b).T
    store(do, do_out)
    for which in range(2):
        def widen(i):
            act_load(i, which).wait()
            act_wide[which, i] = act[which, i].astype(F32)
            act_store(i, which).start()

        loop(seqs, widen)

    at = lax.rem(UNIT - s * he, UNIT)
    turned = pltpu.roll(small_ref[...], at, 1)
    for out, base, count in ((qb_out, 0, 1), (vb_out, 2, 1), (eb_out, 4, e_units)):
        for i in range(count):
            line = jnp.where(c == 0, turned[base + i : base + i + 1, :], turned[base + count + i : base + count + i + 1, :])
            for h in range(8):
                out[8 * i + h : 8 * i + h + 1, :] = line[:, h * HD : h * HD + he]
    at = lax.rem(UNIT - lax.rem(s * rows, UNIT), UNIT)
    turned = pltpu.roll(small_ref[...], at, 1)
    late = s * rows >= UNIT
    for i, out in enumerate((ob_out, rb_out, g1_out, s1_out, g2_out, s2_out)):
        r = 4 + 2 * e_units + 2 * i
        line = jnp.where(late, turned[r + 1 : r + 2, :], turned[r : r + 1, :])
        out[...] = line[:, :rows].reshape(rows)
    for i in stores:
        i.wait()
    for which in range(2):
        loop(seqs, lambda i: act_store(i, which).wait())


def finish(n, grads, ys, dx, small, heads):
    _, rows, _ = grads.shape
    seqs, block, model = ys.shape
    wide = heads[2].shape[0] // 8 * UNIT
    square, tall = (rows, UNIT), (UNIT, rows)
    outs = [ys.shape, ys.shape, square, square, square, tall, (rows, wide), (wide, rows)]
    small_outs = [v.shape for v in heads] + [(rows,)] * 6
    return pl.pallas_call(
        functools.partial(finish_kernel, n),
        name="widen_results",
        out_shape=[jax.ShapeDtypeStruct(a, F32) for a in outs + small_outs],
        in_specs=[ANY] * 3 + [VMEM],
        out_specs=[ANY] * len(outs) + [VMEM] * len(small_outs),
        scratch_shapes=[pltpu.VMEM(grads.shape, BF16), pltpu.VMEM((2, *ys.shape), BF16), pltpu.VMEM((2, *ys.shape), F32)]
        + [pltpu.VMEM(a, F32) for a in outs[2:]]
        + [DMA, DMA((6,)), DMA((2, seqs)), DMA((2, seqs))],
        compiler_params=pltpu.CompilerParams(vmem_limit_bytes=61 * 2**20),
    )(grads, ys, dx, small)


def body(n, nz, inputs, lengths, wq, wk, wv, wo, we, wr, qb, vb, eb, ob, rb, g1, s1, g2, s2, cotangent):
    heads = (qb, vb, eb)
    (full, x, q, k, v, o, p, n1, r1, u, h, gp, ds, dz, y, vec, small) = forward(
        n, nz, lengths, inputs, cotangent, wq, wk, wv, wo, we, wr, heads, (ob, rb, g1, s1, g2, s2)
    )
    grads, ys, dx, small, _, _ = backward(
        n, nz, full, x, q, k, v, o, p, n1, r1, u, h, gp, ds, dz, y, vec, small
    )
    return tuple(finish(n, grads, ys, dx, small, heads))


def solution(mesh):
    w, wt, v = P("shard", "tp"), P("tp", "shard"), P("shard")
    rows = P("shard", "ctx", None)
    return jax.shard_map(
        functools.partial(body, mesh.shape["shard"], mesh.shape["ctx"]),
        mesh=mesh,
        in_specs=(rows, v, w, w, w, wt, w, wt, wt, wt, wt, v, v, v, v, v, v, rows),
        out_specs=(rows, rows, w, w, w, wt, w, wt, wt, wt, wt, v, v, v, v, v, v),
        check_vma=False,
    )
```

time: 344 us -> 299 us (0.87)
  local copies, waits for them, and re-layouts: 23 us -> 2.75 us
  Pallas kernels: 311 us -> 295 us
  other arithmetic: 8.78 us -> 0 us
    pallas_call x1, Pallas kernels: 184 us -> 156 us  [backward(): pl.pallas_call(functools.partial(backward_kernel, n, nz), name='backward_...]
    unnamed x17 -> x1, local copies, waits for them, and re-layouts: 10.6 us -> 1.36 us
    pallas_call x0 -> x1, Pallas kernels: none -> 9.18 us  [finish(): pl.pallas_call(functools.partial(finish_kernel, n), name='widen_results',...]
    convert_element_type x4 -> x0, other arithmetic: 7.62 us -> none  [the longest x2 2.66 us: joined(): return jnp.concatenate([grads[i] for i in picks], 1).astype(F32)]
    reshape x12 -> x0, local copies, waits for them, and re-layouts: 5.9 us -> none  [the longest x9 5.58 us: lines(): v = v.reshape(count, -1)]
where the time goes in v3:
time: 299 us; the launch traced here: 298 us
  Pallas kernels  295 us (99%)
    pallas_call x1, Pallas kernels, backward(): pl.pallas_call(functools.partial(backward_kernel, n, nz), name='backward_...  156 us
    pallas_call x1, Pallas kernels, forward(): pl.pallas_call(functools.partial(forward_kernel, n, nz), name='gather_and...  129 us
    pallas_call x1, Pallas kernels, finish(): pl.pallas_call(functools.partial(finish_kernel, n), name='widen_results',...  9.18 us

profile of v3, /device:TPU:0, one launch (start us, length us, event | category | flops | bytes accessed | tf_op | source)
XLA Modules:
  0.0 298.0 jit_solution(10090058211891303828)
XLA Ops:
  0.7 1.4 copy.35.eb_ref
  2.0 129.1 %gather_and_forward.1 = (bf16[2,12,1024,512]{3,2,1,0:T(8,128)(2,1)}, bf16[512,1024]{1,0:T(8,128)(2,1)}, bf16[512,1024]{1,0:T(8,128)(2,1)}, bf16[512,1024]{1,0:T(...) custom-call(s32[8]{0:T(128)} %len_ref.1, ...), custom_call_target="tpu_custom_call" | custom-call | tf_op jit(solution)/shard_map/gather_and_forward/pallas_call | solution.py:482
  131.1 156.3 %backward_and_reduce.1 = (bf16[24,256,256]{2,1,0:T(8,128)(2,1)}, bf16[8,128,1024]{2,1,0:T(8,128)(2,1)}, bf16[8,128,1024]{2,1,0:T(8,128)(2,1)}, f32[24,512]{1,0:T...) custom-call(bf16[2,12,1024,512]{3,2,1,0:T(8,128)(2,1)} %get-tuple-element.38.full_ref, ...), custom_call_target="tpu_custom_call" | custom-call | tf_op jit(solution)/shard_map/backward_and_reduce/pallas_call | solution.py:1023
  287.4 9.2 %widen_results.1 = (f32[8,128,1024]{2,1,0:T(8,128)}, f32[8,128,1024]{2,1,0:T(8,128)}, f32[256,512]{1,0:T(8,128)}, f32[256,512]{1,0:T(8,128)}, f32[256,512]{1,0:T...) custom-call(bf16[24,256,256]{2,1,0:T(8,128)(2,1)} %get-tuple-element, ...), custom_call_target="tpu_custom_call" | custom-call | tf_op jit(solution)/shard_map/widen_results/pallas_call | solution.py:1124
  296.6 1.4 copy.36

commit v4 on v3

--- a/solution.py
+++ b/solution.py
@@ -13,7 +13,7 @@
 SLOTS = 4
 LAGS = (0, 5, 3, 1, 11, 9, 7)
 PACE = 5
-PASS = 24
+PASS = 22
 PIECES = 8
 ACTS = (0, 10)
 EPSILON = 1e-05
@@ -84,7 +84,7 @@
     ds_out, dz_out, y_out, vec_out, small_out,
     own, wo_in, wr_in, xin, act_low, xv, cotv, qkv, o_v, p_v, n1_v, r1_v, u_v, ulow_v, h_v, gp_v, acc,
     dz_v, y_v, wbuf, pk_ref, pk_wide, pkall, head_bias, bias, vec, small,
-    own_send, own_recv, fwd_send, fwd_recv, core_send, core_recv, act_send, act_recv,
+    own_send, own_recv, fwd_send, fwd_recv, core_send, core_recv, z_send, z_recv, act_send, act_recv,
     pk_send, pk_recv, in_sem, act_sem, fetch_sem, out_sem, p_sem,
 ):
     s, z, c = place()
@@ -112,25 +112,38 @@
         src = (x_ref, g_ref)[which]
         return lcopy(src.at[2 * to(k) + c], xin.at[k], act_sem.at[k])
 
-    def act(which, k):
+    some = block // PIECES
+
+    def act(which, k, i):
         dst = (xv, cotv)[which]
+        at = pl.ds(pl.multiple_of(z * block + i * some, some), some)
         return rcopy(
-            act_low.at[which, k], dst.at[zrows, :], act_send.at[which, k], act_recv.at[which, k], (s, to(k), c)
+            act_low.at[which, k, rows_at(i, some), :], dst.at[at, :],
+            act_send.at[which, k, i], act_recv.at[which, k, i], (s, to(k), c),
         )
 
-    def act_in(which, k):
+    def act_in(which, k, i):
         dst = (xv, cotv)[which]
         src = lax.rem(z + nz - k, nz)
-        at = dst.at[rows_at(src, block), :]
-        return rcopy(at, at, act_send.at[which, k], act_recv.at[which, k], (s, src, c))
-
-    def act_share(which):
+        at = dst.at[pl.ds(pl.multiple_of(src * block + i * some, some), some), :]
+        return rcopy(at, at, act_send.at[which, k, i], act_recv.at[which, k, i], (s, src, c))
+
+    def act_some(which, i):
+        for k in range(1, nz):
+            act(which, k, i).start()
+
+    def act_share(which, send):
         for k in range(1, nz):
             act_load(which, k).wait()
             act_low[which, k] = xin[k].astype(BF16)
-            act(which, k).start()
+            if send:
+                loop(PIECES, lambda i: act(which, k, i).start())
         act_load(which, 0).wait()
         (xv, cotv)[which][zrows, :] = xin[0].astype(BF16)
+
+    def act_arrive(which):
+        for k in range(1, nz):
+            loop(PIECES, lambda i: act_in(which, k, i).wait_recv())
 
     for k in range(1, nz):
         act_load(0, k).start()
@@ -197,13 +210,30 @@
         at = full_ref.at[1 - c, u, rows_at(s ^ k, rows), :]
         return rcopy(at, at, core_send.at[u, k], core_recv.at[u, k], (s, z, 1 - c))
 
-    ahead = 2
+    par = lax.rem(z, 2)
+    slots_of_units = units - 2
+
+    def unit_at(i):
+        u = jnp.where(i < 3, i, jnp.where(i == 3, 4 + par, jnp.where(i == 4, 3, 8 + par)))
+        return jnp.where(i > 5, jnp.where(i < 8, i, i + 2), u)
+
+    def theirs_at(i):
+        return jnp.where(i == 3, 5 - par, 9 - par)
+
+    def z_copy(u, k):
+        at = full_ref.at[c, u, rows_at(s ^ k, rows), :]
+        return rcopy(at, at, z_send.at[u, k], z_recv.at[u, k], (s, z + 1 - 2 * par, c))
+
+    def is_paired(i):
+        return jnp.logical_or(i == 3, i == 5)
+
+    ahead = 1
     for i in ins[:ahead]:
         i.wait()
     for u in range(ahead):
         for k in direct:
             own_copy(u, k).start()
-    act_share(0)
+    act_share(0, True)
     for k in range(nz):
         act_load(1, k).start()
     for i in ins[ahead:]:
@@ -224,7 +254,7 @@
     share.start()
     theirs = full_ref.at[1 - c, :, mine, :]
     share_in = rcopy(theirs, theirs, core_send.at[units, 0], core_recv.at[units, 0], (s, z, 1 - c))
-    act_share(1)
+    act_share(1, False)
 
     for k, j in pk_pairs:
         pk_in(k, j).wait_recv()
@@ -308,21 +338,15 @@
 
         @pl.when(u == 0)
         def _():
-            for k in range(1, nz):
-                act_in(0, k).wait_recv()
+            act_arrive(0)
 
         @pl.when(u < 3)
         def _():
             add = jnp.where(u == 0, bias[0:1, :], jnp.where(u == 2, bias[1:2, :], 0.0))
             qkv[u] = (mm(xv[...], w[...]) + add).astype(BF16)
 
-        @pl.when(u == 2)
-        def _():
-            loop(pairs // 2, attention)
-
         @pl.when(u == 3)
         def _():
-            loop(pairs // 2, lambda p: attention(p + pairs // 2))
             acc[...] = mm_nt(o_v[...], w[...]) + xv[...].astype(F32)
 
             def norm(i):
@@ -360,13 +384,15 @@
         def _():
             u_v[...] += mm_nt(h_v[u - 4 - e_units], w[...])
 
-    def step(u):
-        @pl.when(u < units)
-        def _():
-            @pl.when(u + ahead < units)
+    def exchange(t):
+        @pl.when(t < slots_of_units)
+        def _():
+            u = unit_at(t)
+
+            @pl.when(t + ahead < slots_of_units)
             def _():
                 for k in direct:
-                    own_copy(u + ahead, k).start()
+                    own_copy(unit_at(t + ahead), k).start()
 
             for k in direct:
                 own_in(u, k).wait_recv()
@@ -374,29 +400,66 @@
                     fwd_copy(u, 2 - k).start()
                 core_copy(u, k).start()
 
+                @pl.when(is_paired(t))
+                def _():
+                    z_copy(u, k).start()
+
         if n == 4:
-            @pl.when(jnp.logical_and(u > 0, u <= units))
+            @pl.when(jnp.logical_and(t > 0, t <= slots_of_units))
             def _():
+                u = unit_at(t - 1)
                 for h in range(2):
-                    fwd_in(u - 1, h).wait_recv()
-                core_copy(u - 1, 3).start()
-
-        @pl.when(u >= 2)
-        def _():
-            for i in fetch(u - 2):
+                    fwd_in(u, h).wait_recv()
+                core_copy(u, 3).start()
+
+                @pl.when(is_paired(t - 1))
+                def _():
+                    z_copy(u, 3).start()
+
+        for late, ks in ((2, [k for k in range(1, n) if n != 4 or k < 3]), (3, [3] if n == 4 else [])):
+            @pl.when(is_paired(t - late))
+            def _(late=late, ks=ks):
+                u = theirs_at(t - late)
+                for k in ks:
+                    z_copy(u, k).wait_recv()
+                    core_copy(u, k).start()
+
+        @pl.when(jnp.logical_and(t >= 1, t <= PIECES))
+        def _():
+            act_some(1, t - 1)
+
+    def first_at(t):
+        u = jnp.clip(t - 2, 0, 3)
+        for late in (6, 7, 7, 8, 8, 9, 9, 9, 10):
+            u = u + jnp.where(t > late, 1, 0)
+        return u
+
+    def start_fetch(u):
+        ready(u)
+        for i in fetch(u):
+            i.start()
+
+    def step(t):
+        exchange(t)
+        first, after = first_at(t), first_at(t + 1)
+        pl.when(t == slots_of_units)(lambda: start_fetch(units - 1))
+
+        def one(u, carry):
+            for i in fetch(u):
                 i.wait()
-            compute(u - 2)
-
-        @pl.when(jnp.logical_and(u > 0, u <= units))
-        def _():
-            ready(u - 1)
-            for i in fetch(u - 1):
-                i.start()
-
-    loop(units + 2, step)
-
-    for k in range(1, nz):
-        act_in(1, k).wait_recv()
+            pl.when(u + 1 < after)(lambda: start_fetch(u + 1))
+            compute(u)
+            return carry
+
+        lax.fori_loop(first, after, one, 0)
+        pl.when(jnp.logical_or(t == 4, t == 5))(
+            lambda: loop(pairs // 2, lambda p: attention(p + (t - 4) * (pairs // 2)))
+        )
+        pl.when(jnp.logical_and(first_at(t + 2) > after, t + 1 < slots_of_units))(lambda: start_fetch(after))
+
+    loop(slots_of_units + 1, step)
+
+    act_arrive(1)
 
     def norm2(i):
         at = rows_at(i, rb)
@@ -426,22 +489,32 @@
     for i in last:
         i.start()
 
-    def finish(u):
+    def sent(t):
+        u = unit_at(t)
         for k in direct:
             own_copy(u, k).wait_send()
         if n == 4:
             for h in range(2):
                 fwd_copy(u, h).wait_send()
+
+        @pl.when(is_paired(t))
+        def _():
+            for k in range(1, n):
+                z_copy(u, k).wait_send()
+
+    loop(slots_of_units, sent)
+
+    def passed(u):
         for k in range(1, n):
             core_copy(u, k).wait_send()
 
-    loop(units, finish)
+    loop(units, passed)
     share.wait_send()
     for k, j in pk_pairs:
         pk_copy(k, j).wait_send()
     for which in range(2):
         for k in range(1, nz):
-            act(which, k).wait_send()
+            loop(PIECES, lambda i: act(which, k, i).wait_send())
     vec_copy.wait()
     for p in (pairs - 2, pairs - 1):
         p_copy(p).wait()
@@ -488,7 +561,8 @@
         scratch_shapes=[pltpu.VMEM(a, b) for a, b in scratch]
         + [
             DMA((units, n)), DMA((units, n)), DMA((units, 2)), DMA((units, 2)),
-            DMA((units + 1, n)), DMA((units + 1, n)), DMA((2, nz)), DMA((2, nz)),
+            DMA((units + 1, n)), DMA((units + 1, n)), DMA((units, n)), DMA((units, n)),
+            DMA((2, nz, PIECES)), DMA((2, nz, PIECES)),
             DMA((n, 2)), DMA((n, 2)), DMA((6 + e_units,)), DMA((nz,)), DMA((2, 2)), DMA((16,)), DMA((2,)),
         ],
         compiler_params=pltpu.CompilerParams(
@@ -614,18 +688,16 @@
         return rcopy(got_ref.at[u], got_ref.at[u], core_send.at[u], core_recv.at[u], (s, z, 1 - c))
 
     def part_copy(u):
-        return lcopy(pbuf.at[1], part_ref.at[u], part_sem.at[0])
-
-    def settle(u):
-        core_copy(u).wait_send()
-        part_copy(u).wait()
+        return lcopy(pbuf.at[1 + lax.rem(u, 3)], part_ref.at[u], part_sem.at[lax.rem(u, 3)])
 
     def emit(u, i, value):
         low = value.astype(BF16)
         for b in range(2):
-            pbuf[i, b] = low[:, b * SUB : (b + 1) * SUB]
+            pbuf[jnp.where(i == 0, 0, 1 + lax.rem(u, 3)), b] = low[:, b * SUB : (b + 1) * SUB]
 
     def produce(u, make):
+        pl.when(u > 0)(lambda: core_copy(u - 1).wait_send())
+
         def one(i):
             emit(u, i, make(lax.rem(1 - c + i, 2)))
 
@@ -828,8 +900,9 @@
             return [near_copy(w, h, i) for h in range(2) for i in range(2)]
         return [straight(w, k) for k in range(1, n)]
 
-    def z_to(w, src, dst, i, to):
-        return rcopy(src.at[w], dst.at[w], z_send.at[w, i], z_recv.at[w, i], (s, to, c))
+    def z_to(w, h, src, dst, i, to):
+        at = pl.ds(h * half, half)
+        return rcopy(src.at[w, at], dst.at[w, at], z_send.at[w, i, h], z_recv.at[w, i, h], (s, to, c))
 
     last = nz - 1
     edge = jnp.logical_or(z == 0, z == last)
@@ -840,6 +913,7 @@
     def s0(w):
         @pl.when(lax.rem(w, 2) == 0)
         def _():
+            part_copy(w // 2).wait()
             core_in(w // 2).wait_recv()
 
         for i in loads_of(w):
@@ -876,40 +950,42 @@
 
     def s3(w):
         slot = lax.rem(w, SLOTS)
-        if n == 4:
-            for h in range(2):
+        if n != 4:
+            acc = total[slot, blk(0), :].astype(F32)
+            for k in range(1, n):
+                acc = acc + near[w, k - 1].astype(F32)
+            block_out[w] = acc.astype(BF16)
+        for h in range(2):
+            if n == 4:
                 far_copy(w, h).wait_recv()
                 block_out[w, h * half : (h + 1) * half] = (
                     total[slot, blk_half(0, h), :].astype(F32) + near[w, h, 0].astype(F32) + far[w, h].astype(F32)
                 ).astype(BF16)
-        else:
-            acc = total[slot, blk(0), :].astype(F32)
-            for k in range(1, n):
-                acc = acc + near[w, k - 1].astype(F32)
-            block_out[w] = acc.astype(BF16)
-
-        @pl.when(edge)
-        def _():
-            z_to(w, block_out, up, 0, inner).start()
+            pl.when(edge)(lambda: z_to(w, h, block_out, up, 0, inner).start())
 
     def s4(w):
         @pl.when(jnp.logical_not(edge))
         def _():
-            z_to(w, block_out, up, 0, outer).wait_recv()
-            block_out[w] = (block_out[w].astype(F32) + up[w].astype(F32)).astype(BF16)
-            z_to(w, block_out, across, 1, other).start()
+            for h in range(2):
+                at = pl.ds(h * half, half)
+                z_to(w, h, block_out, up, 0, outer).wait_recv()
+                block_out[w, at] = (block_out[w, at].astype(F32) + up[w, at].astype(F32)).astype(BF16)
+                z_to(w, h, block_out, across, 1, other).start()
 
     def s5(w):
         @pl.when(jnp.logical_not(edge))
         def _():
-            z_to(w, block_out, across, 1, other).wait_recv()
-            down[w] = (block_out[w].astype(F32) + across[w].astype(F32)).astype(BF16)
-            z_to(w, down, down, 2, outer).start()
+            for h in range(2):
+                at = pl.ds(h * half, half)
+                z_to(w, h, block_out, across, 1, other).wait_recv()
+                down[w, at] = (block_out[w, at].astype(F32) + across[w, at].astype(F32)).astype(BF16)
+                z_to(w, h, down, down, 2, outer).start()
 
     def s6(w):
         @pl.when(edge)
         def _():
-            z_to(w, down, down, 2, inner).wait_recv()
+            for h in range(2):
+                z_to(w, h, down, down, 2, inner).wait_recv()
 
         lcopy(down.at[w], grad_ref.at[w], store_sem.at[w]).start()
 
@@ -934,8 +1010,6 @@
         return jnp.clip(2 * (t - 1), 0, 4) + jnp.maximum(PACE * (t - 3) // 4, 0)
 
     def step(t):
-        pl.when(one_of(t, [i + 1 for i in makes]))(lambda: settle(unit_of(t - 1)))
-
         lax.fori_loop(served(t), served(t + 1), lambda w, carry: (serve(w), carry)[1], 0)
         pl.when(t <= max(makes))(lambda: compute(t))
 
@@ -970,18 +1044,18 @@
             for h in range(2):
                 far_copy(w, h).wait_send()
 
-        @pl.when(edge)
-        def _():
-            z_to(w, block_out, up, 0, inner).wait_send()
-
-        @pl.when(jnp.logical_not(edge))
-        def _():
-            z_to(w, block_out, across, 1, other).wait_send()
-            z_to(w, down, down, 2, outer).wait_send()
+        for h in range(2):
+            pl.when(edge)(lambda: z_to(w, h, block_out, up, 0, inner).wait_send())
+
+            @pl.when(jnp.logical_not(edge))
+            def _():
+                z_to(w, h, block_out, across, 1, other).wait_send()
+                z_to(w, h, down, down, 2, outer).wait_send()
 
         lcopy(down.at[w], grad_ref.at[w], store_sem.at[w]).wait()
 
     loop(subs, finish)
+    core_copy(units - 1).wait_send()
     for w in range(subs - SLOTS, subs):
         for i in sends_of(w):
             i.wait_send()
@@ -1015,7 +1089,7 @@
         ((slots, model), BF16), ((3, slots, model), BF16), ((slots, model), BF16), ((2, 2, slots, slots), BF16),
         ((slots, model), F32), ((slots, 128), F32), ((slots, model), BF16), ((slots, model), BF16),
         ((slots, model), F32), ((model, 2 * UNIT), BF16), ((model, 2 * UNIT), BF16), ((slots, model), BF16),
-        ((slots, model), BF16), ((e_units, slots, model), BF16), ((2, 2, model, SUB), BF16), ((24, UNIT), F32),
+        ((slots, model), BF16), ((e_units, slots, model), BF16), ((4, 2, model, SUB), BF16), ((24, UNIT), F32),
         ((hops, 24, UNIT), F32),
         ((2, model, SUB), BF16), ((2, model, SUB), BF16), ((SLOTS, model, SUB), BF16),
         (near, BF16), (far, BF16), (far, BF16), (blocks, BF16), (blocks, BF16), (blocks, BF16), (blocks, BF16),
@@ -1028,9 +1102,9 @@
         out_specs=[ANY] * len(outs),
         scratch_shapes=[pltpu.VMEM(a, b) for a, b in scratch]
         + [
-            DMA((12,)), DMA((3, 2)), DMA((2,)), DMA((1,)), DMA((units,)), DMA((units,)), DMA((2, 2)),
+            DMA((12,)), DMA((3, 2)), DMA((2,)), DMA((3,)), DMA((units,)), DMA((units,)), DMA((2, 2)),
             DMA(near_sems), DMA(near_sems), DMA((subs, 2)), DMA((subs, 2)),
-            DMA((subs, 3)), DMA((subs, 3)), DMA((subs,)),
+            DMA((subs, 3, 2)), DMA((subs, 3, 2)), DMA((subs,)),
             DMA((2, nz, PIECES)), DMA((2, nz, PIECES)), DMA((2, nz)), DMA((2, nz)), DMA((3,)), DMA((hops,)), DMA((hops,)),
         ],
         compiler_params=pltpu.CompilerParams(

time: 299 us -> 278 us (0.930)
  Pallas kernels: 295 us -> 274 us
    pallas_call x1, Pallas kernels: 129 us -> 115 us  [forward(): pl.pallas_call(functools.partial(forward_kernel, n, nz), name='gather_and...]
    pallas_call x1, Pallas kernels: 156 us -> 150 us  [backward(): pl.pallas_call(functools.partial(backward_kernel, n, nz), name='backward_...]
where the time goes in v4:
time: 278 us; the launch traced here: 277 us
  Pallas kernels  274 us (99%)
    pallas_call x1, Pallas kernels, backward(): pl.pallas_call(functools.partial(backward_kernel, n, nz), name='backward_...  150 us
    pallas_call x1, Pallas kernels, forward(): pl.pallas_call(functools.partial(forward_kernel, n, nz), name='gather_and...  115 us
    pallas_call x1, Pallas kernels, finish(): pl.pallas_call(functools.partial(finish_kernel, n), name='widen_results',...  9.18 us

profile of v4, /device:TPU:0, one launch (start us, length us, event | category | flops | bytes accessed | tf_op | source)
XLA Modules:
  0.0 277.2 jit_solution(11455125828493584739)
XLA Ops:
  0.7 1.4 copy.35.eb_ref
  2.0 114.6 %gather_and_forward.1 = (bf16[2,12,1024,512]{3,2,1,0:T(8,128)(2,1)}, bf16[512,1024]{1,0:T(8,128)(2,1)}, bf16[512,1024]{1,0:T(8,128)(2,1)}, bf16[512,1024]{1,0:T(...) custom-call(s32[8]{0:T(128)} %len_ref.1, ...), custom_call_target="tpu_custom_call" | custom-call | tf_op jit(solution)/shard_map/gather_and_forward/pallas_call | solution.py:555
  116.6 150.1 %backward_and_reduce.1 = (bf16[24,256,256]{2,1,0:T(8,128)(2,1)}, bf16[8,128,1024]{2,1,0:T(8,128)(2,1)}, bf16[8,128,1024]{2,1,0:T(8,128)(2,1)}, f32[24,512]{1,0:T...) custom-call(bf16[2,12,1024,512]{3,2,1,0:T(8,128)(2,1)} %get-tuple-element.38.full_ref, ...), custom_call_target="tpu_custom_call" | custom-call | tf_op jit(solution)/shard_map/backward_and_reduce/pallas_call | solution.py:1097
  266.7 9.2 %widen_results.1 = (f32[8,128,1024]{2,1,0:T(8,128)}, f32[8,128,1024]{2,1,0:T(8,128)}, f32[256,512]{1,0:T(8,128)}, f32[256,512]{1,0:T(8,128)}, f32[256,512]{1,0:T...) custom-call(bf16[24,256,256]{2,1,0:T(8,128)(2,1)} %get-tuple-element, ...), custom_call_target="tpu_custom_call" | custom-call | tf_op jit(solution)/shard_map/widen_results/pallas_call | solution.py:1198
  275.9 1.4 copy.36

commit v5 on v4

--- a/solution.py
+++ b/solution.py
@@ -76,16 +76,17 @@
     return jnp.mean(v, -1, keepdims=True)
 
 
-def forward_kernel(
+def layer_kernel(
     n, nz,
     len_ref, x_ref, g_ref, wq_ref, wk_ref, wv_ref, wo_ref, we_ref, wr_ref,
     qb_ref, vb_ref, eb_ref, ob_ref, rb_ref, g1_ref, s1_ref, g2_ref, s2_ref,
-    full_ref, x_out, q_out, k_out, v_out, o_out, p_out, n1_out, r1_out, u_out, h_out, gp_out,
-    ds_out, dz_out, y_out, vec_out, small_out,
-    own, wo_in, wr_in, xin, act_low, xv, cotv, qkv, o_v, p_v, n1_v, r1_v, u_v, ulow_v, h_v, gp_v, acc,
-    dz_v, y_v, wbuf, pk_ref, pk_wide, pkall, head_bias, bias, vec, small,
+    grad_ref, ys_ref, dx_ref, small_out, full_ref, p_ref, part_ref, got_ref,
+    own, turn_in, xv, cotv, qkv, o_v, p_v, n1_v, r1_v, u_v, ulow_v, h_v, gp_v, dz_v, wbuf,
+    pk_ref, pk_wide, turned, pkall, head_bias, bias, vec, small,
+    pbuf, round_in, stage, gstage, total, near, pair_sum, far, up, across,
     own_send, own_recv, fwd_send, fwd_recv, core_send, core_recv, z_send, z_recv, act_send, act_recv,
-    pk_send, pk_recv, in_sem, act_sem, fetch_sem, out_sem, p_sem,
+    pk_send, pk_recv, in_sem, turn_sem, act_sem, fetch_sem, p_sem,
+    *later_sems,
 ):
     s, z, c = place()
     units, rows, width = own.shape
@@ -102,31 +103,32 @@
     ins += [
         lcopy(we_ref.at[:, pl.ds(j * width, width)], own.at[4 + j], in_sem.at[3 + j]) for j in range(e_units)
     ]
-    ins_o = lcopy(wo_ref, wo_in, in_sem.at[3 + e_units])
-    ins_r = lcopy(wr_ref, wr_in, in_sem.at[4 + e_units])
+    tall = [(wo_ref, 3)] + [(wr_ref.at[rows_at(j, width), :], 4 + e_units + j) for j in range(e_units)]
+    ins_t = [lcopy(r, turn_in.at[i % 2], turn_sem.at[i % 2]) for i, (r, _) in enumerate(tall)]
 
     def to(k):
         return lax.rem(z + k, nz)
 
     def act_load(which, k):
         src = (x_ref, g_ref)[which]
-        return lcopy(src.at[2 * to(k) + c], xin.at[k], act_sem.at[k])
-
-    some = block // PIECES
+        return lcopy(src.at[2 * to(k) + c], u_v.at[rows_at(k, block), :], act_sem.at[k])
+
+    chunks = model // SUB
+
+    def held(which, k, i):
+        q = (which * (nz - 1) + k - 1) * chunks
+        return pbuf.at[q // 16, (q // 8) % 2, rows_at(q % 8 + i, block), :]
 
     def act(which, k, i):
         dst = (xv, cotv)[which]
-        at = pl.ds(pl.multiple_of(z * block + i * some, some), some)
         return rcopy(
-            act_low.at[which, k, rows_at(i, some), :], dst.at[at, :],
+            held(which, k, i), dst.at[zrows, rows_at(i, SUB)],
             act_send.at[which, k, i], act_recv.at[which, k, i], (s, to(k), c),
         )
 
     def act_in(which, k, i):
-        dst = (xv, cotv)[which]
-        src = lax.rem(z + nz - k, nz)
-        at = dst.at[pl.ds(pl.multiple_of(src * block + i * some, some), some), :]
-        return rcopy(at, at, act_send.at[which, k, i], act_recv.at[which, k, i], (s, src, c))
+        at = (xv, cotv)[which].at[rows_at(lax.rem(z + nz - k, nz), block), rows_at(i, SUB)]
+        return rcopy(at, at, act_send.at[which, k, i], act_recv.at[which, k, i], (s, lax.rem(z + nz - k, nz), c))
 
     def act_some(which, i):
         for k in range(1, nz):
@@ -135,31 +137,33 @@
     def act_share(which, send):
         for k in range(1, nz):
             act_load(which, k).wait()
-            act_low[which, k] = xin[k].astype(BF16)
-            if send:
-                loop(PIECES, lambda i: act(which, k, i).start())
+            for i in range(chunks):
+                held(which, k, i)[...] = u_v[rows_at(k, block), i * SUB : (i + 1) * SUB].astype(BF16)
+                if send:
+                    act(which, k, i).start()
         act_load(which, 0).wait()
-        (xv, cotv)[which][zrows, :] = xin[0].astype(BF16)
+        (xv, cotv)[which][zrows, :] = u_v[:block, :].astype(BF16)
 
     def act_arrive(which):
         for k in range(1, nz):
-            loop(PIECES, lambda i: act_in(which, k, i).wait_recv())
+            loop(chunks, lambda i: act_in(which, k, i).wait_recv())
 
     for k in range(1, nz):
         act_load(0, k).start()
     for i in ins:
         i.start()
     act_load(0, 0).start()
-    ins_o.start()
-    ins_r.start()
+    ins_t[0].start()
+    ins_t[1].start()
 
     he = HD // n
-    heads = [qb_ref, vb_ref, eb_ref]
+    turned[:he, : eb_ref.shape[1]] = eb_ref[...].astype(F32)
+    heads = [qb_ref[...].astype(F32), vb_ref[...].astype(F32), turned[...].T[: eb_ref.shape[1], :he]]
     head_rows = sum(r.shape[0] for r in heads)
     pk_wide[...] = jnp.zeros_like(pk_wide)
     at = 0
     for r in heads:
-        pk_wide[at : at + r.shape[0], :he] = r[...].astype(F32)
+        pk_wide[at : at + r.shape[0], :he] = r
         at += r.shape[0]
     for i, r in enumerate((ob_ref, rb_ref, g1_ref, s1_ref, g2_ref, s2_ref)):
         pk_wide[at + 8 + i : at + 9 + i, :rows] = r[...].reshape(1, rows).astype(F32)
@@ -222,7 +226,8 @@
 
     def z_copy(u, k):
         at = full_ref.at[c, u, rows_at(s ^ k, rows), :]
-        return rcopy(at, at, z_send.at[u, k], z_recv.at[u, k], (s, z + 1 - 2 * par, c))
+        i = lax.rem(u, 4) + jnp.where(u >= 4 + e_units, 2, 0)
+        return rcopy(at, at, z_send.at[i, k], z_recv.at[i, k], (s, z + 1 - 2 * par, c))
 
     def is_paired(i):
         return jnp.logical_or(i == 3, i == 5)
@@ -238,14 +243,11 @@
         act_load(1, k).start()
     for i in ins[ahead:]:
         i.wait()
-    ins_o.wait()
-    own[3] = wo_in[...].T
-    ins_r.wait()
-
-    def turn(j):
-        own[4 + e_units + j] = wr_in[rows_at(j, width), :].T
-
-    loop(e_units, turn)
+    for i, (_, u) in enumerate(tall):
+        ins_t[i].wait()
+        own[u] = turn_in[i % 2].T
+        if i + 2 < len(tall):
+            ins_t[i + 2].start()
     keep = lcopy(own, full_ref.at[c, :, mine, :], in_sem.at[5 + e_units])
     keep.start()
     share = rcopy(
@@ -283,12 +285,9 @@
                 head_bias[j, 8 * i : 8 * i + 8, :], 0, keepdims=True
             )
     small[...] = jnp.zeros_like(small)
-    vec_copy = lcopy(vec, vec_out, out_sem.at[0])
-    vec_copy.start()
     length = len_ref[2 * z + c]
     live_keys = lax.broadcasted_iota(jnp.int32, (1, slots), 1) < length
     lane = lax.broadcasted_iota(jnp.int32, (slots, 128), 1)
-    outs = []
 
     def fetch(u):
         slot = lax.rem(u, 2)
@@ -307,7 +306,36 @@
             core_in(u, k).wait_recv()
 
     def p_copy(p):
-        return lcopy(p_v.at[lax.rem(p, 2)], p_out.at[p], p_sem.at[lax.rem(p, 2)])
+        return lcopy(p_v.at[lax.rem(p, 2)], p_ref.at[p], p_sem.at[lax.rem(p, 2)])
+
+    class Weights:
+        def __init__(self, buf, i):
+            self.buf, self.i = buf, i
+
+        def copies(self, u):
+            return [
+                lcopy(full_ref.at[hf, u], self.buf.at[:, hf * width : (hf + 1) * width], fetch_sem.at[self.i, hf])
+                for hf in range(2)
+            ]
+
+        def start(self, u):
+            for i in self.copies(u):
+                i.start()
+
+        def wait(self, u):
+            for i in self.copies(u):
+                i.wait()
+
+    wr, we = Weights(wbuf.at[0], 0), Weights(wbuf.at[1], 1)
+
+    def load_p(p):
+        return lcopy(p_ref.at[p], p_v.at[lax.rem(p, 2)], p_sem.at[lax.rem(p, 2)])
+
+    def started():
+        wr.start(4 + e_units)
+        we.start(4)
+        for p in range(2):
+            load_p(p).start()
 
     def attention(p):
         at = rows_at(p, 128)
@@ -347,11 +375,11 @@
 
         @pl.when(u == 3)
         def _():
-            acc[...] = mm_nt(o_v[...], w[...]) + xv[...].astype(F32)
+            u_v[...] = mm_nt(o_v[...], w[...]) + xv[...].astype(F32)
 
             def norm(i):
                 at = rows_at(i, rb)
-                first = acc[at, :] + vec[8:9, :]
+                first = u_v[at, :] + vec[8:9, :]
                 centred = first - mean(first)
                 inv = lax.rsqrt(mean(centred * centred) + EPSILON)
                 n1 = centred * inv
@@ -362,11 +390,6 @@
                 u_v[at, :] = up
 
             loop(slots // rb, norm)
-            for i, (src, dst) in enumerate(
-                ((qkv.at[0], q_out), (qkv.at[1], k_out), (qkv.at[2], v_out), (o_v, o_out),
-                 (n1_v, n1_out), (r1_v, r1_out), (ulow_v, u_out), (xv, x_out))
-            ):
-                lcopy(src, dst, out_sem.at[1 + i]).start()
 
         @pl.when(jnp.logical_and(u >= 4, u < 4 + e_units))
         def _():
@@ -375,10 +398,6 @@
             phi = 0.5 * (1.0 + lax.erf(pre * 0.7071067811865476))
             h_v[j] = (pre * phi).astype(BF16)
             gp_v[j] = (phi + pre * jnp.exp(-0.5 * pre * pre) * 0.3989422804014327).astype(BF16)
-            lcopy(h_v.at[j], h_out.at[j], out_sem.at[10]).start()
-            lcopy(gp_v.at[j], gp_out.at[j], out_sem.at[11]).start()
-            lcopy(h_v.at[j], h_out.at[j], out_sem.at[10]).wait()
-            lcopy(gp_v.at[j], gp_out.at[j], out_sem.at[11]).wait()
 
         @pl.when(u >= 4 + e_units)
         def _():
@@ -424,9 +443,9 @@
                     z_copy(u, k).wait_recv()
                     core_copy(u, k).start()
 
-        @pl.when(jnp.logical_and(t >= 1, t <= PIECES))
-        def _():
-            act_some(1, t - 1)
+        @pl.when(jnp.logical_and(lax.rem(t, 2) == 1, t < 2 * chunks))
+        def _():
+            act_some(1, t // 2)
 
     def first_at(t):
         u = jnp.clip(t - 2, 0, 3)
@@ -459,6 +478,9 @@
 
     loop(slots_of_units + 1, step)
 
+    for p in (pairs - 2, pairs - 1):
+        p_copy(p).wait()
+    started()
     act_arrive(1)
 
     def norm2(i):
@@ -468,12 +490,13 @@
         inv = lax.rsqrt(mean(centred * centred) + EPSILON)
         n2 = centred * inv
         gain = vec[12:13, :]
-        y_v[at, :] = (n2 * gain + vec[13:14, :]).astype(BF16)
+        y = (n2 * gain + vec[13:14, :]).astype(BF16)
         row = lax.broadcasted_iota(jnp.int32, (rb, 1), 0) + i * rb
         grad = jnp.where(row < length, cotv[at, :].astype(F32), 0.0)
         scaled = grad * gain
         back = inv * (scaled - mean(scaled) - n2 * mean(scaled * n2))
-        acc[at, :] = back
+        cotv[at, :] = y
+        u_v[at, :] = back
         low = back.astype(BF16)
         dz_v[at, :] = low
         for r, v in ((14, low.astype(F32)), (20, grad * n2), (22, grad)):
@@ -482,13 +505,6 @@
             small[r + 1 : r + 2, :] += v[:, width:]
 
     loop(slots // rb, norm2)
-    last = [
-        lcopy(src, dst, out_sem.at[12 + i])
-        for i, (src, dst) in enumerate(((acc, ds_out), (dz_v, dz_out), (y_v, y_out), (small, small_out)))
-    ]
-    for i in last:
-        i.start()
-
     def sent(t):
         u = unit_at(t)
         for k in direct:
@@ -514,202 +530,78 @@
         pk_copy(k, j).wait_send()
     for which in range(2):
         for k in range(1, nz):
-            loop(PIECES, lambda i: act(which, k, i).wait_send())
-    vec_copy.wait()
-    for p in (pairs - 2, pairs - 1):
-        p_copy(p).wait()
-    for i, (src, dst) in enumerate(
-        ((qkv.at[0], q_out), (qkv.at[1], k_out), (qkv.at[2], v_out), (o_v, o_out),
-         (n1_v, n1_out), (r1_v, r1_out), (ulow_v, u_out), (xv, x_out))
-    ):
-        lcopy(src, dst, out_sem.at[1 + i]).wait()
-    for i in last:
-        i.wait()
-
-
-def forward(n, nz, lengths, inputs, cotangent, wq, wk, wv, wo, we, wr, heads, vectors):
-    seqs, block, model = inputs.shape
-    rows = wq.shape[0]
-    e_units = we.shape[1] // UNIT
-    units = 4 + 2 * e_units
-    slots = nz * block
-    head_rows = sum(v.shape[0] for v in heads)
-    pk = (head_rows + 16, max(rows, 128))
-    outs = [
-        ((2, units, model, UNIT), BF16), ((slots, model), BF16),
-        ((slots, model), BF16), ((slots, model), BF16), ((slots, model), BF16), ((slots, model), BF16),
-        ((model // 128, 2, slots, slots), BF16), ((slots, model), F32), ((slots, 128), F32), ((slots, model), BF16),
-        ((e_units, slots, model), BF16), ((e_units, slots, model), BF16),
-        ((slots, model), F32), ((slots, model), BF16), ((slots, model), BF16), ((16, model), F32),
-        ((24, UNIT), F32),
-    ]
-    scratch = [
-        ((units, rows, UNIT), BF16), (wo.shape, BF16), (wr.shape, BF16), ((nz, block, model), F32),
-        ((2, nz, block, model), BF16), ((slots, model), BF16), ((slots, model), BF16), ((3, slots, model), BF16),
-        ((slots, model), BF16), ((2, 2, slots, slots), BF16), ((slots, model), F32), ((slots, 128), F32),
-        ((slots, model), F32), ((slots, model), BF16), ((e_units, slots, model), BF16),
-        ((e_units, slots, model), BF16), ((slots, model), F32),
-        ((slots, model), BF16), ((slots, model), BF16), ((2, model, 2 * UNIT), BF16),
-        (pk, BF16), (pk, F32), ((n, 2, *pk), BF16), ((2, head_rows, UNIT), F32), ((16, 2 * UNIT), F32), ((16, model), F32), ((24, UNIT), F32),
-    ]
-    return pl.pallas_call(
-        functools.partial(forward_kernel, n, nz),
-        name="gather_and_forward",
-        out_shape=[jax.ShapeDtypeStruct(a, b) for a, b in outs],
-        in_specs=[SMEM] + [ANY] * 8 + [VMEM] * 9,
-        out_specs=[ANY] * len(outs),
-        scratch_shapes=[pltpu.VMEM(a, b) for a, b in scratch]
-        + [
-            DMA((units, n)), DMA((units, n)), DMA((units, 2)), DMA((units, 2)),
-            DMA((units + 1, n)), DMA((units + 1, n)), DMA((units, n)), DMA((units, n)),
-            DMA((2, nz, PIECES)), DMA((2, nz, PIECES)),
-            DMA((n, 2)), DMA((n, 2)), DMA((6 + e_units,)), DMA((nz,)), DMA((2, 2)), DMA((16,)), DMA((2,)),
-        ],
-        compiler_params=pltpu.CompilerParams(
-            collective_id=0, has_side_effects=True, vmem_limit_bytes=60 * 2**20
-        ),
-    )(lengths, inputs, cotangent, wq, wk, wv, wo, we, wr, *heads, *vectors)
-
-
-def backward_kernel(
-    n, nz,
-    full_ref, x_ref, q_ref, k_ref, v_ref, o_ref, p_ref, n1_ref, r1_ref, u_ref, h_ref, gp_ref,
-    ds_ref, dz_ref, y_ref, vec_ref, small_ref,
-    grad_ref, ys_ref, dx_ref, small_out, part_ref, got_ref,
-    x_v, qkv, o_v, p_v, n1_v, r1_v, u_v, dz_v, du, wr_v, we_v, h_v, gp_v, dpre, pbuf, small, round_in,
-    stage, gstage, total, near, pair_sum, far, up, across, down, block_out,
-    load_sem, w_sem, p_sem, part_sem, core_send, core_recv, stage_sem, near_send, near_recv, far_send, far_recv,
-    z_send, z_recv, store_sem, act_send, act_recv, pass_send, pass_recv, keep_sem, small_send, small_recv,
-):
-    s, z, c = place()
-    units = part_ref.shape[0]
+            loop(chunks, lambda i: act(which, k, i).wait_send())
+
+    (part_sem, give_send, give_recv, stage_sem, near_send, near_recv, far_send, far_recv, chain_send, chain_recv,
+     store_sem, back_send, back_recv, pass_send, pass_recv, keep_sem, small_send, small_recv) = later_sems
     subs = 2 * units
-    e_units = h_ref.shape[0]
-    model = total.shape[1]
-    width = UNIT
-    rows = model // n
-    half = rows // 2
-    slots = x_v.shape[0]
-    block = slots // nz
-    zrows = rows_at(z, block)
-    mates = [(dz_ref, dz_v), (small_ref, small), (ds_ref, du), (n1_ref, n1_v), (r1_ref, r1_v), (o_ref, o_v),
-             (u_ref, u_v), (q_ref, qkv.at[0]), (k_ref, qkv.at[1]), (v_ref, qkv.at[2]), (x_ref, x_v)]
-    loads = [lcopy(a, b, load_sem.at[i]) for i, (a, b) in enumerate(mates)]
-
-    class Weights:
-        def __init__(self, buf, i):
-            self.buf, self.i = buf, i
-
-        def copies(self, u):
-            return [
-                lcopy(full_ref.at[hf, u], self.buf.at[:, hf * width : (hf + 1) * width], w_sem.at[self.i, hf])
-                for hf in range(2)
-            ]
-
-        def start(self, u):
-            for i in self.copies(u):
-                i.start()
-
-        def wait(self, u):
-            for i in self.copies(u):
-                i.wait()
-
-    wr, we = Weights(wr_v, 0), Weights(we_v, 1)
-
-    def load_h(j):
-        return lcopy(h_ref.at[j], h_v, w_sem.at[2, 0])
-
-    def load_gp(j):
-        return lcopy(gp_ref.at[j], gp_v, w_sem.at[2, 1])
-
-    def load_p(p):
-        return lcopy(p_ref.at[p], p_v.at[lax.rem(p, 2)], p_sem.at[lax.rem(p, 2)])
-
-    loads[0].start()
-    load_h(0).start()
-    loads[1].start()
-    load_gp(0).start()
-    wr.start(4 + e_units)
-    we.start(4)
-    for i in loads[2:]:
-        i.start()
-    for p in range(2):
-        load_p(p).start()
-    greet(
-        [(s ^ k, z, c) for k in range(1, n)]
-        + [(s, z, 1 - c)]
-        + [(s, lax.rem(z + k, nz), c) for k in range(1, nz)]
-    )
-
-    def act(which, k, i):
-        src, dst = ((y_ref, ys_ref), (dz_v, dx_ref))[which]
+    def back_act(which, k, i):
+        src, dst = ((cotv, ys_ref), (dz_v, dx_ref))[which]
         to = lax.rem(z + k, nz)
         some = block // PIECES
         return rcopy(
             src.at[pl.ds(pl.multiple_of(to * block + i * some, some), some), :],
             dst.at[2 * z + c, rows_at(i, some), :],
-            act_send.at[which, k, i], act_recv.at[which, k, i], (s, to, c),
+            back_send.at[which, k, i], back_recv.at[which, k, i], (s, to, c),
         )
 
-    def act_in(which, k, i):
+    def back_act_in(which, k, i):
         src = lax.rem(z + nz - k, nz)
         at = (ys_ref, dx_ref)[which].at[2 * src + c, rows_at(i, block // PIECES), :]
-        return rcopy(at, at, act_send.at[which, k, i], act_recv.at[which, k, i], (s, src, c))
-
-    def act_keep(which):
-        src, dst = ((y_ref, ys_ref), (dz_v, dx_ref))[which]
+        return rcopy(at, at, back_send.at[which, k, i], back_recv.at[which, k, i], (s, src, c))
+
+    def back_act_keep(which):
+        src, dst = ((cotv, ys_ref), (dz_v, dx_ref))[which]
         return lcopy(src.at[zrows, :], dst.at[2 * z + c], keep_sem.at[which])
 
-    def pass_copy(which, k):
+    def back_pass_copy(which, k):
         at = (ys_ref, dx_ref)[which].at[2 * lax.rem(z + nz - k, nz) + c]
         return rcopy(at, at, pass_send.at[which, k], pass_recv.at[which, k], (s, z, 1 - c))
 
-    def pass_in(which, k):
+    def back_pass_in(which, k):
         at = (ys_ref, dx_ref)[which].at[2 * lax.rem(z + nz - k, nz) + 1 - c]
         return rcopy(at, at, pass_send.at[which, k], pass_recv.at[which, k], (s, z, 1 - c))
 
-    def act_some(which, i):
+    def back_act_some(which, i):
         for k in range(1, nz):
-            act(which, k, i).start()
-
-    def act_pass(which):
+            back_act(which, k, i).start()
+
+    def back_act_pass(which):
         for k in range(1, nz):
-            loop(PIECES, lambda i: act_in(which, k, i).wait_recv())
-            pass_copy(which, k).start()
-        act_keep(which).wait()
-        pass_copy(which, 0).start()
-
-    act_keep(0).start()
-
-    def core_copy(u):
-        return rcopy(pbuf.at[0], got_ref.at[u], core_send.at[u], core_recv.at[u], (s, z, 1 - c))
-
-    def core_in(u):
-        return rcopy(got_ref.at[u], got_ref.at[u], core_send.at[u], core_recv.at[u], (s, z, 1 - c))
+            loop(PIECES, lambda i: back_act_in(which, k, i).wait_recv())
+            back_pass_copy(which, k).start()
+        back_act_keep(which).wait()
+        back_pass_copy(which, 0).start()
+
+    back_act_keep(0).start()
+
+    def back_core_copy(u):
+        return rcopy(pbuf.at[0], got_ref.at[u], give_send.at[u], give_recv.at[u], (s, z, 1 - c))
+
+    def back_core_in(u):
+        return rcopy(got_ref.at[u], got_ref.at[u], give_send.at[u], give_recv.at[u], (s, z, 1 - c))
 
     def part_copy(u):
-        return lcopy(pbuf.at[1 + lax.rem(u, 3)], part_ref.at[u], part_sem.at[lax.rem(u, 3)])
+        return lcopy(pbuf.at[1 + lax.rem(u, 2)], part_ref.at[u], part_sem.at[lax.rem(u, 2)])
 
     def emit(u, i, value):
         low = value.astype(BF16)
         for b in range(2):
-            pbuf[jnp.where(i == 0, 0, 1 + lax.rem(u, 3)), b] = low[:, b * SUB : (b + 1) * SUB]
+            pbuf[jnp.where(i == 0, 0, 1 + lax.rem(u, 2)), b] = low[:, b * SUB : (b + 1) * SUB]
 
     def produce(u, make):
-        pl.when(u > 0)(lambda: core_copy(u - 1).wait_send())
+        pl.when(u > 0)(lambda: back_core_copy(u - 1).wait_send())
 
         def one(i):
             emit(u, i, make(lax.rem(1 - c + i, 2)))
 
             @pl.when(i == 0)
             def _():
-                core_copy(u).start()
+                back_core_copy(u).start()
 
         loop(2, one)
         part_copy(u).start()
 
-    lane = lax.broadcasted_iota(jnp.int32, (slots, 128), 1)
-    rb = 128
     last_e = e_units - 1
 
     def cols(hf):
@@ -721,24 +613,17 @@
             small[pl.ds(r[hf], 1), :] += v[:, hf * width : (hf + 1) * width]
 
     def make_r(j):
-        load_h(j).wait()
-        produce(j, lambda hf: mm_tn(dz_v[...], h_v[:, cols(hf)]))
-
-        @pl.when(j < last_e)
-        def _():
-            load_h(j + 1).start()
+        produce(j, lambda hf: mm_tn(dz_v[...], h_v[j, :, cols(hf)]))
 
     def make_dpre(j):
         wr.wait(4 + e_units + j)
-        load_gp(j).wait()
-        low = (mm(dz_v[...], wr_v[...]) * gp_v[...].astype(F32)).astype(BF16)
-        dpre[j] = low
+        low = (mm(dz_v[...], wr.buf[...]) * gp_v[j].astype(F32)).astype(BF16)
+        gp_v[j] = low
         add_small((4 + j, 4 + e_units + j), low.astype(F32))
 
         @pl.when(j < last_e)
         def _():
             wr.start(5 + e_units + j)
-            load_gp(j + 1).start()
 
         @pl.when(j == last_e)
         def _():
@@ -746,7 +631,7 @@
 
     def make_du(j):
         we.wait(4 + j)
-        du[...] += mm_nt(dpre[j], we_v[...])
+        u_v[...] += mm_nt(gp_v[j], we.buf[...])
 
         @pl.when(j < last_e)
         def _():
@@ -757,32 +642,30 @@
             we.start(1)
 
     def make_e(u, j):
-        produce(u, lambda hf: mm_tn(u_v[...], dpre[j, :, cols(hf)]))
-
-    def norm(i):
+        produce(u, lambda hf: mm_tn(ulow_v[...], gp_v[j, :, cols(hf)]))
+
+    def norm_back(i):
         at = rows_at(i, rb)
-        grad = du[at, :]
+        grad = u_v[at, :]
         n1 = n1_v[at, :]
-        scaled = grad * vec_ref[10:11, :]
+        scaled = grad * vec[10:11, :]
         back = r1_v[at, 0:1] * (scaled - mean(scaled) - n1 * mean(scaled * n1))
-        du[at, :] = back
+        u_v[at, :] = back
         low = back.astype(BF16)
         dz_v[at, :] = low
         for r, v in ((12, low.astype(F32)), (16, grad * n1), (18, grad)):
             add_small((r, r + 1), v)
 
     def make_o():
-        for i in loads[3:6]:
-            i.wait()
-        loop(slots // rb, norm)
+        loop(slots // rb, norm_back)
         produce(e_units, lambda hf: mm_tn(dz_v[...], o_v[:, cols(hf)]))
 
     def make_do():
         wr.wait(3)
-        o_v[...] = mm(dz_v[...], wr_v[...]).astype(BF16)
+        o_v[...] = mm(dz_v[...], wr.buf[...]).astype(BF16)
         wr.start(0)
 
-    def attention(p):
+    def attention_back(p):
         at = rows_at(p, 128)
         q, k, v, do = qkv[0, :, at], qkv[1, :, at], qkv[2, :, at], o_v[:, at]
         load_p(p).wait()
@@ -804,14 +687,13 @@
         def _():
             load_p(p + 2).start()
 
-    pairs = model // 128
 
     def make_w(u, i):
-        produce(u, lambda hf: mm_tn(x_v[...], qkv[i, :, cols(hf)]))
+        produce(u, lambda hf: mm_tn(xv[...], qkv[i, :, cols(hf)]))
 
     def make_dx(i, weights):
         weights.wait(i)
-        du[...] += mm_nt(qkv[i], weights.buf[...])
+        u_v[...] += mm_nt(qkv[i], weights.buf[...])
         if i != 1:
             add_small((i, i + 1), qkv[i].astype(F32))
 
@@ -826,25 +708,15 @@
     def unit_of(t):
         return t - jnp.where(t > 4, 1, 0) - jnp.where(t > 9, 1, 0)
 
-    def compute(t):
-        @pl.when(t == 0)
-        def _():
-            loads[0].wait()
-            loads[1].wait()
-
+    def work(t):
         pl.when(t < 4)(lambda: make_r(t))
-        pl.when(t == 1)(lambda: loads[2].wait())
         pl.when(jnp.logical_and(t > 0, t < 5))(lambda: make_du(t - 1))
         pl.when(t < 4)(lambda: make_dpre(t))
         pl.when(t == 4)(make_o)
 
-        @pl.when(t == 5)
-        def _():
-            make_do()
-            for i in loads[6:]:
-                i.wait()
-
-        pl.when(jnp.logical_and(t > 4, t < 9))(lambda: loop(2, lambda i: attention(2 * (t - 5) + i)))
+        pl.when(t == 5)(make_do)
+
+        pl.when(jnp.logical_and(t > 4, t < 9))(lambda: loop(2, lambda i: attention_back(2 * (t - 5) + i)))
 
         @pl.when(one_of(t, (6, 7, 12, 13)))
         def _():
@@ -860,8 +732,8 @@
             wr.start(2)
             make_dx(1, we)
             make_dx(2, wr)
-            dz_v[...] = du[...].astype(BF16)
-            act_keep(1).start()
+            dz_v[...] = u_v[...].astype(BF16)
+            back_act_keep(1).start()
 
     def loads_of(w):
         slot = lax.rem(w, 2)
@@ -881,7 +753,7 @@
         k = (1 + h, 3)[i]
         return rcopy(
             total.at[lax.rem(w, SLOTS), blk_half(k, h), :], near.at[w, h, i],
-            near_send.at[w, h, i], near_recv.at[w, h, i], (s ^ (1 + h), z, c),
+            near_send.at[lax.rem(w, SLOTS), h, i], near_recv.at[w, h, i], (s ^ (1 + h), z, c),
         )
 
     def far_copy(w, h):
@@ -892,7 +764,7 @@
     def straight(w, k):
         return rcopy(
             total.at[lax.rem(w, SLOTS), blk(k), :], near.at[w, k - 1],
-            near_send.at[w, k - 1], near_recv.at[w, k - 1], (s ^ k, z, c),
+            near_send.at[lax.rem(w, SLOTS), k - 1], near_recv.at[w, k - 1], (s ^ k, z, c),
         )
 
     def sends_of(w):
@@ -900,9 +772,15 @@
             return [near_copy(w, h, i) for h in range(2) for i in range(2)]
         return [straight(w, k) for k in range(1, n)]
 
+    block_out = own
+
+    def part_cols(w):
+        return rows_at(lax.rem(w, 2), SUB)
+
     def z_to(w, h, src, dst, i, to):
         at = pl.ds(h * half, half)
-        return rcopy(src.at[w, at], dst.at[w, at], z_send.at[w, i, h], z_recv.at[w, i, h], (s, to, c))
+        source = own.at[w // 2, at, part_cols(w)] if src is own else src.at[w, at]
+        return rcopy(source, dst.at[w, at], chain_send.at[w, i, h], chain_recv.at[w, i, h], (s, to, c))
 
     last = nz - 1
     edge = jnp.logical_or(z == 0, z == last)
@@ -914,7 +792,7 @@
         @pl.when(lax.rem(w, 2) == 0)
         def _():
             part_copy(w // 2).wait()
-            core_in(w // 2).wait_recv()
+            back_core_in(w // 2).wait_recv()
 
         for i in loads_of(w):
             i.start()
@@ -954,11 +832,11 @@
             acc = total[slot, blk(0), :].astype(F32)
             for k in range(1, n):
                 acc = acc + near[w, k - 1].astype(F32)
-            block_out[w] = acc.astype(BF16)
+            block_out[w // 2, :, part_cols(w)] = acc.astype(BF16)
         for h in range(2):
             if n == 4:
                 far_copy(w, h).wait_recv()
-                block_out[w, h * half : (h + 1) * half] = (
+                block_out[w // 2, h * half : (h + 1) * half, part_cols(w)] = (
                     total[slot, blk_half(0, h), :].astype(F32) + near[w, h, 0].astype(F32) + far[w, h].astype(F32)
                 ).astype(BF16)
             pl.when(edge)(lambda: z_to(w, h, block_out, up, 0, inner).start())
@@ -969,7 +847,7 @@
             for h in range(2):
                 at = pl.ds(h * half, half)
                 z_to(w, h, block_out, up, 0, outer).wait_recv()
-                block_out[w, at] = (block_out[w, at].astype(F32) + up[w, at].astype(F32)).astype(BF16)
+                block_out[w // 2, at, part_cols(w)] = (block_out[w // 2, at, part_cols(w)].astype(F32) + up[w, at].astype(F32)).astype(BF16)
                 z_to(w, h, block_out, across, 1, other).start()
 
     def s5(w):
@@ -978,16 +856,16 @@
             for h in range(2):
                 at = pl.ds(h * half, half)
                 z_to(w, h, block_out, across, 1, other).wait_recv()
-                down[w, at] = (block_out[w, at].astype(F32) + across[w, at].astype(F32)).astype(BF16)
-                z_to(w, h, down, down, 2, outer).start()
+                up[w, at] = (block_out[w // 2, at, part_cols(w)].astype(F32) + across[w, at].astype(F32)).astype(BF16)
+                z_to(w, h, up, up, 2, outer).start()
 
     def s6(w):
         @pl.when(edge)
         def _():
             for h in range(2):
-                z_to(w, h, down, down, 2, inner).wait_recv()
-
-        lcopy(down.at[w], grad_ref.at[w], store_sem.at[w]).start()
+                z_to(w, h, up, up, 2, inner).wait_recv()
+
+        lcopy(up.at[w], grad_ref.at[w], store_sem.at[w]).start()
 
     stages = list(zip(LAGS, (s0, s3, s2, s1, s6, s5, s4)))
 
@@ -1007,22 +885,23 @@
     done = max(makes) + 2
 
     def served(t):
-        return jnp.clip(2 * (t - 1), 0, 4) + jnp.maximum(PACE * (t - 3) // 4, 0)
-
-    def step(t):
+        late = jnp.maximum((PACE * (t - 3) + 2) // 4, 0) + jnp.where(t > 13, 1, 0)
+        return jnp.clip(2 * (t - 1), 0, 4) + late
+
+    def tick(t):
         lax.fori_loop(served(t), served(t + 1), lambda w, carry: (serve(w), carry)[1], 0)
-        pl.when(t <= max(makes))(lambda: compute(t))
+        pl.when(t <= max(makes))(lambda: work(t))
 
         for which, first in enumerate(ACTS):
-            pl.when(jnp.logical_and(t >= first, t < first + PIECES))(lambda: act_some(which, t - first))
+            pl.when(jnp.logical_and(t >= first, t < first + PIECES))(lambda: back_act_some(which, t - first))
 
         @pl.when(t == PIECES)
         def _():
-            act_pass(0)
+            back_act_pass(0)
 
         @pl.when(t == PASS)
         def _():
-            act_pass(1)
+            back_act_pass(1)
 
         for i in range(len(hops) + 1):
             @pl.when(t == done + i)
@@ -1037,7 +916,7 @@
                     lcopy(small, small_out, keep_sem.at[2]).start()
 
     ticks = (4 * (subs + max(LAGS) - 4) + PACE - 1) // PACE + 3
-    loop(ticks, step)
+    loop(ticks, tick)
 
     def finish(w):
         if n == 4:
@@ -1050,74 +929,85 @@
             @pl.when(jnp.logical_not(edge))
             def _():
                 z_to(w, h, block_out, across, 1, other).wait_send()
-                z_to(w, h, down, down, 2, outer).wait_send()
-
-        lcopy(down.at[w], grad_ref.at[w], store_sem.at[w]).wait()
+                z_to(w, h, up, up, 2, outer).wait_send()
+
+        lcopy(up.at[w], grad_ref.at[w], store_sem.at[w]).wait()
 
     loop(subs, finish)
-    core_copy(units - 1).wait_send()
+    back_core_copy(units - 1).wait_send()
     for w in range(subs - SLOTS, subs):
         for i in sends_of(w):
             i.wait_send()
     for which in range(2):
         for k in range(1, nz):
-            loop(PIECES, lambda i: act(which, k, i).wait_send())
+            loop(PIECES, lambda i: back_act(which, k, i).wait_send())
         for k in range(nz):
-            pass_copy(which, k).wait_send()
-            pass_in(which, k).wait_recv()
+            back_pass_copy(which, k).wait_send()
+            back_pass_in(which, k).wait_recv()
     lcopy(small, small_out, keep_sem.at[2]).wait()
 
 
-def backward(n, nz, full, x, q, k, v, o, p, n1, r1, u, h, gp, ds, dz, y, vec, small):
-    _, units, model, width = full.shape
-    e_units = h.shape[0]
-    rows = model // n
+def layer(n, nz, lengths, inputs, cotangent, wq, wk, wv, wo, we, wr, heads, vectors):
+    seqs, block, model = inputs.shape
+    rows = wq.shape[0]
     half = rows // 2
-    slots = x.shape[0]
-    block = slots // nz
+    e_units = we.shape[1] // UNIT
+    units = 4 + 2 * e_units
     subs = 2 * units
+    slots = nz * block
+    head_rows = heads[0].shape[0] + heads[1].shape[0] + heads[2].shape[1]
+    pk = (head_rows + 16, max(rows, 128))
     near = (subs, 2, 2, half, SUB) if n == 4 else (subs, n - 1, rows, SUB)
     near_sems = near[:3] if n == 4 else near[:2]
     far = (subs, 2, half, SUB) if n == 4 else (1, 2, 16, SUB)
     blocks = (subs, rows, SUB)
     hops = 1 + (n.bit_length() - 1) + (nz.bit_length() - 1)
+    low, wide = ((slots, model), BF16), ((slots, model), F32)
+    hidden = ((e_units, slots, model), BF16)
     outs = [
-        (blocks, BF16), ((2 * nz, block, model), BF16), ((2 * nz, block, model), BF16), ((24, UNIT), F32),
+        (blocks, BF16), ((seqs, block, model), BF16), ((seqs, block, model), BF16), ((24, UNIT), F32),
+        ((2, units, model, UNIT), BF16), ((model // 128, 2, slots, slots), BF16),
         ((units, 2, model, SUB), BF16), ((units, 2, model, SUB), BF16),
     ]
     scratch = [
-        ((slots, model), BF16), ((3, slots, model), BF16), ((slots, model), BF16), ((2, 2, slots, slots), BF16),
-        ((slots, model), F32), ((slots, 128), F32), ((slots, model), BF16), ((slots, model), BF16),
-        ((slots, model), F32), ((model, 2 * UNIT), BF16), ((model, 2 * UNIT), BF16), ((slots, model), BF16),
-        ((slots, model), BF16), ((e_units, slots, model), BF16), ((4, 2, model, SUB), BF16), ((24, UNIT), F32),
-        ((hops, 24, UNIT), F32),
+        ((units, rows, UNIT), BF16), ((2, UNIT, rows), BF16),
+        low, low, ((3, slots, model), BF16), low, ((2, 2, slots, slots), BF16), wide, ((slots, 128), F32), wide, low,
+        hidden, hidden, low, ((2, model, 2 * UNIT), BF16),
+        (pk, BF16), (pk, F32), ((128, 128), F32), ((n, 2, *pk), BF16), ((2, head_rows, UNIT), F32),
+        ((16, 2 * UNIT), F32), ((16, model), F32), ((24, UNIT), F32),
+        ((3, 2, model, SUB), BF16), ((hops, 24, UNIT), F32),
         ((2, model, SUB), BF16), ((2, model, SUB), BF16), ((SLOTS, model, SUB), BF16),
-        (near, BF16), (far, BF16), (far, BF16), (blocks, BF16), (blocks, BF16), (blocks, BF16), (blocks, BF16),
+        (near, BF16), (far, BF16), (far, BF16), (blocks, BF16), (blocks, BF16),
     ]
     return pl.pallas_call(
-        functools.partial(backward_kernel, n, nz),
-        name="backward_and_reduce",
+        functools.partial(layer_kernel, n, nz),
+        name="layer_forward_and_backward",
         out_shape=[jax.ShapeDtypeStruct(a, b) for a, b in outs],
-        in_specs=[ANY] * 15 + [VMEM, ANY],
+        in_specs=[SMEM] + [ANY] * 8 + [VMEM] * 9,
         out_specs=[ANY] * len(outs),
         scratch_shapes=[pltpu.VMEM(a, b) for a, b in scratch]
         + [
-            DMA((12,)), DMA((3, 2)), DMA((2,)), DMA((3,)), DMA((units,)), DMA((units,)), DMA((2, 2)),
-            DMA(near_sems), DMA(near_sems), DMA((subs, 2)), DMA((subs, 2)),
+            DMA((units, n)), DMA((units, n)), DMA((units, 2)), DMA((units, 2)),
+            DMA((units + 1, n)), DMA((units + 1, n)), DMA((4, n)), DMA((4, n)),
+            DMA((2, nz, model // SUB)), DMA((2, nz, model // SUB)),
+            DMA((n, 2)), DMA((n, 2)), DMA((6 + e_units,)), DMA((2,)), DMA((nz,)), DMA((2, 2)), DMA((2,)),
+            DMA((2,)), DMA((units,)), DMA((units,)), DMA((2, 2)),
+            DMA((SLOTS, *near_sems[1:])), DMA(near_sems), DMA((subs, 2)), DMA((subs, 2)),
             DMA((subs, 3, 2)), DMA((subs, 3, 2)), DMA((subs,)),
-            DMA((2, nz, PIECES)), DMA((2, nz, PIECES)), DMA((2, nz)), DMA((2, nz)), DMA((3,)), DMA((hops,)), DMA((hops,)),
+            DMA((2, nz, PIECES)), DMA((2, nz, PIECES)), DMA((2, nz)), DMA((2, nz)), DMA((3,)),
+            DMA((hops,)), DMA((hops,)),
         ],
         compiler_params=pltpu.CompilerParams(
-            collective_id=1, has_side_effects=True, vmem_limit_bytes=61 * 2**20
+            collective_id=0, has_side_effects=True, vmem_limit_bytes=63 * 2**20
         ),
-    )(full, x, q, k, v, o, p, n1, r1, u, h, gp, ds, dz, y, vec, small)
+    )(lengths, inputs, cotangent, wq, wk, wv, wo, we, wr, *heads, *vectors)
 
 
 def finish_kernel(
     n, grad_ref, ys_ref, dx_ref, small_ref,
     y_out, dx_out, dq_out, dk_out, dv_out, do_out, de_out, dr_out,
     qb_out, vb_out, eb_out, ob_out, rb_out, g1_out, s1_out, g2_out, s2_out,
-    grads, act, act_wide, dq, dk, dv, do, de, dr, in_sem, out_sem, act_in, act_out,
+    grads, act, act_wide, dq, dk, dv, do, de, dr, eb_turned, in_sem, out_sem, act_in, act_out,
 ):
     s, _, c = place()
     rows = dq.shape[0]
@@ -1170,11 +1060,12 @@
 
     at = lax.rem(UNIT - s * he, UNIT)
     turned = pltpu.roll(small_ref[...], at, 1)
-    for out, base, count in ((qb_out, 0, 1), (vb_out, 2, 1), (eb_out, 4, e_units)):
+    for out, base, count in ((qb_out, 0, 1), (vb_out, 2, 1), (eb_turned, 4, e_units)):
         for i in range(count):
             line = jnp.where(c == 0, turned[base + i : base + i + 1, :], turned[base + count + i : base + count + i + 1, :])
             for h in range(8):
-                out[8 * i + h : 8 * i + h + 1, :] = line[:, h * HD : h * HD + he]
+                out[8 * i + h : 8 * i + h + 1, :he] = line[:, h * HD : h * HD + he]
+    eb_out[...] = eb_turned[...].T[:he, : 8 * e_units]
     at = lax.rem(UNIT - lax.rem(s * rows, UNIT), UNIT)
     turned = pltpu.roll(small_ref[...], at, 1)
     late = s * rows >= UNIT
@@ -1191,7 +1082,7 @@
 def finish(n, grads, ys, dx, small, heads):
     _, rows, _ = grads.shape
     seqs, block, model = ys.shape
-    wide = heads[2].shape[0] // 8 * UNIT
+    wide = heads[2].shape[1] // 8 * UNIT
     square, tall = (rows, UNIT), (UNIT, rows)
     outs = [ys.shape, ys.shape, square, square, square, tall, (rows, wide), (wide, rows)]
     small_outs = [v.shape for v in heads] + [(rows,)] * 6
@@ -1203,20 +1094,20 @@
         out_specs=[ANY] * len(outs) + [VMEM] * len(small_outs),
         scratch_shapes=[pltpu.VMEM(grads.shape, BF16), pltpu.VMEM((2, *ys.shape), BF16), pltpu.VMEM((2, *ys.shape), F32)]
         + [pltpu.VMEM(a, F32) for a in outs[2:]]
+        + [pltpu.VMEM((128, 128), F32)]
         + [DMA, DMA((6,)), DMA((2, seqs)), DMA((2, seqs))],
         compiler_params=pltpu.CompilerParams(vmem_limit_bytes=61 * 2**20),
     )(grads, ys, dx, small)
 
 
 def body(n, nz, inputs, lengths, wq, wk, wv, wo, we, wr, qb, vb, eb, ob, rb, g1, s1, g2, s2, cotangent):
-    heads = (qb, vb, eb)
-    (full, x, q, k, v, o, p, n1, r1, u, h, gp, ds, dz, y, vec, small) = forward(
+    heads = (qb, vb, eb.T)
+    grads, ys, dx, small, *_ = layer(
         n, nz, lengths, inputs, cotangent, wq, wk, wv, wo, we, wr, heads, (ob, rb, g1, s1, g2, s2)
     )
-    grads, ys, dx, small, _, _ = backward(
-        n, nz, full, x, q, k, v, o, p, n1, r1, u, h, gp, ds, dz, y, vec, small
-    )
-    return tuple(finish(n, grads, ys, dx, small, heads))
+    results = list(finish(n, grads, ys, dx, small, heads))
+    results[10] = results[10].T
+    return tuple(results)
 
 
 def solution(mesh):

time: 278 us -> 264 us (0.950)
  Pallas kernels: 274 us -> 263 us
    pallas_call x2 -> x1, Pallas kernels: 265 us -> 253 us  [layer(): pl.pallas_call(functools.partial(layer_kernel, n, nz), name='layer_forwar...]
where the time goes in v5:
time: 264 us; the launch traced here: 263 us
  Pallas kernels  263 us (100%)
    pallas_call x1, Pallas kernels, layer(): pl.pallas_call(functools.partial(layer_kernel, n, nz), name='layer_forwar...  253 us
    pallas_call x1, Pallas kernels, finish(): pl.pallas_call(functools.partial(finish_kernel, n), name='widen_results',...  9.17 us

profile of v5, /device:TPU:0, one launch (start us, length us, event | category | flops | bytes accessed | tf_op | source)
XLA Modules:
  0.0 263.5 jit_solution(14517023193717994615)
XLA Ops:
  0.7 253.4 %layer_forward_and_backward.1 = (bf16[24,256,256]{2,1,0:T(8,128)(2,1)}, bf16[8,128,1024]{2,1,0:T(8,128)(2,1)}, bf16[8,128,1024]{2,1,0:T(8,128)(2,1)}, f32[24,512...) custom-call(s32[8]{0:T(128)} %len_ref.1, ...), custom_call_target="tpu_custom_call" | custom-call | tf_op jit(solution)/shard_map/layer_forward_and_backward/pallas_call | solution.py:982
  254.1 9.2 %widen_results.1 = (f32[8,128,1024]{2,1,0:T(8,128)}, f32[8,128,1024]{2,1,0:T(8,128)}, f32[256,512]{1,0:T(8,128)}, f32[256,512]{1,0:T(8,128)}, f32[256,512]{1,0:T...) custom-call(bf16[24,256,256]{2,1,0:T(8,128)(2,1)} %get-tuple-element, ...), custom_call_target="tpu_custom_call" | custom-call | tf_op jit(solution)/shard_map/widen_results/pallas_call | solution.py:1089

commit v6 on v5

--- a/solution.py
+++ b/solution.py
@@ -15,7 +15,7 @@
 PACE = 5
 PASS = 22
 PIECES = 8
-ACTS = (0, 10)
+ACTS = (0, 9)
 EPSILON = 1e-05
 MASKED = -1e30
 MESH = pl.DeviceIdType.MESH
@@ -232,7 +232,7 @@
     def is_paired(i):
         return jnp.logical_or(i == 3, i == 5)
 
-    ahead = 1
+    ahead = 2
     for i in ins[:ahead]:
         i.wait()
     for u in range(ahead):
@@ -408,10 +408,10 @@
         def _():
             u = unit_at(t)
 
-            @pl.when(t + ahead < slots_of_units)
+            @pl.when(jnp.logical_and(t > 0, t + 1 < slots_of_units))
             def _():
                 for k in direct:
-                    own_copy(unit_at(t + ahead), k).start()
+                    own_copy(unit_at(t + 1), k).start()
 
             for k in direct:
                 own_in(u, k).wait_recv()
@@ -904,7 +904,7 @@
             back_act_pass(1)
 
         for i in range(len(hops) + 1):
-            @pl.when(t == done + i)
+            @pl.when(t == done + 2 * i)
             def _(i=i):
                 if i > 0:
                     small_copy(i - 1).wait_send()
@@ -1014,8 +1014,13 @@
     seqs = act.shape[1]
     e_units = de.shape[1] // UNIT
     he = HD // n
-    load = lcopy(grad_ref, grads, in_sem)
-    load.start()
+    units = grads.shape[0] // 2
+
+    def load(u):
+        at = pl.ds(2 * u, 2)
+        return lcopy(grad_ref.at[at], grads.at[at], in_sem.at[u])
+
+    loop(units, lambda u: load(u).start())
 
     def act_load(i, which):
         return lcopy((ys_ref, dx_ref)[which].at[i], act.at[which, i], act_in.at[which, i])
@@ -1025,7 +1030,6 @@
 
     for which in range(2):
         loop(seqs, lambda i: act_load(i, which).start())
-    load.wait()
     stores = []
 
     def store(src, dst):
@@ -1037,18 +1041,22 @@
 
     spots = [e_units + 1, e_units + 2, e_units + 6, e_units + 7]
     for j in range(e_units):
+        load(j).wait()
+        load(spots[j]).wait()
         for b in range(2):
             at = j * UNIT + b * SUB
-            dr[at : at + SUB, :] = part(j, b).T
+            dr[at : at + SUB, :] = grads[2 * j + b].T.astype(F32)
             de[:, at : at + SUB] = part(spots[j], b)
     store(dr, dr_out)
     store(de, de_out)
     for i, (v, out) in enumerate(((dq, dq_out), (dk, dk_out), (dv, dv_out))):
+        load(e_units + 3 + i).wait()
         for b in range(2):
             v[:, b * SUB : (b + 1) * SUB] = part(e_units + 3 + i, b)
         store(v, out)
+    load(e_units).wait()
     for b in range(2):
-        do[b * SUB : (b + 1) * SUB, :] = part(e_units, b).T
+        do[b * SUB : (b + 1) * SUB, :] = grads[2 * e_units + b].T.astype(F32)
     store(do, do_out)
     for which in range(2):
         def widen(i):
@@ -1095,7 +1103,7 @@
         scratch_shapes=[pltpu.VMEM(grads.shape, BF16), pltpu.VMEM((2, *ys.shape), BF16), pltpu.VMEM((2, *ys.shape), F32)]
         + [pltpu.VMEM(a, F32) for a in outs[2:]]
         + [pltpu.VMEM((128, 128), F32)]
-        + [DMA, DMA((6,)), DMA((2, seqs)), DMA((2, seqs))],
+        + [DMA((grads.shape[0] // 2,)), DMA((6,)), DMA((2, seqs)), DMA((2, seqs))],
         compiler_params=pltpu.CompilerParams(vmem_limit_bytes=61 * 2**20),
     )(grads, ys, dx, small)
 

time: 264 us -> 263 us (level)
  no operation moved by 1% of the time
where the time goes in v6:
time: 263 us
  Pallas kernels  262 us (100%)
    pallas_call x1, Pallas kernels, layer(): pl.pallas_call(functools.partial(layer_kernel, n, nz), name='layer_forwar...  253 us
    pallas_call x1, Pallas kernels, finish(): pl.pallas_call(functools.partial(finish_kernel, n), name='widen_results',...  9.05 us

profile of v6, /device:TPU:0, one launch (start us, length us, event | category | flops | bytes accessed | tf_op | source)
XLA Modules:
  0.0 262.6 jit_solution(12030181931191077309)
XLA Ops:
  0.7 252.7 %layer_forward_and_backward.1 = (bf16[24,256,256]{2,1,0:T(8,128)(2,1)}, bf16[8,128,1024]{2,1,0:T(8,128)(2,1)}, bf16[8,128,1024]{2,1,0:T(8,128)(2,1)}, f32[24,512...) custom-call(s32[8]{0:T(128)} %len_ref.1, ...), custom_call_target="tpu_custom_call" | custom-call | tf_op jit(solution)/shard_map/layer_forward_and_backward/pallas_call | solution.py:982
  253.4 9.0 %widen_results.1 = (f32[8,128,1024]{2,1,0:T(8,128)}, f32[8,128,1024]{2,1,0:T(8,128)}, f32[256,512]{1,0:T(8,128)}, f32[256,512]{1,0:T(8,128)}, f32[256,512]{1,0:T...) custom-call(bf16[24,256,256]{2,1,0:T(8,128)(2,1)} %get-tuple-element, ...), custom_call_target="tpu_custom_call" | custom-call | tf_op jit(solution)/shard_map/widen_results/pallas_call | solution.py:1097
